TPU v7x, 512 devices: a whole 4x4x16 slice. The times are simulated.
512 devices in a mesh: seq: 64 (over z, x), head: 8 (over y, core).
Axes of the slice: x: 4, y: 4, z: 16, core: 2. Of those that a mesh axis runs over, the one named last changes fastest.
Arguments:
- query_input: bfloat16 [8192, 5120], P(('seq', 'head')), may hold values from -6 to 6
- key_input: bfloat16 [32768, 5120], P(('seq', 'head')), may hold values from -6 to 6
- value_input: bfloat16 [32768, 5120], P(('seq', 'head')), may hold values from -6 to 6
- query_gain: float32 [5120], replicated, may hold values from 0.1 to 1.9
- key_gain: float32 [5120], replicated, may hold values from 0.1 to 1.9
- band_lists: int32 [64, 8], replicated, may hold values from -1 to 255, as said below
- out_weight: bfloat16 [5120, 5120], P('head', 'seq'), may hold values from -4 to 4
Outputs:
- projected: bfloat16 [8192, 5120], P('seq', 'head')
Inputs may be any that keep to these rules, and one draw needn't show every extreme that they name: `band_lists`: each row lists distinct key blocks, live entries first and then -1, 3 or more live. Entry 0 of query block j is key block 4 * j. Every listed block b has |b // 4 - j| <= 2; for query block j, at most 2 distinct blocks are listed from each of s - 1 and s + 1 and at most 1 from each of s - 2 and s + 2, and these counts are reached wherever that index exists.
All inputs are finite; a program needn't handle non-finite values.
Results may differ from a plain program's by a relative error of at most 0.017.
The roundings to bfloat16 on the way count: a program that leaves them out, or rounds other values in their place, can miss the bound.
Values may be sent and summed in bfloat16 or wider, within the bound.
No kernel may reach another device: no remote copies, remote signals or barrier semaphores. Data moves between devices by JAX's collectives and lax.ppermute only.
A program may use at most 64 MiB of HBM per device.

v0:
```python
import jax
import jax.numpy as jnp
from jax import lax
from jax.sharding import PartitionSpec as P

HD = 128
BT = 128
QB_DEV = 1
KB_DEV = 4
MAXB = 8


def from_behind(value, axis, steps):
    count = lax.axis_size(axis)
    initial, last = (max(0, -steps), min(count, count - steps))
    return lax.ppermute(value, axis, [(source, source + steps) for source in range(initial, last)])


def normalize(band_rows, gain_vector):
    widened = band_rows.astype(jnp.float32)
    inverse = lax.rsqrt(jnp.mean(widened * widened, axis=-1, keepdims=True) + 1e-06)
    return (widened * inverse * gain_vector).astype(jnp.bfloat16)


def per_device(query_input, key_input, value_input, query_gain, key_gain, band_lists, out_weight):
    queries_normed = normalize(query_input, query_gain)
    keys_normed = normalize(key_input, key_gain)
    queries, key_rows, value_rows = (
        lax.all_to_all(queries_normed, "head", split_axis=1, concat_axis=0, tiled=True),
        lax.all_to_all(keys_normed, "head", split_axis=1, concat_axis=0, tiled=True),
        lax.all_to_all(value_input, "head", split_axis=1, concat_axis=0, tiled=True),
    )
    group_width = queries.shape[1]
    local_heads = group_width // HD
    own_index = lax.axis_index("seq")
    seq_count = lax.axis_size("seq")
    stacked = jnp.stack(
        [key_rows.reshape(KB_DEV, BT, group_width), value_rows.reshape(KB_DEV, BT, group_width)]
    )
    own_band = lax.dynamic_slice_in_dim(band_lists, own_index * QB_DEV, QB_DEV, 0)
    tile_list = [stacked]
    block_ids = [own_index * KB_DEV + jnp.arange(KB_DEV, dtype=jnp.int32)]
    for offset in (-2, -1, 1, 2):
        received = from_behind(stacked, "seq", -offset)
        source = own_index + offset
        inside = (source >= 0) & (source < seq_count)
        tile_list.append(received)
        block_ids.append(
            jnp.where(inside, source * KB_DEV + jnp.arange(KB_DEV, dtype=jnp.int32), -1)
        )
    window = jnp.concatenate(tile_list, axis=1)
    window_ids = jnp.concatenate(block_ids)
    listed = own_band >= 0
    matches = (own_band[:, :, None] == window_ids[None, None, :]) & listed[:, :, None]
    window_slot = jnp.sum(matches * jnp.arange(window_ids.shape[0], dtype=jnp.int32), axis=2)
    key_heads = window[0][window_slot].reshape(QB_DEV, MAXB, BT, local_heads, HD)
    value_heads = window[1][window_slot].reshape(QB_DEV, MAXB, BT, local_heads, HD)
    query_tiles = queries.reshape(QB_DEV, BT, local_heads, HD)
    scores = jnp.einsum(
        "jqhd,jmkhd->jhqmk", query_tiles, key_heads, preferred_element_type=jnp.float32
    ) * HD ** (-0.5)
    scores = jnp.where(listed[:, None, None, :, None], scores, -jnp.inf)
    row_max = jnp.max(scores, axis=(3, 4), keepdims=True)
    exponent = jnp.exp(scores - row_max)
    totals = jnp.sum(exponent, axis=(3, 4))
    weights = exponent.astype(jnp.bfloat16)
    attended = jnp.einsum(
        "jhqmk,jmkhd->jqhd", weights, value_heads, preferred_element_type=jnp.float32
    )
    attended = attended / jnp.transpose(totals, (0, 2, 1))[:, :, :, None]
    attended = attended.astype(jnp.bfloat16).reshape(QB_DEV * BT, group_width)
    partial_value = jnp.dot(
        attended,
        lax.all_gather(out_weight, "seq", axis=1, tiled=True),
        preferred_element_type=jnp.float32,
    )
    rounded = lax.optimization_barrier(partial_value.astype(jnp.bfloat16)).astype(jnp.float32)
    return lax.psum_scatter(rounded.astype(jnp.bfloat16), "head", scatter_dimension=1, tiled=True)


def solution(mesh):
    return jax.shard_map(
        per_device,
        mesh=mesh,
        in_specs=(
            P(("seq", "head"), None),
            P(("seq", "head"), None),
            P(("seq", "head"), None),
            P(),
            P(),
            P(),
            P("head", "seq"),
        ),
        out_specs=P("seq", "head"),
        check_vma=False,
    )
```

profile of v0, /device:TPU:1, one launch (start us, length us, event | category | flops | bytes accessed | tf_op | source)
XLA Modules:
  0.0 286.5 jit_solution(9553166211743396176)
XLA Ops:
  6.5 0.7 all-gather.2.cloned.1.call-update
  7.3 2.1 copy.62
  9.3 10.5 %all-to-all-start.1 = ((bf16[64,8,640]{2,0,1:T(8,128)(2,1)}), bf16[64,8,640]{2,0,1:T(8,128)(2,1)S(1)}, u32[]{:S(2)}, u32[]{:S(2)}) async-start(bf16[64,8,640]{2,0,1:T(8,128)(2,1)} %bitcast.57), calls=%async_computation.1 | async-start | bytes 1310720 | tf_op jit(solution)/shard_map/all_to_all | solution.py:31
  19.8 0.2 fusion.3
  20.1 0.2 fusion.5
  20.3 0.0 copy-start.2
  20.3 0.9 copy.63
  21.2 9.5 %all-to-all-done.1 = bf16[64,8,640]{2,0,1:T(8,128)(2,1)S(1)} async-done(((bf16[64,8,640]{2,0,1:T(8,128)(2,1)}), bf16[64,8,640]{2,0,1:T(8,128)(2,1)S(1)}, u32[]{:S(2)}, u32[]{:S(2)}) %all-to-all-start.1) | async-done | bytes 655392 | tf_op jit(solution)/shard_map/all_to_all | solution.py:31
  30.7 4.3 %all-to-all-start = ((bf16[64,8,640]{2,0,1:T(8,128)(2,1)}), bf16[64,8,640]{2,0,1:T(8,128)(2,1)S(1)}, u32[]{:S(2)}, u32[]{:S(2)}) async-start(bf16[64,8,640]{2,0,1:T(8,128)(2,1)} %bitcast.58), calls=%async_computation | async-start | bytes 1310720 | tf_op jit(solution)/shard_map/all_to_all | solution.py:30
  35.0 0.2 fusion.17
  35.2 10.7 %all-to-all-done = bf16[64,8,640]{2,0,1:T(8,128)(2,1)S(1)} async-done(((bf16[64,8,640]{2,0,1:T(8,128)(2,1)}), bf16[64,8,640]{2,0,1:T(8,128)(2,1)S(1)}, u32[]{:S(2)}, u32[]{:S(2)}) %all-to-all-start) | async-done | bytes 655392 | tf_op jit(solution)/shard_map/all_to_all | solution.py:30
  45.9 1.8 pad_maximum_fusion
  47.7 2.3 collective-permute-start
  50.1 2.4 collective-permute-start.1
  52.4 1.3 collective-permute-start.2
  53.7 1.3 collective-permute-start.3
  55.0 0.1 fusion.19
  55.2 0.7 copy.64
  55.8 4.6 %all-to-all-start.2 = ((bf16[16,8,640]{2,0,1:T(8,128)(2,1)}), bf16[16,8,640]{2,0,1:T(8,128)(2,1)S(1)}, u32[]{:S(2)}, u32[]{:S(2)}) async-start(bf16[16,8,640]{2,0,1:T(8,128)(2,1)} %bitcast.59), calls=%async_computation.2 | async-start | bytes 327680 | tf_op jit(solution)/shard_map/all_to_all | solution.py:29
  60.5 0.2 dynamic-slice_reduce_fusion
  60.7 0.1 concatenate.7
  60.8 0.2 compare_reduce_fusion
  61.0 0.2 select_reduce_fusion
  61.2 4.9 %all-to-all-done.2 = bf16[16,8,640]{2,0,1:T(8,128)(2,1)S(1)} async-done(((bf16[16,8,640]{2,0,1:T(8,128)(2,1)}), bf16[16,8,640]{2,0,1:T(8,128)(2,1)S(1)}, u32[]{:S(2)}, u32[]{:S(2)}) %all-to-all-start.2) | async-done | bytes 163872 | tf_op jit(solution)/shard_map/all_to_all | solution.py:29
  66.1 0.2 reshape.189
  66.3 11.2 %collective-permute-done = bf16[2,4,128,640]{3,2,1,0:T(8,128)(2,1)} collective-permute-done((bf16[2,4,128,640]{3,2,1,0:T(8,128)(2,1)}, bf16[2,4,128,640]{3,2,1,0:T(8,128)(2,1)}, u32[]{:S(2)}, u32[]{:S(2)}) %collective-permute-start) | collective-permute-done | bytes 1310752 | tf_op jit(solution)/shard_map/ppermute | solution.py:16
  77.5 2.5 constant_dynamic-update-slice_fusion.3
  80.0 25.6 %collective-permute-done.1 = bf16[2,4,128,640]{3,2,1,0:T(8,128)(2,1)} collective-permute-done((bf16[2,4,128,640]{3,2,1,0:T(8,128)(2,1)}, bf16[2,4,128,640]{3,2,1,0:T(8,128)(2,1)}, u32[]{:S(2)}, u32[]{:S(2)}) %collective-permute-start.1) | collective-permute-done | bytes 1310752 | tf_op jit(solution)/shard_map/ppermute | solution.py:16
  105.6 2.5 constant_dynamic-update-slice_fusion.2
  108.1 53.1 %collective-permute-done.2 = bf16[2,4,128,640]{3,2,1,0:T(8,128)(2,1)S(1)} collective-permute-done((bf16[2,4,128,640]{3,2,1,0:T(8,128)(2,1)}, bf16[2,4,128,640]{3,2,1,0:T(8,128)(2,1)S(1)}, u32[]{:S(2)}, u32[]{:S(2)}) %collective-permute-start.2) | collective-permute-done | bytes 1310752 | tf_op jit(solution)/shard_map/ppermute | solution.py:16
  161.2 1.2 constant_dynamic-update-slice_fusion.1
  162.4 1.2 constant_dynamic-update-slice_fusion
  163.6 5.4 %slice_bitcast_fusion = (bf16[20,128,640]{2,1,0:T(8,128)(2,1)S(1)}, bf16[20,128,640]{2,1,0:T(8,128)(2,1)}) fusion(bf16[2,20,128,640]{3,2,1,0:T(8,128)(2,1)} %constant_dynamic-update-slice_fusion), kind=kLoop, calls=%fused_computation.3 | loop fusion | bytes 13107200 | tf_op jit(solution)/shard_map/squeeze | solution.py:56
  169.0 3.8 %gather_fusion = bf16[8,128,640]{2,1,0:T(8,128)(2,1)} fusion(bf16[20,128,640]{2,1,0:T(8,128)(2,1)} %get-tuple-element.6, s32[1024]{0:T(1024)S(1)} %pad_clamp_fusion), kind=kCustom, calls=%fused_computation | custom fusion | bytes 2621472 | tf_op jit(solution)/shard_map/gather | solution.py:57
  172.8 2.4 copy.34
  175.2 1.9 gather_fusion.1
  177.1 1.8 copy.36
  178.9 0.8 copy.38
  179.7 0.5 fusion
  180.2 0.7 fusion.1
  180.9 0.6 copy-done.1
  181.5 0.5 fusion.14
  182.0 48.3 %all-gather.2.cloned.1.call-done = bf16[640,5120]{0,1:T(8,128)(2,1)} async-done(((bf16[640,80]{0,1:T(8,128)(2,1)}), bf16[640,5120]{0,1:T(8,128)(2,1)}) %all-gather.2.cloned.1.call-update) | async-done | bytes 6553616 | tf_op jit(solution)/shard_map/all_gather | solution.py:74
  230.3 5.1 %convolution_convert_fusion = bf16[128,5120]{1,0:T(8,128)(2,1)S(1)} fusion(bf16[128,640]{0,1:T(8,128)(2,1)S(1)} %bitcast.71, bf16[640,5120]{0,1:T(8,128)(2,1)} %all-gather.2.cloned.1.call-done), kind=kOutput, calls=%fused_computation.2 | convolution fusion | flops 839516160 | bytes 8028160 | tf_op jit(solution)/shard_map/dot_general | solution.py:72
  235.4 1.4 copy.42
  236.9 0.0 reduce-scatter.4.cloned.1.call-update
  236.9 41.0 %reduce-scatter.4.cloned.1.call-done = bf16[640,128]{1,0:T(8,128)(2,1)} async-done(((bf16[5120,128]{1,0:T(8,128)(2,1)}), bf16[640,128]{1,0:T(8,128)(2,1)}) %reduce-scatter.4.cloned.1.call-update) | async-done | bytes 163856
  277.9 1.7 copy.43
  (20 shorter events, 0.1 us)
Async XLA Ops:
  6.5 223.8 %all-gather.2.cloned.1.call-start = ((), (), s32[]{:S(2)}) async-start(), calls=%async_computation.4 | async-start | bytes 6656000 | tf_op jit(solution)/shard_map/all_gather | solution.py:74
  7.3 12.5 %copy-start = (bf16[64,5120]{1,0:T(8,128)(2,1)S(1)}, bf16[64,5120]{1,0:T(8,128)(2,1)}, u32[]{:S(2)}) copy-start(bf16[64,5120]{1,0:T(8,128)(2,1)} %param.8) | copy-start | bytes 1966084
  9.3 10.7 %copy-start.4 = (f32[5120]{0:T(1024)S(1)}, f32[5120]{0:T(1024)}, u32[]{:S(2)}) copy-start(f32[5120]{0:T(1024)} %param.11) | copy-start | bytes 61444
  9.3 21.4 %all-to-all-start.1 = ((bf16[64,8,640]{2,0,1:T(8,128)(2,1)}), bf16[64,8,640]{2,0,1:T(8,128)(2,1)S(1)}, u32[]{:S(2)}, u32[]{:S(2)}) async-start(bf16[64,8,640]{2,0,1:T(8,128)(2,1)} %bitcast.57), calls=%async_computation.1 | async-start | bytes 1310720 | tf_op jit(solution)/shard_map/all_to_all | solution.py:31
  20.3 14.7 %copy-start.2 = (bf16[16,5120]{1,0:T(8,128)(2,1)S(1)}, bf16[16,5120]{1,0:T(8,128)(2,1)}, u32[]{:S(2)}) copy-start(bf16[16,5120]{1,0:T(8,128)(2,1)} %param.7) | copy-start | bytes 491524
  30.7 15.2 %all-to-all-start = ((bf16[64,8,640]{2,0,1:T(8,128)(2,1)}), bf16[64,8,640]{2,0,1:T(8,128)(2,1)S(1)}, u32[]{:S(2)}, u32[]{:S(2)}) async-start(bf16[64,8,640]{2,0,1:T(8,128)(2,1)} %bitcast.58), calls=%async_computation | async-start | bytes 1310720 | tf_op jit(solution)/shard_map/all_to_all | solution.py:30
  45.9 9.1 %copy-start.3 = (f32[5120]{0:T(1024)S(1)}, f32[5120]{0:T(1024)}, u32[]{:S(2)}) copy-start(f32[5120]{0:T(1024)} %param.10) | copy-start | bytes 61444
  45.9 14.5 %copy-start.5 = (s32[64,8]{0,1:T(8,128)S(1)}, s32[64,8]{0,1:T(8,128)}, u32[]{:S(2)}) copy-start(s32[64,8]{0,1:T(8,128)} %param.12) | copy-start | bytes 6148
  47.7 29.7 %collective-permute-start = (bf16[2,4,128,640]{3,2,1,0:T(8,128)(2,1)}, bf16[2,4,128,640]{3,2,1,0:T(8,128)(2,1)}, u32[]{:S(2)}, u32[]{:S(2)}) collective-permute-start(bf16[2,4,128,640]{3,2,1,0:T(8,128)(2,1)} %get-tuple-element.9), channel_id=1, source_target_pairs={{0,16},{8,24},{16,32},{24,40},{32,48},{40,56},{48,64},{56,72},{64,... | collective-permute-start | bytes 3932168 | tf_op jit(solution)/shard_map/ppermute | solution.py:16
  50.1 55.5 %collective-permute-start.1 = (bf16[2,4,128,640]{3,2,1,0:T(8,128)(2,1)}, bf16[2,4,128,640]{3,2,1,0:T(8,128)(2,1)}, u32[]{:S(2)}, u32[]{:S(2)}) collective-permute-start(bf16[2,4,128,640]{3,2,1,0:T(8,128)(2,1)} %get-tuple-element.9), channel_id=1, source_target_pairs={{0,8},{8,16},{16,24},{24,32},{32,40},{40,48},{48,56},{56,64},{64,7... | collective-permute-start | bytes 3932168 | tf_op jit(solution)/shard_map/ppermute | solution.py:16
  52.4 108.8 %collective-permute-start.2 = (bf16[2,4,128,640]{3,2,1,0:T(8,128)(2,1)}, bf16[2,4,128,640]{3,2,1,0:T(8,128)(2,1)S(1)}, u32[]{:S(2)}, u32[]{:S(2)}) collective-permute-start(bf16[2,4,128,640]{3,2,1,0:T(8,128)(2,1)} %get-tuple-element.9), channel_id=1, source_target_pairs={{8,0},{16,8},{24,16},{32,24},{40,32},{48,40},{56,48},{64,56},{72,6... | collective-permute-start | bytes 3932168 | tf_op jit(solution)/shard_map/ppermute | solution.py:16
  53.7 108.7 %collective-permute-start.3 = (bf16[2,4,128,640]{3,2,1,0:T(8,128)(2,1)}, bf16[2,4,128,640]{3,2,1,0:T(8,128)(2,1)S(1)}, u32[]{:S(2)}, u32[]{:S(2)}) collective-permute-start(bf16[2,4,128,640]{3,2,1,0:T(8,128)(2,1)} %get-tuple-element.9), channel_id=1, source_target_pairs={{16,0},{24,8},{32,16},{40,24},{48,32},{56,40},{64,48},{72,56},{80,... | collective-permute-start | bytes 3932168 | tf_op jit(solution)/shard_map/ppermute | solution.py:16
  55.8 10.2 %all-to-all-start.2 = ((bf16[16,8,640]{2,0,1:T(8,128)(2,1)}), bf16[16,8,640]{2,0,1:T(8,128)(2,1)S(1)}, u32[]{:S(2)}, u32[]{:S(2)}) async-start(bf16[16,8,640]{2,0,1:T(8,128)(2,1)} %bitcast.59), calls=%async_computation.2 | async-start | bytes 327680 | tf_op jit(solution)/shard_map/all_to_all | solution.py:29
  60.5 217.5 %reduce-scatter.4.cloned.1.call-start = ((), (), s32[]{:S(2)}) async-start(), calls=%async_computation.5 | async-start | bytes 1474560
  180.2 1.4 copy-start.1
Sparse Core Ops, SparseCore 0:
  10.3 219.9 all-gather.1
  237.0 40.8 reduce-scatter.3
where the time goes:
time: 288 us; the launch traced here: 286 us
  waiting for transfers between devices  205 us (71%)
  local copies, waits for them, and re-layouts  31.4 us (11%)
  starting transfers between devices  26.7 us (9%)
  between operations  13.5 us (5%)
  matrix products  6.1 us (2%)
  other arithmetic  3.66 us (1%)
    ppermute x4, waiting for transfers between devices, from_behind(): lax.ppermute(value, axis, [(source, source + steps) for source in range(i...  89.9 us
    all_gather x1, waiting for transfers between devices, per_device(): lax.all_gather(out_weight, 'seq', axis=1, tiled=True)  48.3 us
    unnamed x3, waiting for transfers between devices  41.7 us
    all_to_all x1, waiting for transfers between devices, per_device(): lax.all_to_all(keys_normed, 'head', split_axis=1, concat_axis=0, tiled=True)  10.7 us
    all_to_all x1, starting transfers between devices, per_device(): lax.all_to_all(value_input, 'head', split_axis=1, concat_axis=0, tiled=True)  10.5 us
    unnamed x17, local copies, waits for them, and re-layouts  10 us
    all_to_all x1, waiting for transfers between devices, per_device(): lax.all_to_all(value_input, 'head', split_axis=1, concat_axis=0, tiled=True)  9.52 us
    ppermute x4, starting transfers between devices, from_behind(): lax.ppermute(value, axis, [(source, source + steps) for source in range(i...  7.27 us
  transfers between devices with their start and end apart: 9, of which 8 were waited for; matrix products, arithmetic and copies ran while one was open for 11% of the time, Pallas kernels for 0%

commit v1 on v0

v1 whole, which is shorter than its diff:
```python
import jax
import jax.numpy as jnp
from jax import lax
from jax.experimental import pallas as pl
from jax.experimental.pallas import tpu as pltpu
from jax.sharding import Mesh, PartitionSpec as P

HD = 128
HALF = 64
QROWS = 16
NX = 4
NH = 8
NZ = 16
MAXB = 8
GROUP = 5
K0, V0, K5, V5, Q0, Q5, CHUNK = 0, 64, 128, 144, 160, 176, 192
KV = 160
BF = jnp.bfloat16
F32 = jnp.float32
VMEM = pl.BlockSpec(memory_space=pltpu.VMEM)
SMEM = pl.BlockSpec(memory_space=pltpu.SMEM)
ANY = pl.BlockSpec(memory_space=pl.ANY)
LIMIT = 40 * 1024 * 1024


def dot(a, b, contract):
    return lax.dot_general(a, b, ((contract[:1], contract[1:]), ((), ())), preferred_element_type=F32)


def pack_kernel(q_ref, k_ref, v_ref, qg_ref, kg_ref, out_ref):
    def inverse(ref):
        wide = ref[...].astype(F32)
        return lax.rsqrt(jnp.mean(wide * wide, axis=-1, keepdims=True) + 1e-06)

    q_inv, k_inv = inverse(q_ref), inverse(k_ref)
    for group in range(NH):
        for at in range(GROUP):
            cols = slice((group * GROUP + at) * HD, (group * GROUP + at + 1) * HD)
            q = (q_ref[:, cols].astype(F32) * q_inv * qg_ref[:, cols]).astype(BF)
            k = (k_ref[:, cols].astype(F32) * k_inv * kg_ref[:, cols]).astype(BF)
            v = v_ref[:, cols]
            if at < NX:
                chunk = at * NH + group
                out_ref[chunk, K0 : K0 + HALF] = k
                out_ref[chunk, V0 : V0 + HALF] = v
                out_ref[chunk, Q0 : Q0 + QROWS] = q
            else:
                for x in range(NX):
                    chunk = x * NH + group
                    rows = slice(x * 16, x * 16 + 16)
                    out_ref[chunk, K5 : K5 + 16] = k[rows]
                    out_ref[chunk, V5 : V5 + 16] = v[rows]
                    out_ref[chunk, Q5 : Q5 + QROWS] = q


def listed_of(lists, block, seq, count):
    found = [jnp.int32(-1)] * count
    for m in range(MAXB):
        entry = lists[block * MAXB + m]
        hit = (entry >= 0) & ((entry >> 2) == seq)
        for i in reversed(range(count)):
            free = found[i] < 0
            if i:
                free = free & (found[i - 1] >= 0)
            found[i] = jnp.where(hit & free, entry, found[i])
    return found


def select_kernel(lists, zi, r_ref, up_ref, down_ref, sems):
    z = zi[0]
    above = jnp.minimum(z + 1, NZ - 1) * 4
    below = jnp.maximum(z - 1, 0) * 4
    first = z * 4
    up = (
        listed_of(lists, above, first + 2, 1)
        + listed_of(lists, above, first + 3, 2)
        + listed_of(lists, above + 1, first + 3, 1)
    )
    down = (
        listed_of(lists, below + 3, first + 1, 1)
        + listed_of(lists, below + 3, first, 2)
        + listed_of(lists, below + 2, first, 1)
    )
    copies = []
    for side, (blocks, target) in enumerate(((up, up_ref), (down, down_ref))):
        for slot, block in enumerate(blocks):
            at = jnp.clip(block - z * 16, 0, 15)
            copies.append(
                pltpu.make_async_copy(
                    r_ref.at[pl.ds(at * 2, 2), pl.ds(0, KV)],
                    target.at[pl.ds(slot * 2, 2)],
                    sems.at[side * 4 + slot],
                )
            )
    for copy in copies:
        copy.start()
    for copy in copies:
        copy.wait()


def softmax(scores):
    top = jnp.max(scores, axis=0, keepdims=True)
    exponent = jnp.exp(scores - top)
    return top, jnp.sum(exponent, axis=0, keepdims=True), exponent.astype(BF)


def attend_kernel(lists, zi, r_ref, prev_ref, next_ref, out_ref, win, kg, vg, k5g, v5g, sems):
    z = zi[0]
    copies = [
        pltpu.make_async_copy(r_ref, win.at[pl.ds(0, 32)], sems.at[0]),
        pltpu.make_async_copy(prev_ref, win.at[pl.ds(32, 8), pl.ds(0, KV)], sems.at[1]),
        pltpu.make_async_copy(next_ref, win.at[pl.ds(40, 8), pl.ds(0, KV)], sems.at[2]),
    ]
    for copy in copies:
        copy.start()
    for copy in copies:
        copy.wait()
    scale = HD**-0.5
    for x in range(NX):
        near_before, near_after = jnp.int32(0), jnp.int32(0)
        biases = []
        for m in range(MAXB):
            entry = lists[(z * 4 + x) * MAXB + m]
            live = entry >= 0
            rel = entry - z * 16
            at = jnp.clip(rel, 0, 15)
            quarter = rel >> 2
            if x == 0:
                at = jnp.where(quarter == -2, 16, at)
                at = jnp.where(quarter == -1, 17 + jnp.minimum(near_before, 1), at)
                near_before = near_before + ((quarter == -1) & live).astype(jnp.int32)
            if x == 1:
                at = jnp.where(quarter == -1, 19, at)
            if x == 2:
                at = jnp.where(quarter == 4, 23, at)
            if x == 3:
                at = jnp.where(quarter == 5, 20, at)
                at = jnp.where(quarter == 4, 21 + jnp.minimum(near_after, 1), at)
                near_after = near_after + ((quarter == 4) & live).astype(jnp.int32)
            at = jnp.where(live, at, 0)
            biases.append(jnp.where(live, 0.0, -jnp.inf))
            for half in range(2):
                row = m * 2 + half
                block = win.at[at * 2 + half]
                kg[row * 64 : row * 64 + 64] = block[K0 : K0 + 64]
                vg[row * 64 : row * 64 + 64] = block[V0 : V0 + 64]
                k5g[row * 16 : row * 16 + 16] = block[K5 : K5 + 16]
                v5g[row * 16 : row * 16 + 16] = block[V5 : V5 + 16]
        cols = slice(x * 128, x * 128 + 128)
        q = win[x * NH : x * NH + NH, Q0 : Q0 + QROWS].reshape(128, HD)
        raw = dot(kg[...], q, (1, 1)) * scale
        scores = jnp.concatenate([raw[m * 128 : m * 128 + 128] + biases[m] for m in range(MAXB)], axis=0)
        top, total, weights = softmax(scores)
        out_ref[0:128, cols] = (dot(vg[...], weights, (0, 0)) / total).astype(BF)

        q5 = win[x * NH : x * NH + NH, Q5 : Q5 + QROWS].reshape(128, HD)
        raw = dot(k5g[...], q5, (1, 1)) * scale
        scores = jnp.concatenate([raw[m * 32 : m * 32 + 32] + biases[m] for m in range(MAXB)], axis=0)
        top, total, weights = softmax(scores)
        out_ref[128:256, cols] = (dot(v5g[...], weights, (0, 0)) / total).astype(BF)
        level = top + jnp.log(total)
        high = level.astype(BF)
        rest = level - high.astype(F32)
        middle = rest.astype(BF)
        low = (rest - middle.astype(F32)).astype(BF)
        zeros = jnp.zeros((13, 128), F32)
        out_ref[256:272, cols] = jnp.concatenate(
            [high.astype(F32), middle.astype(F32), low.astype(F32), zeros], axis=0
        ).astype(BF)


def project_kernel(g_ref, w_ref, out_ref, a_ref):
    levels = []
    for x in range(NX):
        parts = g_ref[x, 256:272].astype(F32)
        levels.append(parts[0:1] + parts[1:2] + parts[2:3])
    top = jnp.maximum(jnp.maximum(levels[0], levels[1]), jnp.maximum(levels[2], levels[3]))
    shares = [jnp.exp(level - top) for level in levels]
    total = shares[0] + shares[1] + shares[2] + shares[3]
    shared = jnp.zeros((128, 512), F32)
    for x in range(NX):
        a_ref[x * 128 : x * 128 + 128] = g_ref[x, 0:128]
        shared = shared + g_ref[x, 128:256].astype(F32) * (shares[x] / total)
    a_ref[512:640] = shared.astype(BF)
    a = a_ref[...]
    for group in range(NH):
        part = dot(w_ref[group * 160 : group * 160 + 160], a, (1, 0)).astype(BF)
        for x in range(NX):
            out_ref[x * NH + group] = part[:, x * 128 : x * 128 + 128]


def final_kernel(r_ref, out_ref, t_ref):
    for x in range(NX):
        total = r_ref[x * NH].astype(F32)
        for group in range(1, NH):
            total = total + r_ref[x * NH + group].astype(F32)
        t_ref[x * 80 : x * 80 + 80] = total[0:80]
        t_ref[320 + x * 80 : 320 + x * 80 + 80] = total[80:160]
    out_ref[...] = t_ref[...].T.astype(BF)


def call(kernel, out, specs, out_specs=VMEM, scratch=(), cost=None):
    return pl.pallas_call(
        kernel,
        out_shape=out,
        in_specs=specs,
        out_specs=out_specs,
        scratch_shapes=list(scratch),
        compiler_params=pltpu.CompilerParams(vmem_limit_bytes=LIMIT),
        cost_estimate=cost,
    )


def shape(*dims):
    return jax.ShapeDtypeStruct(dims, BF)


def cost(us):
    return pl.CostEstimate(flops=int(us * 1e9), bytes_accessed=1 << 20, transcendentals=0)


def per_device(query_input, key_input, value_input, query_gain, key_gain, band_lists, out_weight):
    plane = ("x", "y", "c")
    weight = lax.all_gather(out_weight.T, "z", axis=0, tiled=True)
    lists = band_lists.reshape(-1)
    zi = lax.axis_index("z").reshape(1)
    packed = call(pack_kernel, shape(32, CHUNK, HD), [VMEM] * 5)(
        query_input, key_input, value_input, query_gain.reshape(1, -1), key_gain.reshape(1, -1)
    )
    mine = lax.all_to_all(packed, plane, split_axis=0, concat_axis=0, tiled=True)
    up, down = call(
        select_kernel,
        (shape(8, KV, HD), shape(8, KV, HD)),
        [SMEM, SMEM, ANY],
        (ANY, ANY),
        [pltpu.SemaphoreType.DMA((8,))],
    )(lists, zi, mine)
    before = lax.ppermute(up, "z", [(i, i + 1) for i in range(NZ - 1)])
    after = lax.ppermute(down, "z", [(i + 1, i) for i in range(NZ - 1)])
    attended = call(
        attend_kernel,
        shape(272, 512),
        [SMEM, SMEM, ANY, ANY, ANY],
        VMEM,
        [
            pltpu.VMEM((48, CHUNK, HD), BF),
            pltpu.VMEM((1024, HD), BF),
            pltpu.VMEM((1024, HD), BF),
            pltpu.VMEM((256, HD), BF),
            pltpu.VMEM((256, HD), BF),
            pltpu.SemaphoreType.DMA((3,)),
        ],
    )(lists, zi, mine, before, after)
    gathered = lax.all_gather(attended, "x", axis=0, tiled=False)
    terms = call(project_kernel, shape(32, 160, 128), [VMEM, VMEM], VMEM, [pltpu.VMEM((640, 512), BF)])(
        gathered, weight
    )
    summands = lax.all_to_all(terms, plane, split_axis=0, concat_axis=0, tiled=True)
    return call(final_kernel, shape(128, 640), [VMEM], VMEM, [pltpu.VMEM((640, 128), F32)])(summands)


def solution(mesh):
    split = Mesh(mesh.devices.reshape(NZ, NX, 4, 2), ("z", "x", "y", "c"))
    rows = P(("z", "x", "y", "c"), None)
    return jax.shard_map(
        per_device,
        mesh=split,
        in_specs=(rows, rows, rows, P(), P(), P(), P(("y", "c"), ("z", "x"))),
        out_specs=P(("z", "x"), ("y", "c")),
        check_vma=False,
    )
```

time: 288 us -> 158 us (0.55)
  waiting for transfers between devices: 205 us -> 87.1 us
  blocking collectives: 0 us -> 27.9 us
  local copies, waits for them, and re-layouts: 31.4 us -> 7.39 us
  starting transfers between devices: 26.7 us -> 13.5 us
  Pallas kernels: 0 us -> 8.32 us
  matrix products: 6.1 us -> 0 us
  other arithmetic: 3.66 us -> 0 us
    ppermute x4 -> x2, waiting for transfers between devices: 89.9 us -> 11.2 us  [the longest x1 7.48 us: per_device(): before = lax.ppermute(up, 'z', [(i, i + 1) for i in range(NZ - 1)])]
    unnamed x3 -> x2, waiting for transfers between devices: 41.7 us -> 0.73 us
    all_to_all x0 -> x1, blocking collectives: none -> 27.9 us  [per_device(): lax.all_to_all(terms, plane, split_axis=0, concat_axis=0, tiled=True)]
    gather x4 -> x0, local copies, waits for them, and re-layouts: 9.82 us -> none  [the longest x2 6.19 us: per_device(): window[1][window_slot].reshape(QB_DEV, MAXB, BT, local_heads, HD)]
    all_to_all x3 -> x1, starting transfers between devices: 19.4 us -> 10.6 us  [per_device(): lax.all_to_all(packed, plane, split_axis=0, concat_axis=0, tiled=True)]
    pallas_call x0 -> x5, Pallas kernels: none -> 8.32 us  [the longest x1 3.23 us: per_device(): call(attend_kernel, shape(272, 512), [SMEM, SMEM, ANY, ANY, ANY], VMEM, [...]
    dot_general x2 -> x0, matrix products: 5.58 us -> none  [the longest x1 5.09 us: per_device(): jnp.dot(attended, lax.all_gather(out_weight, 'seq', axis=1, tiled=True),...]
    squeeze x1 -> x0, local copies, waits for them, and re-layouts: 5.41 us -> none  [per_device(): window[0][window_slot].reshape(QB_DEV, MAXB, BT, local_heads, HD)]
  transfers between devices with their start and end apart: 9 -> 5, of which waited for: 8 -> 5; matrix products, arithmetic and copies ran while one was open for 11% -> 0% of each run, Pallas kernels for 0% -> 4%
where the time goes in v1:
time: 158 us
  waiting for transfers between devices  87.1 us (55%)
  blocking collectives  27.9 us (18%)
  starting transfers between devices  13.5 us (9%)
  between operations  13.5 us (9%)
  Pallas kernels  8.32 us (5%)
  local copies, waits for them, and re-layouts  7.39 us (5%)
    all_gather x1, waiting for transfers between devices, per_device(): gathered = lax.all_gather(attended, 'x', axis=0, tiled=False)  38.5 us
    all_to_all x1, blocking collectives, per_device(): lax.all_to_all(terms, plane, split_axis=0, concat_axis=0, tiled=True)  27.9 us
    all_to_all x1, waiting for transfers between devices, per_device(): lax.all_to_all(packed, plane, split_axis=0, concat_axis=0, tiled=True)  22.5 us
    all_gather x1, waiting for transfers between devices, per_device(): weight = lax.all_gather(out_weight.T, 'z', axis=0, tiled=True)  14.1 us
    all_to_all x1, starting transfers between devices, per_device(): lax.all_to_all(packed, plane, split_axis=0, concat_axis=0, tiled=True)  10.6 us
    ppermute x1, waiting for transfers between devices, per_device(): before = lax.ppermute(up, 'z', [(i, i + 1) for i in range(NZ - 1)])  7.48 us
    unnamed x17, local copies, waits for them, and re-layouts  7.3 us
    ppermute x1, waiting for transfers between devices, per_device(): after = lax.ppermute(down, 'z', [(i + 1, i) for i in range(NZ - 1)])  3.77 us
  transfers between devices with their start and end apart: 5, of which 5 were waited for; matrix products, arithmetic and copies ran while one was open for 0% of the time, Pallas kernels for 4%

profile of v1, /device:TPU:1, one launch (start us, length us, event | category | flops | bytes accessed | tf_op | source)
XLA Modules:
  0.0 157.7 jit_solution(18119503489711293636)
XLA Ops:
  6.5 0.0 all-gather.4.cloned.1.call-start
  6.5 0.7 all-gather.4.cloned.1.call-update
  7.3 0.0 copy-start.2
  7.3 1.1 copy-done.2
  8.3 0.0 copy-start.3
  8.3 1.1 copy-done.3
  9.4 0.0 copy-start.4
  9.4 0.9 copy-done.4
  10.3 0.0 copy-start.5
  10.4 0.7 copy-done.5
  11.1 0.0 copy-start.6
  11.1 0.7 copy-done.6
  11.8 1.6 shard_map.73
  13.4 0.0 copy-start.7
  13.4 10.6 %all-to-all-start = ((bf16[32,192,128]{2,1,0:T(8,128)(2,1)}), bf16[32,192,128]{2,1,0:T(8,128)(2,1)S(1)}, u32[]{:S(2)}, u32[]{:S(2)}) async-start(bf16[32,192,128]{2,1,0:T(8,128)(2,1)} %shard_map.73), calls=%async_computation | async-start | bytes 3145728 | tf_op jit(solution)/shard_map/all_to_all | solution.py:230
  24.0 0.0 all-gather.6.cloned.1.call-start
  24.1 0.0 copy-done.7
  24.1 0.1 copy.8
  24.2 0.1 reshape.12.lists
  24.2 22.5 %all-to-all-done.r_ref = bf16[32,192,128]{2,1,0:T(8,128)(2,1)S(1)} async-done(((bf16[32,192,128]{2,1,0:T(8,128)(2,1)}), bf16[32,192,128]{2,1,0:T(8,128)(2,1)S(1)}, u32[]{:S(2)}, u32[]{:S(2)}) %all-to-all-start) | async-done | bytes 1572896 | tf_op jit(solution)/shard_map/all_to_all | solution.py:230
  46.8 1.3 shard_map.74
  48.1 1.6 collective-permute-start
  49.7 1.3 collective-permute-start.1
  51.0 7.5 %collective-permute-done.prev_ref = bf16[8,160,128]{2,1,0:T(8,128)(2,1)S(1)} collective-permute-done((bf16[8,160,128]{2,1,0:T(8,128)(2,1)S(1)}, bf16[8,160,128]{2,1,0:T(8,128)(2,1)S(1)}, u32[]{:S(2)}, u32[]{:S(2)}) %collective-permute-start) | collective-permute-done | bytes 327712 | tf_op jit(solution)/shard_map/ppermute | solution.py:238
  58.5 3.8 %collective-permute-done.1.next_ref = bf16[8,160,128]{2,1,0:T(8,128)(2,1)S(1)} collective-permute-done((bf16[8,160,128]{2,1,0:T(8,128)(2,1)S(1)}, bf16[8,160,128]{2,1,0:T(8,128)(2,1)S(1)}, u32[]{:S(2)}, u32[]{:S(2)}) %collective-permute-start.1) | collective-permute-done | bytes 327712 | tf_op jit(solution)/shard_map/ppermute | solution.py:239
  62.2 3.2 %shard_map.75 = bf16[272,512]{1,0:T(8,128)(2,1)} custom-call(s32[512]{0:T(512)S(1)} %reshape.12.lists, s32[1]{0:T(128)} %bitcast.zi, bf16[32,192,128]{2,1,0:T(8,128)(2,1)S(1)} %all-to-all-done.r_ref, bf16[8,160,128]{2,1,0:T(8,128)(2,1)S(1)} %collective-permute-done.prev_ref, bf16[8,160,128]{2,1,0:T(8,128)(2,1)S(1)} %collective-permute-done.1.next_ref), custom_call_target="tpu_custom_call" | custom-call | tf_op jit(solution)/shard_map/pallas_call | solution.py:240
  65.5 0.0 all-gather.6.cloned.1.call-update
  65.5 14.1 %all-gather.4.cloned.1.call-done.w_ref = bf16[1280,640]{1,0:T(8,128)(2,1)} async-done(((bf16[80,640]{1,0:T(8,128)(2,1)}), bf16[1280,640]{1,0:T(8,128)(2,1)}) %all-gather.4.cloned.1.call-update) | async-done | bytes 1638416 | tf_op jit(solution)/shard_map/all_gather | solution.py:224
  79.6 38.5 %all-gather.6.cloned.1.call-done = bf16[1088,512]{1,0:T(8,128)(2,1)} async-done(((bf16[272,512]{1,0:T(8,128)(2,1)}), bf16[1088,512]{1,0:T(8,128)(2,1)}) %all-gather.6.cloned.1.call-update) | async-done | bytes 1114128 | tf_op jit(solution)/shard_map/all_gather | solution.py:254
  118.1 0.0 copy-start
  118.1 1.4 copy-done
  119.5 0.0 copy-start.1
  119.6 1.2 copy-done.1
  120.8 1.3 shard_map.76
  122.1 27.9 %all_to_all.10.r_ref = bf16[32,160,128]{2,1,0:T(8,128)(2,1)S(1)} all-to-all(bf16[32,160,128]{2,1,0:T(8,128)(2,1)S(1)} %shard_map.76), channel_id=1, replica_groups=mesh['z'=16,'x'=4,'y'=4,'c'=2] {'x','y','c'}, dimensions={0} | all-to-all | bytes 2621440 | tf_op jit(solution)/shard_map/all_to_all | solution.py:258
  150.0 0.9 shard_map.77
Async XLA Ops:
  6.5 73.1 %all-gather.4.cloned.1.call-start = ((), (), s32[]{:S(2)}) async-start(), calls=%async_computation.2 | async-start | bytes 1740800 | tf_op jit(solution)/shard_map/all_gather | solution.py:224
  7.3 1.1 copy-start.2
  8.3 1.1 copy-start.3
  9.4 0.9 copy-start.4
  10.3 0.7 copy-start.5
  11.1 0.7 copy-start.6
  13.4 10.7 %copy-start.7 = (s32[64,8]{0,1:T(8,128)S(1)}, s32[64,8]{0,1:T(8,128)}, u32[]{:S(2)}) copy-start(s32[64,8]{0,1:T(8,128)} %param.12) | copy-start | bytes 6148
  13.4 33.4 %all-to-all-start = ((bf16[32,192,128]{2,1,0:T(8,128)(2,1)}), bf16[32,192,128]{2,1,0:T(8,128)(2,1)S(1)}, u32[]{:S(2)}, u32[]{:S(2)}) async-start(bf16[32,192,128]{2,1,0:T(8,128)(2,1)} %shard_map.73), calls=%async_computation | async-start | bytes 3145728 | tf_op jit(solution)/shard_map/all_to_all | solution.py:230
  24.0 94.1 %all-gather.6.cloned.1.call-start = ((), (), s32[]{:S(2)}) async-start(), calls=%async_computation.3 | async-start | bytes 1392640 | tf_op jit(solution)/shard_map/all_gather | solution.py:254
  48.1 10.3 %collective-permute-start = (bf16[8,160,128]{2,1,0:T(8,128)(2,1)S(1)}, bf16[8,160,128]{2,1,0:T(8,128)(2,1)S(1)}, u32[]{:S(2)}, u32[]{:S(2)}) collective-permute-start(bf16[8,160,128]{2,1,0:T(8,128)(2,1)S(1)} %get-tuple-element.7), channel_id=1, source_target_pairs={{0,32},{32,64},{64,96},{96,128},{128,160},{160,192},{192,224},{224... | collective-permute-start | bytes 983048 | tf_op jit(solution)/shard_map/ppermute | solution.py:238
  49.7 12.5 %collective-permute-start.1 = (bf16[8,160,128]{2,1,0:T(8,128)(2,1)S(1)}, bf16[8,160,128]{2,1,0:T(8,128)(2,1)S(1)}, u32[]{:S(2)}, u32[]{:S(2)}) collective-permute-start(bf16[8,160,128]{2,1,0:T(8,128)(2,1)S(1)} %get-tuple-element.8), channel_id=1, source_target_pairs={{32,0},{64,32},{96,64},{128,96},{160,128},{192,160},{224,192},{256... | collective-permute-start | bytes 983048 | tf_op jit(solution)/shard_map/ppermute | solution.py:239
  118.1 1.4 copy-start
  119.5 1.2 copy-start.1
Sparse Core Ops, SparseCore 0:
  9.4 70.1 all-gather.3
  81.7 36.3 all-gather.5

commit v2 on v1

--- a/solution.py
+++ b/solution.py
@@ -6,6 +6,7 @@
 from jax.sharding import Mesh, PartitionSpec as P
 
 HD = 128
+D = 5120
 HALF = 64
 QROWS = 16
 NX = 4
@@ -21,13 +22,25 @@
 SMEM = pl.BlockSpec(memory_space=pltpu.SMEM)
 ANY = pl.BlockSpec(memory_space=pl.ANY)
 LIMIT = 40 * 1024 * 1024
+ALL = 60 * 1024 * 1024
+FAR_STEPS = (4, 0, -4, 8)
+NEAR_STEPS = (0, 1, -1, 2, -2)
+NEAR_COUNT = (4, 4, 4, 2, 2)
+PLACES = [(i, FAR_STEPS[(1 if step == -2 else 0) + j]) for i, step in enumerate(NEAR_STEPS) for j in range(NEAR_COUNT[i])]
 
 
 def dot(a, b, contract):
     return lax.dot_general(a, b, ((contract[:1], contract[1:]), ((), ())), preferred_element_type=F32)
 
 
-def pack_kernel(q_ref, k_ref, v_ref, qg_ref, kg_ref, out_ref):
+def pack_kernel(q_hbm, k_hbm, v_hbm, qg_hbm, kg_hbm, out_ref, q_ref, k_ref, v_ref, qg_ref, kg_ref, sems):
+    pairs = ((k_hbm, k_ref), (kg_hbm, kg_ref), (q_hbm, q_ref), (qg_hbm, qg_ref), (v_hbm, v_ref))
+    copies = [pltpu.make_async_copy(*pair, sems.at[i]) for i, pair in enumerate(pairs)]
+    for copy in copies:
+        copy.start()
+    for copy in copies:
+        copy.wait()
+
     def inverse(ref):
         wide = ref[...].astype(F32)
         return lax.rsqrt(jnp.mean(wide * wide, axis=-1, keepdims=True) + 1e-06)
@@ -66,7 +79,8 @@
     return found
 
 
-def select_kernel(lists, zi, r_ref, up_ref, down_ref, sems):
+def select_kernel(lists, zi, r_ref, first_columns, up_ref, down_ref, sems):
+    del first_columns
     z = zi[0]
     above = jnp.minimum(z + 1, NZ - 1) * 4
     below = jnp.maximum(z - 1, 0) * 4
@@ -151,25 +165,36 @@
         raw = dot(kg[...], q, (1, 1)) * scale
         scores = jnp.concatenate([raw[m * 128 : m * 128 + 128] + biases[m] for m in range(MAXB)], axis=0)
         top, total, weights = softmax(scores)
-        out_ref[0:128, cols] = (dot(vg[...], weights, (0, 0)) / total).astype(BF)
+        own = (dot(vg[...], weights, (0, 0)) / total).astype(BF)
 
         q5 = win[x * NH : x * NH + NH, Q5 : Q5 + QROWS].reshape(128, HD)
         raw = dot(k5g[...], q5, (1, 1)) * scale
         scores = jnp.concatenate([raw[m * 32 : m * 32 + 32] + biases[m] for m in range(MAXB)], axis=0)
         top, total, weights = softmax(scores)
-        out_ref[128:256, cols] = (dot(v5g[...], weights, (0, 0)) / total).astype(BF)
+        shared = (dot(v5g[...], weights, (0, 0)) / total).astype(BF)
         level = top + jnp.log(total)
         high = level.astype(BF)
         rest = level - high.astype(F32)
         middle = rest.astype(BF)
         low = (rest - middle.astype(F32)).astype(BF)
         zeros = jnp.zeros((13, 128), F32)
-        out_ref[256:272, cols] = jnp.concatenate(
-            [high.astype(F32), middle.astype(F32), low.astype(F32), zeros], axis=0
-        ).astype(BF)
-
-
-def project_kernel(g_ref, w_ref, out_ref, a_ref):
+        pieces = jnp.concatenate([high.astype(F32), middle.astype(F32), low.astype(F32), zeros], axis=0).astype(BF)
+        for target in range(NX):
+            out_ref[target, 0:128, cols] = own
+            out_ref[target, 128:256, cols] = shared
+            out_ref[target, 256:272, cols] = pieces
+
+
+def project_kernel(zi, g_hbm, *rest):
+    weights, (out_ref, g_ref, w_ref, a_ref, sems) = rest[:5], rest[5:]
+    copies = [pltpu.make_async_copy(g_hbm, g_ref, sems.at[5])]
+    for i, w_hbm in enumerate(weights):
+        at = sum(NEAR_COUNT[:i])
+        copies.append(pltpu.make_async_copy(w_hbm, w_ref.at[pl.ds(at, NEAR_COUNT[i])], sems.at[i]))
+    for copy in copies:
+        copy.start()
+    for copy in copies:
+        copy.wait()
     levels = []
     for x in range(NX):
         parts = g_ref[x, 256:272].astype(F32)
@@ -183,10 +208,12 @@
         shared = shared + g_ref[x, 128:256].astype(F32) * (shares[x] / total)
     a_ref[512:640] = shared.astype(BF)
     a = a_ref[...]
-    for group in range(NH):
-        part = dot(w_ref[group * 160 : group * 160 + 160], a, (1, 0)).astype(BF)
+    for place, (near, stride) in enumerate(PLACES):
+        part = dot(w_ref[place], a, (1, 0)).astype(BF)
+        source = (zi[0] + NEAR_STEPS[near] + stride) & (NZ - 1)
+        rows = pl.ds(pl.multiple_of((source & 1) * 80, 80), 80)
         for x in range(NX):
-            out_ref[x * NH + group] = part[:, x * 128 : x * 128 + 128]
+            out_ref[x * NH + (source >> 1), rows] = part[:, x * 128 : x * 128 + 128]
 
 
 def final_kernel(r_ref, out_ref, t_ref):
@@ -199,15 +226,14 @@
     out_ref[...] = t_ref[...].T.astype(BF)
 
 
-def call(kernel, out, specs, out_specs=VMEM, scratch=(), cost=None):
+def call(kernel, out, specs, out_specs=VMEM, scratch=(), limit=LIMIT):
     return pl.pallas_call(
         kernel,
         out_shape=out,
         in_specs=specs,
         out_specs=out_specs,
         scratch_shapes=list(scratch),
-        compiler_params=pltpu.CompilerParams(vmem_limit_bytes=LIMIT),
-        cost_estimate=cost,
+        compiler_params=pltpu.CompilerParams(vmem_limit_bytes=limit),
     )
 
 
@@ -215,31 +241,45 @@
     return jax.ShapeDtypeStruct(dims, BF)
 
 
-def cost(us):
-    return pl.CostEstimate(flops=int(us * 1e9), bytes_accessed=1 << 20, transcendentals=0)
+def from_plane(value, step):
+    return lax.ppermute(value, "z", [((i + step) % NZ, i) for i in range(NZ)])
 
 
 def per_device(query_input, key_input, value_input, query_gain, key_gain, band_lists, out_weight):
     plane = ("x", "y", "c")
-    weight = lax.all_gather(out_weight.T, "z", axis=0, tiled=True)
     lists = band_lists.reshape(-1)
     zi = lax.axis_index("z").reshape(1)
-    packed = call(pack_kernel, shape(32, CHUNK, HD), [VMEM] * 5)(
-        query_input, key_input, value_input, query_gain.reshape(1, -1), key_gain.reshape(1, -1)
-    )
+    packed = call(
+        pack_kernel,
+        shape(32, CHUNK, HD),
+        [ANY] * 5,
+        VMEM,
+        [
+            pltpu.VMEM((QROWS, D), BF),
+            pltpu.VMEM((HALF, D), BF),
+            pltpu.VMEM((HALF, D), BF),
+            pltpu.VMEM((1, D), F32),
+            pltpu.VMEM((1, D), F32),
+            pltpu.SemaphoreType.DMA((5,)),
+        ],
+        ALL,
+    )(query_input, key_input, value_input, query_gain.reshape(1, -1), key_gain.reshape(1, -1))
+    packed, columns = lax.optimization_barrier((packed, out_weight.T))
+    far = jnp.stack([from_plane(columns, step) if step else columns for step in FAR_STEPS])
+    near = [far, from_plane(far, 1), from_plane(far, -1), from_plane(far[:2], 2), from_plane(far[1:3], -2)]
     mine = lax.all_to_all(packed, plane, split_axis=0, concat_axis=0, tiled=True)
     up, down = call(
         select_kernel,
         (shape(8, KV, HD), shape(8, KV, HD)),
-        [SMEM, SMEM, ANY],
+        [SMEM, SMEM, ANY, ANY],
         (ANY, ANY),
         [pltpu.SemaphoreType.DMA((8,))],
-    )(lists, zi, mine)
+    )(lists, zi, mine, far)
     before = lax.ppermute(up, "z", [(i, i + 1) for i in range(NZ - 1)])
     after = lax.ppermute(down, "z", [(i + 1, i) for i in range(NZ - 1)])
     attended = call(
         attend_kernel,
-        shape(272, 512),
+        shape(NX, 272, 512),
         [SMEM, SMEM, ANY, ANY, ANY],
         VMEM,
         [
@@ -251,10 +291,19 @@
             pltpu.SemaphoreType.DMA((3,)),
         ],
     )(lists, zi, mine, before, after)
-    gathered = lax.all_gather(attended, "x", axis=0, tiled=False)
-    terms = call(project_kernel, shape(32, 160, 128), [VMEM, VMEM], VMEM, [pltpu.VMEM((640, 512), BF)])(
-        gathered, weight
-    )
+    gathered = lax.all_to_all(attended, "x", split_axis=0, concat_axis=0, tiled=True)
+    terms = call(
+        project_kernel,
+        shape(32, 160, 128),
+        [SMEM] + [ANY] * 6,
+        VMEM,
+        [
+            pltpu.VMEM((NX, 272, 512), BF),
+            pltpu.VMEM((NZ, 80, 640), BF),
+            pltpu.VMEM((640, 512), BF),
+            pltpu.SemaphoreType.DMA((6,)),
+        ],
+    )(zi, gathered, *near)
     summands = lax.all_to_all(terms, plane, split_axis=0, concat_axis=0, tiled=True)
     return call(final_kernel, shape(128, 640), [VMEM], VMEM, [pltpu.VMEM((640, 128), F32)])(summands)
 

time: 158 us -> 130 us (0.82); the launches traced: 158 us -> 128 us
  waiting for transfers between devices: 87.1 us -> 33.7 us
  starting transfers between devices: 13.5 us -> 51.6 us
  between operations: 13.5 us -> 0.19 us
  local copies, waits for them, and re-layouts: 7.39 us -> 0.19 us
  Pallas kernels: 8.32 us -> 12.2 us
  blocking collectives: 27.9 us -> 29.8 us
    all_gather x2 -> x0, waiting for transfers between devices: 52.6 us -> none  [the longest x1 38.5 us: per_device(): gathered = lax.all_gather(attended, 'x', axis=0, tiled=False)]
    ppermute x0 -> x7, starting transfers between devices: none -> 34.2 us  [from_plane(): return lax.ppermute(value, 'z', [((i + step) % NZ, i) for i in range(NZ)])]
    ppermute x0 -> x7, waiting for transfers between devices: none -> 24.4 us  [from_plane(): return lax.ppermute(value, 'z', [((i + step) % NZ, i) for i in range(NZ)])]
    all_to_all x1, waiting for transfers between devices: 22.5 us -> 0.01 us  [per_device(): lax.all_to_all(packed, plane, split_axis=0, concat_axis=0, tiled=True)]
    unnamed x17 -> x5, local copies, waits for them, and re-layouts: 7.3 us -> 0.1 us
    all_to_all x0 -> x1, starting transfers between devices: none -> 4.18 us  [per_device(): lax.all_to_all(attended, 'x', split_axis=0, concat_axis=0, tiled=True)]
    pallas_call x3, Pallas kernels: 6.07 us -> 9.99 us  [the longest x1 3.54 us: per_device(): call(attend_kernel, shape(NX, 272, 512), [SMEM, SMEM, ANY, ANY, ANY], VME...]
    ppermute x1, waiting for transfers between devices: 7.48 us -> 5.41 us  [per_device(): before = lax.ppermute(up, 'z', [(i, i + 1) for i in range(NZ - 1)])]
  transfers between devices with their start and end apart: 5 -> 11, of which waited for: 5 -> 5; matrix products, arithmetic and copies ran while one was open for 0% -> 0% of each run, Pallas kernels for 4% -> 0%
where the time goes in v2:
time: 130 us; the launch traced here: 128 us
  starting transfers between devices  51.6 us (40%)
  waiting for transfers between devices  33.7 us (26%)
  blocking collectives  29.8 us (23%)
  Pallas kernels  12.2 us (9%)
    ppermute x7, starting transfers between devices, from_plane(): return lax.ppermute(value, 'z', [((i + step) % NZ, i) for i in range(NZ)])  34.2 us
    all_to_all x1, blocking collectives, per_device(): lax.all_to_all(terms, plane, split_axis=0, concat_axis=0, tiled=True)  29.8 us
    ppermute x7, waiting for transfers between devices, from_plane(): return lax.ppermute(value, 'z', [((i + step) % NZ, i) for i in range(NZ)])  24.4 us
    all_to_all x1, starting transfers between devices, per_device(): lax.all_to_all(packed, plane, split_axis=0, concat_axis=0, tiled=True)  10.6 us
    ppermute x1, waiting for transfers between devices, per_device(): before = lax.ppermute(up, 'z', [(i, i + 1) for i in range(NZ - 1)])  5.41 us
    all_to_all x1, starting transfers between devices, per_device(): lax.all_to_all(attended, 'x', split_axis=0, concat_axis=0, tiled=True)  4.18 us
    ppermute x1, waiting for transfers between devices, per_device(): after = lax.ppermute(down, 'z', [(i + 1, i) for i in range(NZ - 1)])  3.81 us
    pallas_call x1, Pallas kernels, per_device(): call(attend_kernel, shape(NX, 272, 512), [SMEM, SMEM, ANY, ANY, ANY], VME...  3.54 us
  transfers between devices with their start and end apart: 11, of which 5 were waited for; matrix products, arithmetic and copies ran while one was open for 0% of the time, Pallas kernels for 0%

profile of v2, /device:TPU:1, one launch (start us, length us, event | category | flops | bytes accessed | tf_op | source)
XLA Modules:
  0.0 127.8 jit_solution(1278220563297408012)
XLA Ops:
  0.0 3.0 %shard_map.73 = bf16[32,192,128]{2,1,0:T(8,128)(2,1)} custom-call(bf16[16,5120]{1,0:T(8,128)(2,1)} %q_hbm.1, bf16[64,5120]{1,0:T(8,128)(2,1)} %k_hbm.1, bf16[64,5120]{1,0:T(8,128)(2,1)} %v_hbm.1, f32[1,5120]{1,0:T(1,128)} %bitcast.18, f32[1,5120]{1,0:T(1,128)} %bitcast.19), custom_call_target="tpu_custom_call" | custom-call | tf_op jit(solution)/shard_map/pallas_call | solution.py:252
  3.0 0.0 copy-start
  3.0 0.0 copy-start.1
  3.0 10.6 %all-to-all-start = ((bf16[32,192,128]{2,1,0:T(8,128)(2,1)}), bf16[32,192,128]{2,1,0:T(8,128)(2,1)S(1)}, u32[]{:S(2)}, u32[]{:S(2)}) async-start(bf16[32,192,128]{2,1,0:T(8,128)(2,1)} %shard_map.73), calls=%async_computation | async-start | bytes 3145728 | tf_op jit(solution)/shard_map/all_to_all | solution.py:270
  13.7 0.0 copy-done
  13.7 10.5 %collective-permute-start = (bf16[80,640]{1,0:T(8,128)(2,1)S(1)}, bf16[80,640]{1,0:T(8,128)(2,1)S(1)}, u32[]{:S(2)}, u32[]{:S(2)}) collective-permute-start(bf16[80,640]{1,0:T(8,128)(2,1)S(1)} %bitcast.8), channel_id=1, source_target_pairs={{128,0},{160,32},{192,64},{224,96},{256,128},{288,160},{320,192},{... | collective-permute-start | bytes 307208 | tf_op jit(solution)/shard_map/ppermute | solution.py:245
  24.2 1.9 %collective-permute-start.1 = (bf16[80,640]{1,0:T(8,128)(2,1)S(1)}, bf16[80,640]{1,0:T(8,128)(2,1)S(1)}, u32[]{:S(2)}, u32[]{:S(2)}) collective-permute-start(bf16[80,640]{1,0:T(8,128)(2,1)S(1)} %bitcast.9), channel_id=1, source_target_pairs={{384,0},{416,32},{448,64},{480,96},{0,128},{32,160},{64,192},{96,2... | collective-permute-start | bytes 307208 | tf_op jit(solution)/shard_map/ppermute | solution.py:245
  26.2 10.3 %collective-permute-start.2 = (bf16[80,640]{1,0:T(8,128)(2,1)S(1)}, bf16[80,640]{1,0:T(8,128)(2,1)S(1)}, u32[]{:S(2)}, u32[]{:S(2)}) collective-permute-start(bf16[80,640]{1,0:T(8,128)(2,1)S(1)} %bitcast.10), channel_id=1, source_target_pairs={{256,0},{288,32},{320,64},{352,96},{384,128},{416,160},{448,192},{... | collective-permute-start | bytes 307208 | tf_op jit(solution)/shard_map/ppermute | solution.py:245
  36.4 0.0 copy-done.1
  36.5 0.1 copy.8
  36.5 0.1 reshape.13.lists
  36.6 0.0 collective-permute-done
  36.6 0.0 collective-permute-done.1
  36.7 15.7 %collective-permute-done.2 = bf16[80,640]{1,0:T(8,128)(2,1)S(1)} collective-permute-done((bf16[80,640]{1,0:T(8,128)(2,1)S(1)}, bf16[80,640]{1,0:T(8,128)(2,1)S(1)}, u32[]{:S(2)}, u32[]{:S(2)}) %collective-permute-start.2) | collective-permute-done | bytes 102432 | tf_op jit(solution)/shard_map/ppermute | solution.py:245
  52.4 0.1 pad_maximum_fusion.first_columns.rest_0_
  52.4 0.0 all-to-all-done.r_ref
  52.5 1.3 %shard_map.74 = (bf16[8,160,128]{2,1,0:T(8,128)(2,1)S(1)}, bf16[8,160,128]{2,1,0:T(8,128)(2,1)S(1)}) custom-call(s32[512]{0:T(512)S(1)} %reshape.13.lists, s32[1]{0:T(128)} %bitcast.zi, bf16[32,192,128]{2,1,0:T(8,128)(2,1)S(1)} %all-to-all-done.r_ref, bf16[4,80,640]{2,1,0:T(8,128)(2,1)S(1)} %pad_maximum_fusion.first_columns.rest_0_), custom_call_target="tpu_custom_call" | custom-call | tf_op jit(solution)/shard_map/pallas_call | solution.py:271
  53.8 1.3 %collective-permute-start.3 = (bf16[8,160,128]{2,1,0:T(8,128)(2,1)S(1)}, bf16[8,160,128]{2,1,0:T(8,128)(2,1)S(1)}, u32[]{:S(2)}, u32[]{:S(2)}) collective-permute-start(bf16[8,160,128]{2,1,0:T(8,128)(2,1)S(1)} %get-tuple-element.11), channel_id=1, source_target_pairs={{0,32},{32,64},{64,96},{96,128},{128,160},{160,192},{192,224},{224... | collective-permute-start | bytes 983048 | tf_op jit(solution)/shard_map/ppermute | solution.py:278
  55.1 1.3 %collective-permute-start.4 = (bf16[8,160,128]{2,1,0:T(8,128)(2,1)S(1)}, bf16[8,160,128]{2,1,0:T(8,128)(2,1)S(1)}, u32[]{:S(2)}, u32[]{:S(2)}) collective-permute-start(bf16[8,160,128]{2,1,0:T(8,128)(2,1)S(1)} %get-tuple-element.12), channel_id=1, source_target_pairs={{32,0},{64,32},{96,64},{128,96},{160,128},{192,160},{224,192},{256... | collective-permute-start | bytes 983048 | tf_op jit(solution)/shard_map/ppermute | solution.py:279
  56.4 5.4 %collective-permute-done.3.prev_ref = bf16[8,160,128]{2,1,0:T(8,128)(2,1)S(1)} collective-permute-done((bf16[8,160,128]{2,1,0:T(8,128)(2,1)S(1)}, bf16[8,160,128]{2,1,0:T(8,128)(2,1)S(1)}, u32[]{:S(2)}, u32[]{:S(2)}) %collective-permute-start.3) | collective-permute-done | bytes 327712 | tf_op jit(solution)/shard_map/ppermute | solution.py:278
  61.8 3.8 %collective-permute-done.4.next_ref = bf16[8,160,128]{2,1,0:T(8,128)(2,1)S(1)} collective-permute-done((bf16[8,160,128]{2,1,0:T(8,128)(2,1)S(1)}, bf16[8,160,128]{2,1,0:T(8,128)(2,1)S(1)}, u32[]{:S(2)}, u32[]{:S(2)}) %collective-permute-start.4) | collective-permute-done | bytes 327712 | tf_op jit(solution)/shard_map/ppermute | solution.py:279
  65.7 3.5 %shard_map.75 = bf16[4,272,512]{2,1,0:T(8,128)(2,1)} custom-call(s32[512]{0:T(512)S(1)} %reshape.13.lists, s32[1]{0:T(128)} %bitcast.zi, bf16[32,192,128]{2,1,0:T(8,128)(2,1)S(1)} %all-to-all-done.r_ref, bf16[8,160,128]{2,1,0:T(8,128)(2,1)S(1)} %collective-permute-done.3.prev_ref, bf16[8,160,128]{2,1,0:T(8,128)(2,1)S(1)} %collective-permute-done.4.next_ref), custom_call_target="tpu_custom_call" | custom-call | tf_op jit(solution)/shard_map/pallas_call | solution.py:280
  69.2 4.2 %all-to-all-start.1 = ((bf16[4,272,512]{2,1,0:T(8,128)(2,1)}), bf16[4,272,512]{2,1,0:T(8,128)(2,1)S(1)}, u32[]{:S(2)}, u32[]{:S(2)}) async-start(bf16[4,272,512]{2,1,0:T(8,128)(2,1)} %shard_map.75), calls=%async_computation.1 | async-start | bytes 2228224 | tf_op jit(solution)/shard_map/all_to_all | solution.py:294
  73.4 1.9 %collective-permute-start.5 = (bf16[4,80,640]{2,1,0:T(8,128)(2,1)S(1)}, bf16[4,80,640]{2,1,0:T(8,128)(2,1)S(1)}, u32[]{:S(2)}, u32[]{:S(2)}) collective-permute-start(bf16[4,80,640]{2,1,0:T(8,128)(2,1)S(1)} %pad_maximum_fusion.first_columns.rest_0_), channel_id=1, source_target_pairs={{32,0},{64,32},{96,64},{128,96},{160,128},{192,160},{224,192},{256... | collective-permute-start | bytes 1228808 | tf_op jit(solution)/shard_map/ppermute | solution.py:245
  75.3 3.4 %collective-permute-start.6 = (bf16[4,80,640]{2,1,0:T(8,128)(2,1)S(1)}, bf16[4,80,640]{2,1,0:T(8,128)(2,1)S(1)}, u32[]{:S(2)}, u32[]{:S(2)}) collective-permute-start(bf16[4,80,640]{2,1,0:T(8,128)(2,1)S(1)} %pad_maximum_fusion.first_columns.rest_0_), channel_id=1, source_target_pairs={{480,0},{0,32},{32,64},{64,96},{96,128},{128,160},{160,192},{192,2... | collective-permute-start | bytes 1228808 | tf_op jit(solution)/shard_map/ppermute | solution.py:245
  78.7 1.9 %collective-permute-start.7 = (bf16[2,80,640]{2,1,0:T(8,128)(2,1)S(1)}, bf16[2,80,640]{2,1,0:T(8,128)(2,1)S(1)}, u32[]{:S(2)}, u32[]{:S(2)}) collective-permute-start(bf16[2,80,640]{2,1,0:T(8,128)(2,1)S(1)} %get-tuple-element.14), channel_id=1, source_target_pairs={{64,0},{96,32},{128,64},{160,96},{192,128},{224,160},{256,192},{28... | collective-permute-start | bytes 614408 | tf_op jit(solution)/shard_map/ppermute | solution.py:245
  80.6 4.3 %collective-permute-start.8 = (bf16[2,80,640]{2,1,0:T(8,128)(2,1)S(1)}, bf16[2,80,640]{2,1,0:T(8,128)(2,1)S(1)}, u32[]{:S(2)}, u32[]{:S(2)}) collective-permute-start(bf16[2,80,640]{2,1,0:T(8,128)(2,1)S(1)} %get-tuple-element.13), channel_id=1, source_target_pairs={{448,0},{480,32},{0,64},{32,96},{64,128},{96,160},{128,192},{160,2... | collective-permute-start | bytes 614408 | tf_op jit(solution)/shard_map/ppermute | solution.py:245
  84.9 8.0 %collective-permute-done.7.rest_3_ = bf16[2,80,640]{2,1,0:T(8,128)(2,1)S(1)} collective-permute-done((bf16[2,80,640]{2,1,0:T(8,128)(2,1)S(1)}, bf16[2,80,640]{2,1,0:T(8,128)(2,1)S(1)}, u32[]{:S(2)}, u32[]{:S(2)}) %collective-permute-start.7) | collective-permute-done | bytes 204832 | tf_op jit(solution)/shard_map/ppermute | solution.py:245
  93.0 0.6 collective-permute-done.8.rest_4_
  93.6 0.0 collective-permute-done.5.rest_1_
  93.6 0.0 collective-permute-done.6.rest_2_
  93.6 0.0 all-to-all-done.1.g_hbm
  93.6 3.4 %shard_map.76 = bf16[32,160,128]{2,1,0:T(8,128)(2,1)S(1)} custom-call(s32[1]{0:T(128)} %bitcast.zi, bf16[4,272,512]{2,1,0:T(8,128)(2,1)S(1)} %all-to-all-done.1.g_hbm, bf16[4,80,640]{2,1,0:T(8,128)(2,1)S(1)} %pad_maximum_fusion.first_columns.rest_0_, bf16[4,80,640]{2,1,0:T(8,128)(2,1)S(1)} %collective-permute-done.5.rest_1_, ...), custom_call_target="tpu_custom_call" | custom-call | tf_op jit(solution)/shard_map/pallas_call | solution.py:295
  97.1 29.8 %all_to_all.15.r_ref = bf16[32,160,128]{2,1,0:T(8,128)(2,1)S(1)} all-to-all(bf16[32,160,128]{2,1,0:T(8,128)(2,1)S(1)} %shard_map.76), channel_id=1, replica_groups=mesh['z'=16,'x'=4,'y'=4,'c'=2] {'x','y','c'}, dimensions={0} | all-to-all | bytes 2621440 | tf_op jit(solution)/shard_map/all_to_all | solution.py:307
  126.9 0.9 shard_map.77
  (1 shorter events, 0.0 us)
Async XLA Ops:
  3.0 10.7 %copy-start = (bf16[640,80]{0,1:T(8,128)(2,1)S(1)}, bf16[640,80]{0,1:T(8,128)(2,1)}, u32[]{:S(2)}) copy-start(bf16[640,80]{0,1:T(8,128)(2,1)} %param.13) | copy-start | bytes 307204
  3.0 33.4 %copy-start.1 = (s32[64,8]{0,1:T(8,128)S(1)}, s32[64,8]{0,1:T(8,128)}, u32[]{:S(2)}) copy-start(s32[64,8]{0,1:T(8,128)} %param.12) | copy-start | bytes 6148
  3.0 49.4 %all-to-all-start = ((bf16[32,192,128]{2,1,0:T(8,128)(2,1)}), bf16[32,192,128]{2,1,0:T(8,128)(2,1)S(1)}, u32[]{:S(2)}, u32[]{:S(2)}) async-start(bf16[32,192,128]{2,1,0:T(8,128)(2,1)} %shard_map.73), calls=%async_computation | async-start | bytes 3145728 | tf_op jit(solution)/shard_map/all_to_all | solution.py:270
  13.7 22.9 %collective-permute-start = (bf16[80,640]{1,0:T(8,128)(2,1)S(1)}, bf16[80,640]{1,0:T(8,128)(2,1)S(1)}, u32[]{:S(2)}, u32[]{:S(2)}) collective-permute-start(bf16[80,640]{1,0:T(8,128)(2,1)S(1)} %bitcast.8), channel_id=1, source_target_pairs={{128,0},{160,32},{192,64},{224,96},{256,128},{288,160},{320,192},{... | collective-permute-start | bytes 307208 | tf_op jit(solution)/shard_map/ppermute | solution.py:245
  24.2 12.4 %collective-permute-start.1 = (bf16[80,640]{1,0:T(8,128)(2,1)S(1)}, bf16[80,640]{1,0:T(8,128)(2,1)S(1)}, u32[]{:S(2)}, u32[]{:S(2)}) collective-permute-start(bf16[80,640]{1,0:T(8,128)(2,1)S(1)} %bitcast.9), channel_id=1, source_target_pairs={{384,0},{416,32},{448,64},{480,96},{0,128},{32,160},{64,192},{96,2... | collective-permute-start | bytes 307208 | tf_op jit(solution)/shard_map/ppermute | solution.py:245
  26.2 26.2 %collective-permute-start.2 = (bf16[80,640]{1,0:T(8,128)(2,1)S(1)}, bf16[80,640]{1,0:T(8,128)(2,1)S(1)}, u32[]{:S(2)}, u32[]{:S(2)}) collective-permute-start(bf16[80,640]{1,0:T(8,128)(2,1)S(1)} %bitcast.10), channel_id=1, source_target_pairs={{256,0},{288,32},{320,64},{352,96},{384,128},{416,160},{448,192},{... | collective-permute-start | bytes 307208 | tf_op jit(solution)/shard_map/ppermute | solution.py:245
  53.8 8.0 %collective-permute-start.3 = (bf16[8,160,128]{2,1,0:T(8,128)(2,1)S(1)}, bf16[8,160,128]{2,1,0:T(8,128)(2,1)S(1)}, u32[]{:S(2)}, u32[]{:S(2)}) collective-permute-start(bf16[8,160,128]{2,1,0:T(8,128)(2,1)S(1)} %get-tuple-element.11), channel_id=1, source_target_pairs={{0,32},{32,64},{64,96},{96,128},{128,160},{160,192},{192,224},{224... | collective-permute-start | bytes 983048 | tf_op jit(solution)/shard_map/ppermute | solution.py:278
  55.1 10.5 %collective-permute-start.4 = (bf16[8,160,128]{2,1,0:T(8,128)(2,1)S(1)}, bf16[8,160,128]{2,1,0:T(8,128)(2,1)S(1)}, u32[]{:S(2)}, u32[]{:S(2)}) collective-permute-start(bf16[8,160,128]{2,1,0:T(8,128)(2,1)S(1)} %get-tuple-element.12), channel_id=1, source_target_pairs={{32,0},{64,32},{96,64},{128,96},{160,128},{192,160},{224,192},{256... | collective-permute-start | bytes 983048 | tf_op jit(solution)/shard_map/ppermute | solution.py:279
  69.2 24.4 %all-to-all-start.1 = ((bf16[4,272,512]{2,1,0:T(8,128)(2,1)}), bf16[4,272,512]{2,1,0:T(8,128)(2,1)S(1)}, u32[]{:S(2)}, u32[]{:S(2)}) async-start(bf16[4,272,512]{2,1,0:T(8,128)(2,1)} %shard_map.75), calls=%async_computation.1 | async-start | bytes 2228224 | tf_op jit(solution)/shard_map/all_to_all | solution.py:294
  73.4 20.2 %collective-permute-start.5 = (bf16[4,80,640]{2,1,0:T(8,128)(2,1)S(1)}, bf16[4,80,640]{2,1,0:T(8,128)(2,1)S(1)}, u32[]{:S(2)}, u32[]{:S(2)}) collective-permute-start(bf16[4,80,640]{2,1,0:T(8,128)(2,1)S(1)} %pad_maximum_fusion.first_columns.rest_0_), channel_id=1, source_target_pairs={{32,0},{64,32},{96,64},{128,96},{160,128},{192,160},{224,192},{256... | collective-permute-start | bytes 1228808 | tf_op jit(solution)/shard_map/ppermute | solution.py:245
  75.3 18.3 %collective-permute-start.6 = (bf16[4,80,640]{2,1,0:T(8,128)(2,1)S(1)}, bf16[4,80,640]{2,1,0:T(8,128)(2,1)S(1)}, u32[]{:S(2)}, u32[]{:S(2)}) collective-permute-start(bf16[4,80,640]{2,1,0:T(8,128)(2,1)S(1)} %pad_maximum_fusion.first_columns.rest_0_), channel_id=1, source_target_pairs={{480,0},{0,32},{32,64},{64,96},{96,128},{128,160},{160,192},{192,2... | collective-permute-start | bytes 1228808 | tf_op jit(solution)/shard_map/ppermute | solution.py:245
  78.7 14.2 %collective-permute-start.7 = (bf16[2,80,640]{2,1,0:T(8,128)(2,1)S(1)}, bf16[2,80,640]{2,1,0:T(8,128)(2,1)S(1)}, u32[]{:S(2)}, u32[]{:S(2)}) collective-permute-start(bf16[2,80,640]{2,1,0:T(8,128)(2,1)S(1)} %get-tuple-element.14), channel_id=1, source_target_pairs={{64,0},{96,32},{128,64},{160,96},{192,128},{224,160},{256,192},{28... | collective-permute-start | bytes 614408 | tf_op jit(solution)/shard_map/ppermute | solution.py:245
  80.6 13.0 %collective-permute-start.8 = (bf16[2,80,640]{2,1,0:T(8,128)(2,1)S(1)}, bf16[2,80,640]{2,1,0:T(8,128)(2,1)S(1)}, u32[]{:S(2)}, u32[]{:S(2)}) collective-permute-start(bf16[2,80,640]{2,1,0:T(8,128)(2,1)S(1)} %get-tuple-element.13), channel_id=1, source_target_pairs={{448,0},{480,32},{0,64},{32,96},{64,128},{96,160},{128,192},{160,2... | collective-permute-start | bytes 614408 | tf_op jit(solution)/shard_map/ppermute | solution.py:245

commit v3 on v2

v3 whole, which is shorter than its diff:
```python
import jax
import jax.numpy as jnp
from jax import lax
from jax.experimental import pallas as pl
from jax.experimental.pallas import tpu as pltpu
from jax.sharding import Mesh, PartitionSpec as P

HD = 128
D = 5120
HALF = 64
QROWS = 16
NX = 4
NH = 8
NZ = 16
MAXB = 8
GROUP = 5
K0, V0, K5, V5, Q0, Q5, CHUNK = 0, 64, 128, 144, 160, 176, 192
KV = 160
BF = jnp.bfloat16
F32 = jnp.float32
VMEM = pl.BlockSpec(memory_space=pltpu.VMEM)
SMEM = pl.BlockSpec(memory_space=pltpu.SMEM)
ANY = pl.BlockSpec(memory_space=pl.ANY)
LIMIT = 40 * 1024 * 1024
ALL = 60 * 1024 * 1024
HELD = (0, 5, -6)
LAST = -3
BLOCK = 400
SK, SV, SK5, SV5, SW = 0, 512, 1024, 1152, 1280
SENT = SW + 3 * BLOCK


def dot(a, b, contract):
    return lax.dot_general(a, b, ((contract[:1], contract[1:]), ((), ())), preferred_element_type=F32)


def pack_kernel(q_hbm, k_hbm, v_hbm, qg_hbm, kg_hbm, out_ref, q_ref, k_ref, v_ref, qg_ref, kg_ref, sems):
    pairs = ((k_hbm, k_ref), (kg_hbm, kg_ref), (q_hbm, q_ref), (qg_hbm, qg_ref), (v_hbm, v_ref))
    copies = [pltpu.make_async_copy(*pair, sems.at[i]) for i, pair in enumerate(pairs)]
    for copy in copies:
        copy.start()
    for copy in copies[:4]:
        copy.wait()

    def inverse(ref):
        wide = ref[...].astype(F32)
        return lax.rsqrt(jnp.mean(wide * wide, axis=-1, keepdims=True) + 1e-06)

    k_inv, q_inv = inverse(k_ref), inverse(q_ref)

    def heads():
        for group in range(NH):
            for at in range(GROUP):
                yield group, at, slice((group * GROUP + at) * HD, (group * GROUP + at + 1) * HD)

    for group, at, cols in heads():
        k = (k_ref[:, cols].astype(F32) * k_inv * kg_ref[:, cols]).astype(BF)
        q = (q_ref[:, cols].astype(F32) * q_inv * qg_ref[:, cols]).astype(BF)
        if at < NX:
            out_ref[at * NH + group, K0 : K0 + HALF] = k
            out_ref[at * NH + group, Q0 : Q0 + QROWS] = q
        else:
            for x in range(NX):
                out_ref[x * NH + group, K5 : K5 + 16] = k[x * 16 : x * 16 + 16]
                out_ref[x * NH + group, Q5 : Q5 + QROWS] = q
    copies[4].wait()
    for group, at, cols in heads():
        if at < NX:
            out_ref[at * NH + group, V0 : V0 + HALF] = v_ref[:, cols]
        else:
            for x in range(NX):
                out_ref[x * NH + group, V5 : V5 + 16] = v_ref[x * 16 : x * 16 + 16, cols]


def listed_of(lists, block, seq, count):
    found = [jnp.int32(-1)] * count
    for m in range(MAXB):
        entry = lists[block * MAXB + m]
        hit = (entry >= 0) & ((entry >> 2) == seq)
        for i in reversed(range(count)):
            free = found[i] < 0
            if i:
                free = free & (found[i - 1] >= 0)
            found[i] = jnp.where(hit & free, entry, found[i])
    return found


def listed_above(lists, z):
    block = jnp.minimum(z + 1, NZ - 1) * 4
    seq = z * 4
    return (
        listed_of(lists, block, seq + 2, 1) + listed_of(lists, block, seq + 3, 2) + listed_of(lists, block + 1, seq + 3, 1)
    )


def listed_below(lists, z):
    block = jnp.maximum(z - 1, 0) * 4
    seq = z * 4
    return (
        listed_of(lists, block + 3, seq + 1, 1) + listed_of(lists, block + 3, seq, 2) + listed_of(lists, block + 2, seq, 1)
    )


def select_kernel(lists, zi, r_ref, *rest):
    held, (up_ref, down_ref) = rest[:3], rest[3:]
    z = zi[0]
    for blocks, target in ((listed_above(lists, z), up_ref), (listed_below(lists, z), down_ref)):
        for slot, block in enumerate(blocks):
            at = jnp.clip(block - z * 16, 0, 15)
            for half in range(2):
                source, part = r_ref.at[at * 2 + half], slot * 2 + half
                target[SK + part * 64 : SK + part * 64 + 64] = source[K0 : K0 + 64]
                target[SV + part * 64 : SV + part * 64 + 64] = source[V0 : V0 + 64]
                target[SK5 + part * 16 : SK5 + part * 16 + 16] = source[K5 : K5 + 16]
                target[SV5 + part * 16 : SV5 + part * 16 + 16] = source[V5 : V5 + 16]
        for i, ref in enumerate(held):
            target[SW + i * BLOCK : SW + i * BLOCK + BLOCK] = ref[...]


def queries(r_ref, x, first):
    return r_ref[x * NH : x * NH + NH, first : first + QROWS].reshape(128, HD)


def scored(keys, q, biases):
    raw = dot(keys, q, (1, 1)) * HD**-0.5
    rows = keys.shape[0] // len(biases)
    return jnp.concatenate([raw[i * rows : i * rows + rows] + bias for i, bias in enumerate(biases)], axis=0)


def attend_own_kernel(lists, zi, r_ref, sum_ref, stat_ref, kg, vg, k5g, v5g):
    z = zi[0]
    for x in range(NX):
        biases = []
        for m in range(MAXB):
            entry = lists[(z * 4 + x) * MAXB + m]
            here = (entry >> 4) == z
            at = jnp.where(here, entry - z * 16, 0)
            biases.append(jnp.where(here, 0.0, -jnp.inf))
            for half in range(2):
                row = m * 2 + half
                block = r_ref.at[at * 2 + half]
                kg[row * 64 : row * 64 + 64] = block[K0 : K0 + 64]
                vg[row * 64 : row * 64 + 64] = block[V0 : V0 + 64]
                k5g[row * 16 : row * 16 + 16] = block[K5 : K5 + 16]
                v5g[row * 16 : row * 16 + 16] = block[V5 : V5 + 16]
        cols = slice(x * 128, x * 128 + 128)
        for i, (keys, values, first) in enumerate(((kg, vg, Q0), (k5g, v5g, Q5))):
            scores = scored(keys[...], queries(r_ref, x, first), biases)
            top = jnp.max(scores, axis=0, keepdims=True)
            exponent = jnp.exp(scores - top)
            stat_ref[i * 2 : i * 2 + 1, cols] = top
            stat_ref[i * 2 + 1 : i * 2 + 2, cols] = jnp.sum(exponent, axis=0, keepdims=True)
            sum_ref[i * 128 : i * 128 + 128, cols] = dot(values[...], exponent.astype(BF), (0, 0))


def attend_rest_kernel(lists, zi, r_ref, prev_ref, next_ref, sum_ref, stat_ref, last, out_ref, above_ref, below_ref):
    del last
    z = zi[0]
    below_ref[...] = prev_ref[SW:]
    above_ref[...] = next_ref[SW:]
    near = listed_above(lists, z - 1), listed_below(lists, z + 1)
    for x in range(NX):
        ref, side = ((prev_ref, 0), (next_ref, 1))[x // 2]
        first, count = (0, 3) if x in (0, 3) else (3, 1)
        found = near[side][first : first + count]
        inside = (z > 0) if side == 0 else (z < NZ - 1)
        biases = [jnp.where((block >= 0) & inside, 0.0, -jnp.inf) for block in found]
        cols = slice(x * 128, x * 128 + 128)
        for i, (key_row, value_row, size, query_row) in enumerate(((SK, SV, 128, Q0), (SK5, SV5, 32, Q5))):
            keys = ref[key_row + first * size : key_row + (first + count) * size]
            values = ref[value_row + first * size : value_row + (first + count) * size]
            scores = scored(keys, queries(r_ref, x, query_row), biases)
            old = stat_ref[i * 2 : i * 2 + 1, cols]
            top = jnp.maximum(old, jnp.max(scores, axis=0, keepdims=True))
            exponent = jnp.exp(scores - top)
            share = jnp.exp(old - top)
            total = stat_ref[i * 2 + 1 : i * 2 + 2, cols] * share + jnp.sum(exponent, axis=0, keepdims=True)
            added = sum_ref[i * 128 : i * 128 + 128, cols] * share + dot(values, exponent.astype(BF), (0, 0))
            result = (added / total).astype(BF)
            for target in range(NX):
                out_ref[target, i * 128 : i * 128 + 128, cols] = result
        level = top + jnp.log(total)
        high = level.astype(BF)
        left = level - high.astype(F32)
        middle = left.astype(BF)
        low = (left - middle.astype(F32)).astype(BF)
        zeros = jnp.zeros((13, 128), F32)
        pieces = jnp.concatenate([high.astype(F32), middle.astype(F32), low.astype(F32), zeros], axis=0).astype(BF)
        for target in range(NX):
            out_ref[target, 256:272, cols] = pieces


def project_kernel(ci, zi, g_ref, own, up5, down6, last, before, after, before2, after2, keep_ref, give_ref, a_ref, w_ref):
    blocks = [(last, 0, LAST)] + [(ref, 0, step) for ref, step in zip((own, up5, down6), HELD)]
    for ref, step in ((before, -1), (after, 1), (before2, -2), (after2, 2)):
        blocks += [(ref, i * BLOCK, step + offset) for i, offset in enumerate(HELD)]
    for ref, first, step in blocks:
        rows = pl.ds(pl.multiple_of(((zi[0] + step) & (NZ - 1)) * 80, 80), 80)
        for head in range(GROUP):
            w_ref[rows, head * HD : head * HD + HD] = ref[first + head * 80 : first + head * 80 + 80]
    levels = []
    for x in range(NX):
        parts = g_ref[x, 256:272].astype(F32)
        levels.append(parts[0:1] + parts[1:2] + parts[2:3])
    top = jnp.maximum(jnp.maximum(levels[0], levels[1]), jnp.maximum(levels[2], levels[3]))
    shares = [jnp.exp(level - top) for level in levels]
    total = shares[0] + shares[1] + shares[2] + shares[3]
    shared = jnp.zeros((128, 512), F32)
    for x in range(NX):
        a_ref[x * 128 : x * 128 + 128] = g_ref[x, 0:128]
        shared = shared + g_ref[x, 128:256].astype(F32) * (shares[x] / total)
    a_ref[512:640] = shared.astype(BF)
    a = a_ref[...]
    for other, target in ((1, give_ref), (0, keep_ref)):
        parity = ci[0] ^ other
        for y in range(4):
            rows = pl.ds(pl.multiple_of((2 * y + parity) * 160, 160), 160)
            part = dot(w_ref[rows], a, (1, 0)).astype(BF)
            for x in range(NX):
                target[x * 4 + y] = part[:, x * 128 : x * 128 + 128]


def final_kernel(r_ref, out_ref, t_ref):
    for x in range(NX):
        total = r_ref[x * 4].astype(F32)
        for y in range(1, 4):
            total = total + r_ref[x * 4 + y].astype(F32)
        t_ref[x * 80 : x * 80 + 80] = total[0:80]
        t_ref[320 + x * 80 : 320 + x * 80 + 80] = total[80:160]
    out_ref[...] = t_ref[...].T.astype(BF)


def call(kernel, out, specs, out_specs=VMEM, scratch=(), limit=LIMIT):
    return pl.pallas_call(
        kernel,
        out_shape=out,
        in_specs=specs,
        out_specs=out_specs,
        scratch_shapes=list(scratch),
        compiler_params=pltpu.CompilerParams(vmem_limit_bytes=limit),
    )


def shape(*dims):
    return jax.ShapeDtypeStruct(dims, BF)


def from_plane(value, step):
    return lax.ppermute(value, "z", [((i + step) % NZ, i) for i in range(NZ)])


def per_device(query_input, key_input, value_input, query_gain, key_gain, band_lists, out_weight):
    plane = ("x", "y", "c")
    lists = band_lists.reshape(-1)
    zi = lax.axis_index("z").reshape(1)
    packed = call(
        pack_kernel,
        shape(32, CHUNK, HD),
        [ANY] * 5,
        VMEM,
        [
            pltpu.VMEM((QROWS, D), BF),
            pltpu.VMEM((HALF, D), BF),
            pltpu.VMEM((HALF, D), BF),
            pltpu.VMEM((1, D), F32),
            pltpu.VMEM((1, D), F32),
            pltpu.SemaphoreType.DMA((5,)),
        ],
        ALL,
    )(query_input, key_input, value_input, query_gain.reshape(1, -1), key_gain.reshape(1, -1))
    packed, columns = lax.optimization_barrier((packed, out_weight))
    columns = columns.reshape(GROUP, HD, 80).transpose(0, 2, 1).reshape(BLOCK, HD)
    held = [columns] + [from_plane(columns, step) for step in HELD[1:]]
    mine = lax.all_to_all(packed, plane, split_axis=0, concat_axis=0, tiled=True)
    up, down = call(
        select_kernel, (shape(SENT, HD), shape(SENT, HD)), [SMEM, SMEM] + [VMEM] * 4, (VMEM, VMEM)
    )(lists, zi, mine, *held)
    before, after = from_plane(up, -1), from_plane(down, 1)
    last = from_plane(columns, LAST)
    sums, stats = call(
        attend_own_kernel,
        (jax.ShapeDtypeStruct((256, 512), F32), jax.ShapeDtypeStruct((8, 512), F32)),
        [SMEM, SMEM, VMEM],
        (VMEM, VMEM),
        [pltpu.VMEM((1024, HD), BF), pltpu.VMEM((1024, HD), BF), pltpu.VMEM((256, HD), BF), pltpu.VMEM((256, HD), BF)],
    )(lists, zi, mine)
    attended, above_w, below_w = call(
        attend_rest_kernel,
        (shape(NX, 272, 512), shape(3 * BLOCK, HD), shape(3 * BLOCK, HD)),
        [SMEM, SMEM] + [VMEM] * 5 + [ANY],
        (VMEM, VMEM, VMEM),
    )(lists, zi, mine, before, after, sums, stats, last)
    below2, above2 = from_plane(below_w, -1), from_plane(above_w, 1)
    gathered = lax.all_to_all(attended, "x", split_axis=0, concat_axis=0, tiled=True)
    ci = lax.axis_index("c").reshape(1)
    keep, give = call(
        project_kernel,
        (shape(16, 160, 128), shape(16, 160, 128)),
        [SMEM, SMEM] + [VMEM] * 9,
        (VMEM, VMEM),
        [pltpu.VMEM((640, 512), BF), pltpu.VMEM((NZ * 80, 640), BF)],
    )(ci, zi, gathered, *held, last, below_w, above_w, below2, above2)
    other = lax.ppermute(give, "c", [(0, 1), (1, 0)])
    terms = (keep.astype(F32) + other.astype(F32)).astype(BF)
    summands = lax.all_to_all(terms, ("x", "y"), split_axis=0, concat_axis=0, tiled=True)
    return call(final_kernel, shape(128, 640), [VMEM], VMEM, [pltpu.VMEM((640, 128), F32)])(summands)


def solution(mesh):
    split = Mesh(mesh.devices.reshape(NZ, NX, 4, 2), ("z", "x", "y", "c"))
    rows = P(("z", "x", "y", "c"), None)
    return jax.shard_map(
        per_device,
        mesh=split,
        in_specs=(rows, rows, rows, P(), P(), P(), P(("y", "c"), ("z", "x"))),
        out_specs=P(("z", "x"), ("y", "c")),
        check_vma=False,
    )
```

time: 130 us -> 115 us (0.88)
  blocking collectives: 29.8 us -> 18.5 us
  waiting for transfers between devices: 33.7 us -> 25.8 us
  starting transfers between devices: 51.6 us -> 57.4 us
    all_to_all x1, blocking collectives: 29.8 us -> 18.5 us  [per_device(): lax.all_to_all(terms, ('x', 'y'), split_axis=0, concat_axis=0, tiled=True)]
    ppermute x2 -> x1, waiting for transfers between devices: 9.23 us -> 1.7 us  [per_device(): other = lax.ppermute(give, 'c', [(0, 1), (1, 0)])]
    ppermute x7, starting transfers between devices: 34.2 us -> 38.6 us  [from_plane(): return lax.ppermute(value, 'z', [((i + step) % NZ, i) for i in range(NZ)])]
    ppermute x7, waiting for transfers between devices: 24.4 us -> 21.9 us  [from_plane(): return lax.ppermute(value, 'z', [((i + step) % NZ, i) for i in range(NZ)])]
    all_to_all x1, waiting for transfers between devices: 0.01 us -> 2.22 us  [per_device(): lax.all_to_all(packed, plane, split_axis=0, concat_axis=0, tiled=True)]
    ppermute x2 -> x1, starting transfers between devices: 2.6 us -> 4.67 us  [per_device(): other = lax.ppermute(give, 'c', [(0, 1), (1, 0)])]
    pallas_call x3 -> x4, Pallas kernels: 8.34 us -> 7.85 us  [the longest x1 3.14 us: per_device(): call(attend_rest_kernel, (shape(NX, 272, 512), shape(3 * BLOCK, HD), shap...]
  transfers between devices with their start and end apart: 11 -> 10, of which waited for: 5 -> 7; matrix products, arithmetic and copies ran while one was open for 0% -> 0% of each run, Pallas kernels for 0% -> 2%
where the time goes in v3:
time: 115 us; the launch traced here: 114 us
  starting transfers between devices  57.4 us (50%)
  waiting for transfers between devices  25.8 us (22%)
  blocking collectives  18.5 us (16%)
  Pallas kernels  11.5 us (10%)
    ppermute x7, starting transfers between devices, from_plane(): return lax.ppermute(value, 'z', [((i + step) % NZ, i) for i in range(NZ)])  38.6 us
    ppermute x7, waiting for transfers between devices, from_plane(): return lax.ppermute(value, 'z', [((i + step) % NZ, i) for i in range(NZ)])  21.9 us
    all_to_all x1, blocking collectives, per_device(): lax.all_to_all(terms, ('x', 'y'), split_axis=0, concat_axis=0, tiled=True)  18.5 us
    all_to_all x1, starting transfers between devices, per_device(): lax.all_to_all(packed, plane, split_axis=0, concat_axis=0, tiled=True)  10.6 us
    ppermute x1, starting transfers between devices, per_device(): other = lax.ppermute(give, 'c', [(0, 1), (1, 0)])  4.67 us
    all_to_all x1, starting transfers between devices, per_device(): lax.all_to_all(attended, 'x', split_axis=0, concat_axis=0, tiled=True)  3.52 us
    pallas_call x1, Pallas kernels, per_device(): call(attend_rest_kernel, (shape(NX, 272, 512), shape(3 * BLOCK, HD), shap...  3.14 us
    pallas_call x1, Pallas kernels, per_device(): call(pack_kernel, shape(32, CHUNK, HD), [ANY] * 5, VMEM, [pltpu.VMEM((QRO...  2.83 us
  transfers between devices with their start and end apart: 10, of which 7 were waited for; matrix products, arithmetic and copies ran while one was open for 0% of the time, Pallas kernels for 2%

profile of v3, /device:TPU:1, one launch (start us, length us, event | category | flops | bytes accessed | tf_op | source)
XLA Modules:
  0.0 113.9 jit_solution(10973305889642493738)
XLA Ops:
  0.0 2.8 %shard_map.73 = bf16[32,192,128]{2,1,0:T(8,128)(2,1)} custom-call(bf16[16,5120]{1,0:T(8,128)(2,1)} %q_hbm.1, bf16[64,5120]{1,0:T(8,128)(2,1)} %k_hbm.1, bf16[64,5120]{1,0:T(8,128)(2,1)} %v_hbm.1, f32[1,5120]{1,0:T(1,128)} %bitcast.14, f32[1,5120]{1,0:T(1,128)} %bitcast.15), custom_call_target="tpu_custom_call" | custom-call | tf_op jit(solution)/shard_map/pallas_call | solution.py:256
  2.8 0.0 copy-start
  2.9 0.0 copy-start.1
  2.9 10.6 %all-to-all-start = ((bf16[32,192,128]{2,1,0:T(8,128)(2,1)}), bf16[32,192,128]{2,1,0:T(8,128)(2,1)S(1)}, u32[]{:S(2)}, u32[]{:S(2)}) async-start(bf16[32,192,128]{2,1,0:T(8,128)(2,1)} %shard_map.73), calls=%async_computation | async-start | bytes 3145728 | tf_op jit(solution)/shard_map/all_to_all | solution.py:274
  13.5 0.0 copy-done
  13.5 0.1 reshape.26
  13.7 9.6 %collective-permute-start.1 = (bf16[400,128]{1,0:T(8,128)(2,1)S(1)}, bf16[400,128]{1,0:T(8,128)(2,1)S(1)}, u32[]{:S(2)}, u32[]{:S(2)}) collective-permute-start(bf16[400,128]{1,0:T(8,128)(2,1)S(1)} %bitcast.8), channel_id=1, source_target_pairs={{320,0},{352,32},{384,64},{416,96},{448,128},{480,160},{0,192},{32... | collective-permute-start | bytes 307208 | tf_op jit(solution)/shard_map/ppermute | solution.py:249
  23.3 4.5 %collective-permute-start = (bf16[400,128]{1,0:T(8,128)(2,1)S(1)}, bf16[400,128]{1,0:T(8,128)(2,1)S(1)}, u32[]{:S(2)}, u32[]{:S(2)}) collective-permute-start(bf16[400,128]{1,0:T(8,128)(2,1)S(1)} %bitcast.9), channel_id=1, source_target_pairs={{160,0},{192,32},{224,64},{256,96},{288,128},{320,160},{352,192},{... | collective-permute-start | bytes 307208 | tf_op jit(solution)/shard_map/ppermute | solution.py:249
  27.8 0.0 copy-done.1
  27.8 0.1 copy.9
  27.9 0.1 reshape.23.lists
  28.0 1.6 %collective-permute-done.1.rest_2_.down6 = bf16[400,128]{1,0:T(8,128)(2,1)S(1)} collective-permute-done((bf16[400,128]{1,0:T(8,128)(2,1)S(1)}, bf16[400,128]{1,0:T(8,128)(2,1)S(1)}, u32[]{:S(2)}, u32[]{:S(2)}) %collective-permute-start.1) | collective-permute-done | bytes 102432 | tf_op jit(solution)/shard_map/ppermute | solution.py:249
  29.6 4.4 %collective-permute-done.rest_1_.up5 = bf16[400,128]{1,0:T(8,128)(2,1)S(1)} collective-permute-done((bf16[400,128]{1,0:T(8,128)(2,1)S(1)}, bf16[400,128]{1,0:T(8,128)(2,1)S(1)}, u32[]{:S(2)}, u32[]{:S(2)}) %collective-permute-start) | collective-permute-done | bytes 102432 | tf_op jit(solution)/shard_map/ppermute | solution.py:249
  34.1 2.2 %all-to-all-done.r_ref = bf16[32,192,128]{2,1,0:T(8,128)(2,1)S(1)} async-done(((bf16[32,192,128]{2,1,0:T(8,128)(2,1)}), bf16[32,192,128]{2,1,0:T(8,128)(2,1)S(1)}, u32[]{:S(2)}, u32[]{:S(2)}) %all-to-all-start) | async-done | bytes 1572896 | tf_op jit(solution)/shard_map/all_to_all | solution.py:274
  36.3 0.8 shard_map.74
  37.1 1.9 %collective-permute-start.2 = (bf16[2480,128]{1,0:T(8,128)(2,1)S(1)}, bf16[2480,128]{1,0:T(8,128)(2,1)S(1)}, u32[]{:S(2)}, u32[]{:S(2)}) collective-permute-start(bf16[2480,128]{1,0:T(8,128)(2,1)S(1)} %get-tuple-element.18), channel_id=1, source_target_pairs={{480,0},{0,32},{32,64},{64,96},{96,128},{128,160},{160,192},{192,2... | collective-permute-start | bytes 1904648 | tf_op jit(solution)/shard_map/ppermute | solution.py:249
  39.0 9.1 %collective-permute-start.3 = (bf16[2480,128]{1,0:T(8,128)(2,1)S(1)}, bf16[2480,128]{1,0:T(8,128)(2,1)S(1)}, u32[]{:S(2)}, u32[]{:S(2)}) collective-permute-start(bf16[2480,128]{1,0:T(8,128)(2,1)S(1)} %get-tuple-element.19), channel_id=1, source_target_pairs={{32,0},{64,32},{96,64},{128,96},{160,128},{192,160},{224,192},{256... | collective-permute-start | bytes 1904648 | tf_op jit(solution)/shard_map/ppermute | solution.py:249
  48.1 6.9 %collective-permute-start.4 = (bf16[400,128]{1,0:T(8,128)(2,1)S(1)}, bf16[400,128]{1,0:T(8,128)(2,1)S(1)}, u32[]{:S(2)}, u32[]{:S(2)}) collective-permute-start(bf16[400,128]{1,0:T(8,128)(2,1)S(1)} %bitcast.11), channel_id=1, source_target_pairs={{416,0},{448,32},{480,64},{0,96},{32,128},{64,160},{96,192},{128,2... | collective-permute-start | bytes 307208 | tf_op jit(solution)/shard_map/ppermute | solution.py:249
  55.0 2.3 %shard_map.75 = (f32[256,512]{1,0:T(8,128)S(1)}, f32[8,512]{1,0:T(8,128)S(1)}) custom-call(s32[512]{0:T(512)S(1)} %reshape.23.lists, s32[1]{0:T(128)} %bitcast.1.zi, bf16[32,192,128]{2,1,0:T(8,128)(2,1)S(1)} %all-to-all-done.r_ref), custom_call_target="tpu_custom_call" | custom-call | tf_op jit(solution)/shard_map/pallas_call | solution.py:280
  57.4 7.7 %collective-permute-done.4.last = bf16[400,128]{1,0:T(8,128)(2,1)S(1)} collective-permute-done((bf16[400,128]{1,0:T(8,128)(2,1)S(1)}, bf16[400,128]{1,0:T(8,128)(2,1)S(1)}, u32[]{:S(2)}, u32[]{:S(2)}) %collective-permute-start.4) | collective-permute-done | bytes 102432 | tf_op jit(solution)/shard_map/ppermute | solution.py:249
  65.1 0.0 collective-permute-done.2.prev_ref
  65.1 0.0 collective-permute-done.3.next_ref
  65.1 3.1 %shard_map.76 = (bf16[4,272,512]{2,1,0:T(8,128)(2,1)}, bf16[1200,128]{1,0:T(8,128)(2,1)S(1)}, bf16[1200,128]{1,0:T(8,128)(2,1)S(1)}) custom-call(s32[512]{0:T(512)S(1)} %reshape.23.lists, s32[1]{0:T(128)} %bitcast.1.zi, bf16[32,192,128]{2,1,0:T(8,128)(2,1)S(1)} %all-to-all-done.r_ref, bf16[2480,128]{1,0:T(8,128)(2,1)S(1)} %collective-permute-done.2.prev_ref, ...), custom_call_target="tpu_custom_call" | custom-call | tf_op jit(solution)/shard_map/pallas_call | solution.py:287
  68.2 3.5 %all-to-all-start.1 = ((bf16[4,272,512]{2,1,0:T(8,128)(2,1)}), bf16[4,272,512]{2,1,0:T(8,128)(2,1)S(1)}, u32[]{:S(2)}, u32[]{:S(2)}) async-start(bf16[4,272,512]{2,1,0:T(8,128)(2,1)} %get-tuple-element.22), calls=%async_computation.1 | async-start | bytes 2228224 | tf_op jit(solution)/shard_map/all_to_all | solution.py:294
  71.7 2.6 %collective-permute-start.5 = (bf16[1200,128]{1,0:T(8,128)(2,1)S(1)}, bf16[1200,128]{1,0:T(8,128)(2,1)S(1)}, u32[]{:S(2)}, u32[]{:S(2)}) collective-permute-start(bf16[1200,128]{1,0:T(8,128)(2,1)S(1)} %get-tuple-element.23.before), channel_id=1, source_target_pairs={{480,0},{0,32},{32,64},{64,96},{96,128},{128,160},{160,192},{192,2... | collective-permute-start | bytes 921608 | tf_op jit(solution)/shard_map/ppermute | solution.py:249
  74.3 3.9 %collective-permute-start.6 = (bf16[1200,128]{1,0:T(8,128)(2,1)S(1)}, bf16[1200,128]{1,0:T(8,128)(2,1)S(1)}, u32[]{:S(2)}, u32[]{:S(2)}) collective-permute-start(bf16[1200,128]{1,0:T(8,128)(2,1)S(1)} %get-tuple-element.24.after), channel_id=1, source_target_pairs={{32,0},{64,32},{96,64},{128,96},{160,128},{192,160},{224,192},{256... | collective-permute-start | bytes 921608 | tf_op jit(solution)/shard_map/ppermute | solution.py:249
  78.2 2.3 %collective-permute-done.5.before2 = bf16[1200,128]{1,0:T(8,128)(2,1)S(1)} collective-permute-done((bf16[1200,128]{1,0:T(8,128)(2,1)S(1)}, bf16[1200,128]{1,0:T(8,128)(2,1)S(1)}, u32[]{:S(2)}, u32[]{:S(2)}) %collective-permute-start.5) | collective-permute-done | bytes 307232 | tf_op jit(solution)/shard_map/ppermute | solution.py:249
  80.5 5.9 %collective-permute-done.6.after2 = bf16[1200,128]{1,0:T(8,128)(2,1)S(1)} collective-permute-done((bf16[1200,128]{1,0:T(8,128)(2,1)S(1)}, bf16[1200,128]{1,0:T(8,128)(2,1)S(1)}, u32[]{:S(2)}, u32[]{:S(2)}) %collective-permute-start.6) | collective-permute-done | bytes 307232 | tf_op jit(solution)/shard_map/ppermute | solution.py:249
  86.4 0.0 all-to-all-done.1.g_ref
  86.4 1.6 %shard_map.77 = (bf16[16,160,128]{2,1,0:T(8,128)(2,1)S(1)}, bf16[16,160,128]{2,1,0:T(8,128)(2,1)S(1)}) custom-call(s32[1]{0:T(128)} %bitcast.ci, s32[1]{0:T(128)} %bitcast.1.zi, bf16[4,272,512]{2,1,0:T(8,128)(2,1)S(1)} %all-to-all-done.1.g_ref, bf16[400,128]{1,0:T(8,128)(2,1)S(1)} %bitcast.12, bf16[400,128]{1,0:T(8,128)(2,1)S(1)} %collective-permute-done.rest_1_.up5, ...), custom_call_target="tpu_custom_call" | custom-call | tf_op jit(solution)/shard_map/pallas_call | solution.py:296
  88.0 4.7 %collective-permute-start.7 = (bf16[16,160,128]{2,1,0:T(8,128)(2,1)S(1)}, bf16[16,160,128]{2,1,0:T(8,128)(2,1)S(1)}, u32[]{:S(2)}, u32[]{:S(2)}) collective-permute-start(bf16[16,160,128]{2,1,0:T(8,128)(2,1)S(1)} %get-tuple-element.26), channel_id=1, source_target_pairs={{0,1},{1,0},{2,3},{3,2},{4,5},{5,4},{6,7},{7,6},{8,9},{9,8},{10,11... | collective-permute-start | bytes 1966088 | tf_op jit(solution)/shard_map/ppermute | solution.py:303
  92.7 1.7 %collective-permute-done.7 = bf16[16,160,128]{2,1,0:T(8,128)(2,1)S(1)} collective-permute-done((bf16[16,160,128]{2,1,0:T(8,128)(2,1)S(1)}, bf16[16,160,128]{2,1,0:T(8,128)(2,1)S(1)}, u32[]{:S(2)}, u32[]{:S(2)}) %collective-permute-start.7) | collective-permute-done | bytes 655392 | tf_op jit(solution)/shard_map/ppermute | solution.py:303
  94.4 0.2 add_convert_fusion
  94.6 18.5 %all_to_all.15.r_ref = bf16[16,160,128]{2,1,0:T(8,128)(2,1)S(1)} all-to-all(bf16[16,160,128]{2,1,0:T(8,128)(2,1)S(1)} %add_convert_fusion), channel_id=1, replica_groups=mesh['z'=16,'x'=4,'y'=4,'c'=2] {'x','y'}, dimensions={0} | all-to-all | bytes 1310720 | tf_op jit(solution)/shard_map/all_to_all | solution.py:305
  113.1 0.8 shard_map.78
  (1 shorter events, 0.0 us)
Async XLA Ops:
  2.8 10.7 %copy-start = (bf16[640,80]{0,1:T(8,128)(2,1)S(1)}, bf16[640,80]{0,1:T(8,128)(2,1)}, u32[]{:S(2)}) copy-start(bf16[640,80]{0,1:T(8,128)(2,1)} %param.13) | copy-start | bytes 307204
  2.9 25.0 %copy-start.1 = (s32[64,8]{0,1:T(8,128)S(1)}, s32[64,8]{0,1:T(8,128)}, u32[]{:S(2)}) copy-start(s32[64,8]{0,1:T(8,128)} %param.12) | copy-start | bytes 6148
  2.9 33.4 %all-to-all-start = ((bf16[32,192,128]{2,1,0:T(8,128)(2,1)}), bf16[32,192,128]{2,1,0:T(8,128)(2,1)S(1)}, u32[]{:S(2)}, u32[]{:S(2)}) async-start(bf16[32,192,128]{2,1,0:T(8,128)(2,1)} %shard_map.73), calls=%async_computation | async-start | bytes 3145728 | tf_op jit(solution)/shard_map/all_to_all | solution.py:274
  13.7 15.9 %collective-permute-start.1 = (bf16[400,128]{1,0:T(8,128)(2,1)S(1)}, bf16[400,128]{1,0:T(8,128)(2,1)S(1)}, u32[]{:S(2)}, u32[]{:S(2)}) collective-permute-start(bf16[400,128]{1,0:T(8,128)(2,1)S(1)} %bitcast.8), channel_id=1, source_target_pairs={{320,0},{352,32},{384,64},{416,96},{448,128},{480,160},{0,192},{32... | collective-permute-start | bytes 307208 | tf_op jit(solution)/shard_map/ppermute | solution.py:249
  23.3 10.8 %collective-permute-start = (bf16[400,128]{1,0:T(8,128)(2,1)S(1)}, bf16[400,128]{1,0:T(8,128)(2,1)S(1)}, u32[]{:S(2)}, u32[]{:S(2)}) collective-permute-start(bf16[400,128]{1,0:T(8,128)(2,1)S(1)} %bitcast.9), channel_id=1, source_target_pairs={{160,0},{192,32},{224,64},{256,96},{288,128},{320,160},{352,192},{... | collective-permute-start | bytes 307208 | tf_op jit(solution)/shard_map/ppermute | solution.py:249
  37.1 28.0 %collective-permute-start.2 = (bf16[2480,128]{1,0:T(8,128)(2,1)S(1)}, bf16[2480,128]{1,0:T(8,128)(2,1)S(1)}, u32[]{:S(2)}, u32[]{:S(2)}) collective-permute-start(bf16[2480,128]{1,0:T(8,128)(2,1)S(1)} %get-tuple-element.18), channel_id=1, source_target_pairs={{480,0},{0,32},{32,64},{64,96},{96,128},{128,160},{160,192},{192,2... | collective-permute-start | bytes 1904648 | tf_op jit(solution)/shard_map/ppermute | solution.py:249
  39.0 26.1 %collective-permute-start.3 = (bf16[2480,128]{1,0:T(8,128)(2,1)S(1)}, bf16[2480,128]{1,0:T(8,128)(2,1)S(1)}, u32[]{:S(2)}, u32[]{:S(2)}) collective-permute-start(bf16[2480,128]{1,0:T(8,128)(2,1)S(1)} %get-tuple-element.19), channel_id=1, source_target_pairs={{32,0},{64,32},{96,64},{128,96},{160,128},{192,160},{224,192},{256... | collective-permute-start | bytes 1904648 | tf_op jit(solution)/shard_map/ppermute | solution.py:249
  48.1 16.9 %collective-permute-start.4 = (bf16[400,128]{1,0:T(8,128)(2,1)S(1)}, bf16[400,128]{1,0:T(8,128)(2,1)S(1)}, u32[]{:S(2)}, u32[]{:S(2)}) collective-permute-start(bf16[400,128]{1,0:T(8,128)(2,1)S(1)} %bitcast.11), channel_id=1, source_target_pairs={{416,0},{448,32},{480,64},{0,96},{32,128},{64,160},{96,192},{128,2... | collective-permute-start | bytes 307208 | tf_op jit(solution)/shard_map/ppermute | solution.py:249
  68.2 18.2 %all-to-all-start.1 = ((bf16[4,272,512]{2,1,0:T(8,128)(2,1)}), bf16[4,272,512]{2,1,0:T(8,128)(2,1)S(1)}, u32[]{:S(2)}, u32[]{:S(2)}) async-start(bf16[4,272,512]{2,1,0:T(8,128)(2,1)} %get-tuple-element.22), calls=%async_computation.1 | async-start | bytes 2228224 | tf_op jit(solution)/shard_map/all_to_all | solution.py:294
  71.7 8.8 %collective-permute-start.5 = (bf16[1200,128]{1,0:T(8,128)(2,1)S(1)}, bf16[1200,128]{1,0:T(8,128)(2,1)S(1)}, u32[]{:S(2)}, u32[]{:S(2)}) collective-permute-start(bf16[1200,128]{1,0:T(8,128)(2,1)S(1)} %get-tuple-element.23.before), channel_id=1, source_target_pairs={{480,0},{0,32},{32,64},{64,96},{96,128},{128,160},{160,192},{192,2... | collective-permute-start | bytes 921608 | tf_op jit(solution)/shard_map/ppermute | solution.py:249
  74.3 12.1 %collective-permute-start.6 = (bf16[1200,128]{1,0:T(8,128)(2,1)S(1)}, bf16[1200,128]{1,0:T(8,128)(2,1)S(1)}, u32[]{:S(2)}, u32[]{:S(2)}) collective-permute-start(bf16[1200,128]{1,0:T(8,128)(2,1)S(1)} %get-tuple-element.24.after), channel_id=1, source_target_pairs={{32,0},{64,32},{96,64},{128,96},{160,128},{192,160},{224,192},{256... | collective-permute-start | bytes 921608 | tf_op jit(solution)/shard_map/ppermute | solution.py:249
  88.0 6.4 %collective-permute-start.7 = (bf16[16,160,128]{2,1,0:T(8,128)(2,1)S(1)}, bf16[16,160,128]{2,1,0:T(8,128)(2,1)S(1)}, u32[]{:S(2)}, u32[]{:S(2)}) collective-permute-start(bf16[16,160,128]{2,1,0:T(8,128)(2,1)S(1)} %get-tuple-element.26), channel_id=1, source_target_pairs={{0,1},{1,0},{2,3},{3,2},{4,5},{5,4},{6,7},{7,6},{8,9},{9,8},{10,11... | collective-permute-start | bytes 1966088 | tf_op jit(solution)/shard_map/ppermute | solution.py:303

commit v4 on v3

--- a/solution.py
+++ b/solution.py
@@ -26,8 +26,7 @@
 HELD = (0, 5, -6)
 LAST = -3
 BLOCK = 400
-SK, SV, SK5, SV5, SW = 0, 512, 1024, 1152, 1280
-SENT = SW + 3 * BLOCK
+SK, SV, SK5, SV5, SENT = 0, 512, 1024, 1152, 1280
 
 
 def dot(a, b, contract):
@@ -102,7 +101,9 @@
 
 
 def select_kernel(lists, zi, r_ref, *rest):
-    held, (up_ref, down_ref) = rest[:3], rest[3:]
+    held, (up_ref, down_ref, joined_ref) = rest[:3], rest[4:]
+    for i, ref in enumerate(held):
+        joined_ref[i * BLOCK : i * BLOCK + BLOCK] = ref[...]
     z = zi[0]
     for blocks, target in ((listed_above(lists, z), up_ref), (listed_below(lists, z), down_ref)):
         for slot, block in enumerate(blocks):
@@ -113,8 +114,6 @@
                 target[SV + part * 64 : SV + part * 64 + 64] = source[V0 : V0 + 64]
                 target[SK5 + part * 16 : SK5 + part * 16 + 16] = source[K5 : K5 + 16]
                 target[SV5 + part * 16 : SV5 + part * 16 + 16] = source[V5 : V5 + 16]
-        for i, ref in enumerate(held):
-            target[SW + i * BLOCK : SW + i * BLOCK + BLOCK] = ref[...]
 
 
 def queries(r_ref, x, first):
@@ -153,71 +152,88 @@
             sum_ref[i * 128 : i * 128 + 128, cols] = dot(values[...], exponent.astype(BF), (0, 0))
 
 
-def attend_rest_kernel(lists, zi, r_ref, prev_ref, next_ref, sum_ref, stat_ref, last, out_ref, above_ref, below_ref):
-    del last
+def attend_rest_kernel(lists, zi, r_ref, prev_ref, next_ref, sum_ref, stat_ref, out_ref):
     z = zi[0]
-    below_ref[...] = prev_ref[SW:]
-    above_ref[...] = next_ref[SW:]
     near = listed_above(lists, z - 1), listed_below(lists, z + 1)
+    parts = []
     for x in range(NX):
         ref, side = ((prev_ref, 0), (next_ref, 1))[x // 2]
         first, count = (0, 3) if x in (0, 3) else (3, 1)
         found = near[side][first : first + count]
         inside = (z > 0) if side == 0 else (z < NZ - 1)
         biases = [jnp.where((block >= 0) & inside, 0.0, -jnp.inf) for block in found]
-        cols = slice(x * 128, x * 128 + 128)
         for i, (key_row, value_row, size, query_row) in enumerate(((SK, SV, 128, Q0), (SK5, SV5, 32, Q5))):
             keys = ref[key_row + first * size : key_row + (first + count) * size]
             values = ref[value_row + first * size : value_row + (first + count) * size]
-            scores = scored(keys, queries(r_ref, x, query_row), biases)
-            old = stat_ref[i * 2 : i * 2 + 1, cols]
-            top = jnp.maximum(old, jnp.max(scores, axis=0, keepdims=True))
-            exponent = jnp.exp(scores - top)
-            share = jnp.exp(old - top)
-            total = stat_ref[i * 2 + 1 : i * 2 + 2, cols] * share + jnp.sum(exponent, axis=0, keepdims=True)
-            added = sum_ref[i * 128 : i * 128 + 128, cols] * share + dot(values, exponent.astype(BF), (0, 0))
-            result = (added / total).astype(BF)
-            for target in range(NX):
-                out_ref[target, i * 128 : i * 128 + 128, cols] = result
-        level = top + jnp.log(total)
-        high = level.astype(BF)
-        left = level - high.astype(F32)
-        middle = left.astype(BF)
-        low = (left - middle.astype(F32)).astype(BF)
-        zeros = jnp.zeros((13, 128), F32)
-        pieces = jnp.concatenate([high.astype(F32), middle.astype(F32), low.astype(F32), zeros], axis=0).astype(BF)
-        for target in range(NX):
-            out_ref[target, 256:272, cols] = pieces
-
-
-def project_kernel(ci, zi, g_ref, own, up5, down6, last, before, after, before2, after2, keep_ref, give_ref, a_ref, w_ref):
-    blocks = [(last, 0, LAST)] + [(ref, 0, step) for ref, step in zip((own, up5, down6), HELD)]
+            parts.append((i, slice(x * 128, x * 128 + 128), values, scored(keys, queries(r_ref, x, query_row), biases)))
+    done = []
+    for i, cols, values, scores in parts:
+        old = stat_ref[i * 2 : i * 2 + 1, cols]
+        top = jnp.maximum(old, jnp.max(scores, axis=0, keepdims=True))
+        exponent = jnp.exp(scores - top)
+        share = jnp.exp(old - top)
+        total = stat_ref[i * 2 + 1 : i * 2 + 2, cols] * share + jnp.sum(exponent, axis=0, keepdims=True)
+        added = sum_ref[i * 128 : i * 128 + 128, cols] * share + dot(values, exponent.astype(BF), (0, 0))
+        done.append((i, cols, (added / total).astype(BF), top, total))
+    for i, cols, result, top, total in done:
+        out_ref[i * 128 : i * 128 + 128, cols] = result
+        if i:
+            level = top + jnp.log(total)
+            high = level.astype(BF)
+            left = level - high.astype(F32)
+            middle = left.astype(BF)
+            low = (left - middle.astype(F32)).astype(BF)
+            zeros = jnp.zeros((13, 128), F32)
+            pieces = [high.astype(F32), middle.astype(F32), low.astype(F32), zeros]
+            out_ref[256:272, cols] = jnp.concatenate(pieces, axis=0).astype(BF)
+
+
+def project_kernel(ci, zi, xi, g0, g1, g2, g3, own, up5, down6, last, before, after, before2, after2, give_ref, a_ref, keep_w_ref, give_w_ref):
+    blocks = [(last, 0, 0, LAST)] + [(ref, 0, 0, step) for ref, step in zip((own, up5, down6), HELD)]
     for ref, step in ((before, -1), (after, 1), (before2, -2), (after2, 2)):
-        blocks += [(ref, i * BLOCK, step + offset) for i, offset in enumerate(HELD)]
-    for ref, first, step in blocks:
-        rows = pl.ds(pl.multiple_of(((zi[0] + step) & (NZ - 1)) * 80, 80), 80)
-        for head in range(GROUP):
-            w_ref[rows, head * HD : head * HD + HD] = ref[first + head * 80 : first + head * 80 + 80]
+        blocks += [(ref, i * BLOCK, step, offset) for i, offset in enumerate(HELD)]
+    for ref, first, step, offset in blocks:
+        plane = (zi[0] + step + jnp.where(ci[0] == 0, offset, -offset)) & (NZ - 1)
+        rows = pl.ds(pl.multiple_of((plane >> 2) * 160 + (plane & 1) * 80, 80), 80)
+
+        def place(target):
+            for head in range(GROUP):
+                target[rows, head * HD : head * HD + HD] = ref[first + head * 80 : first + head * 80 + 80]
+
+        pl.when(((plane >> 1) & 1) == ci[0])(lambda: place(keep_w_ref))
+        pl.when(((plane >> 1) & 1) != ci[0])(lambda: place(give_w_ref))
+    refs = (g0, g1, g2, g3)
     levels = []
     for x in range(NX):
-        parts = g_ref[x, 256:272].astype(F32)
+        parts = refs[x][256:272].astype(F32)
         levels.append(parts[0:1] + parts[1:2] + parts[2:3])
     top = jnp.maximum(jnp.maximum(levels[0], levels[1]), jnp.maximum(levels[2], levels[3]))
     shares = [jnp.exp(level - top) for level in levels]
     total = shares[0] + shares[1] + shares[2] + shares[3]
     shared = jnp.zeros((128, 512), F32)
     for x in range(NX):
-        a_ref[x * 128 : x * 128 + 128] = g_ref[x, 0:128]
-        shared = shared + g_ref[x, 128:256].astype(F32) * (shares[x] / total)
+        head = (xi[0] + x) & (NX - 1)
+        a_ref[pl.ds(pl.multiple_of(head * 128, 128), 128)] = refs[x][0:128]
+        shared = shared + refs[x][128:256].astype(F32) * (shares[x] / total)
     a_ref[512:640] = shared.astype(BF)
-    a = a_ref[...]
-    for other, target in ((1, give_ref), (0, keep_ref)):
-        parity = ci[0] ^ other
-        for y in range(4):
-            rows = pl.ds(pl.multiple_of((2 * y + parity) * 160, 160), 160)
-            part = dot(w_ref[rows], a, (1, 0)).astype(BF)
-            for x in range(NX):
-                target[x * 4 + y] = part[:, x * 128 : x * 128 + 128]
+    multiply(give_w_ref, a_ref, give_ref)
+
+
+def hand_on_kernel(below_w, above_w, attended, below_ref, above_ref):
+    del attended
+    below_ref[...] = below_w[...]
+    above_ref[...] = above_w[...]
+
+
+def multiply(w_ref, a_ref, out_ref):
+    for y in range(4):
+        part = dot(w_ref[y * 160 : y * 160 + 160], a_ref[...], (1, 0)).astype(BF)
+        for x in range(NX):
+            out_ref[x * 4 + y] = part[:, x * 128 : x * 128 + 128]
+
+
+def keep_kernel(a_ref, w_ref, out_ref):
+    multiply(w_ref, a_ref, out_ref)
 
 
 def final_kernel(r_ref, out_ref, t_ref):
@@ -249,10 +265,16 @@
     return lax.ppermute(value, "z", [((i + step) % NZ, i) for i in range(NZ)])
 
 
+def from_either(value, step):
+    pairs = [((z + (step, -step)[core]) % NZ * 2 + core, z * 2 + core) for z in range(NZ) for core in range(2)]
+    return lax.ppermute(value, ("z", "c"), pairs)
+
+
 def per_device(query_input, key_input, value_input, query_gain, key_gain, band_lists, out_weight):
     plane = ("x", "y", "c")
     lists = band_lists.reshape(-1)
     zi = lax.axis_index("z").reshape(1)
+    xi = lax.axis_index("x").reshape(1)
     packed = call(
         pack_kernel,
         shape(32, CHUNK, HD),
@@ -270,13 +292,13 @@
     )(query_input, key_input, value_input, query_gain.reshape(1, -1), key_gain.reshape(1, -1))
     packed, columns = lax.optimization_barrier((packed, out_weight))
     columns = columns.reshape(GROUP, HD, 80).transpose(0, 2, 1).reshape(BLOCK, HD)
-    held = [columns] + [from_plane(columns, step) for step in HELD[1:]]
+    held = [columns] + [from_either(columns, step) for step in HELD[1:]]
+    last = from_either(columns, LAST)
     mine = lax.all_to_all(packed, plane, split_axis=0, concat_axis=0, tiled=True)
-    up, down = call(
-        select_kernel, (shape(SENT, HD), shape(SENT, HD)), [SMEM, SMEM] + [VMEM] * 4, (VMEM, VMEM)
-    )(lists, zi, mine, *held)
+    up, down, joined = call(
+        select_kernel, (shape(SENT, HD), shape(SENT, HD), shape(3 * BLOCK, HD)), [SMEM, SMEM] + [VMEM] * 4 + [ANY], (VMEM,) * 3
+    )(lists, zi, mine, *held, last)
     before, after = from_plane(up, -1), from_plane(down, 1)
-    last = from_plane(columns, LAST)
     sums, stats = call(
         attend_own_kernel,
         (jax.ShapeDtypeStruct((256, 512), F32), jax.ShapeDtypeStruct((8, 512), F32)),
@@ -284,23 +306,27 @@
         (VMEM, VMEM),
         [pltpu.VMEM((1024, HD), BF), pltpu.VMEM((1024, HD), BF), pltpu.VMEM((256, HD), BF), pltpu.VMEM((256, HD), BF)],
     )(lists, zi, mine)
-    attended, above_w, below_w = call(
-        attend_rest_kernel,
-        (shape(NX, 272, 512), shape(3 * BLOCK, HD), shape(3 * BLOCK, HD)),
-        [SMEM, SMEM] + [VMEM] * 5 + [ANY],
+    attended = call(attend_rest_kernel, shape(304, 512), [SMEM, SMEM] + [VMEM] * 5)(
+        lists, zi, mine, before, after, sums, stats
+    )
+    above_w, below_w = from_plane(joined, 1), from_plane(joined, -1)
+    below_again, above_again = call(
+        hand_on_kernel, (shape(3 * BLOCK, HD),) * 2, [VMEM, VMEM, ANY], (VMEM, VMEM)
+    )(below_w, above_w, attended)
+    below2, above2 = from_plane(below_again, -1), from_plane(above_again, 1)
+    gathered = [attended] + [
+        lax.ppermute(attended, "x", [((i + step) % NX, i) for i in range(NX)]) for step in (1, 2, 3)
+    ]
+    ci = lax.axis_index("c").reshape(1)
+    give, a, keep_w = call(
+        project_kernel,
+        (shape(16, 160, 128), shape(640, 512), shape(640, 640)),
+        [SMEM, SMEM, SMEM] + [VMEM] * 12,
         (VMEM, VMEM, VMEM),
-    )(lists, zi, mine, before, after, sums, stats, last)
-    below2, above2 = from_plane(below_w, -1), from_plane(above_w, 1)
-    gathered = lax.all_to_all(attended, "x", split_axis=0, concat_axis=0, tiled=True)
-    ci = lax.axis_index("c").reshape(1)
-    keep, give = call(
-        project_kernel,
-        (shape(16, 160, 128), shape(16, 160, 128)),
-        [SMEM, SMEM] + [VMEM] * 9,
-        (VMEM, VMEM),
-        [pltpu.VMEM((640, 512), BF), pltpu.VMEM((NZ * 80, 640), BF)],
-    )(ci, zi, gathered, *held, last, below_w, above_w, below2, above2)
+        [pltpu.VMEM((640, 640), BF)],
+    )(ci, zi, xi, *gathered, *held, last, below_w, above_w, below2, above2)
     other = lax.ppermute(give, "c", [(0, 1), (1, 0)])
+    keep = call(keep_kernel, shape(16, 160, 128), [VMEM, VMEM])(a, keep_w)
     terms = (keep.astype(F32) + other.astype(F32)).astype(BF)
     summands = lax.all_to_all(terms, ("x", "y"), split_axis=0, concat_axis=0, tiled=True)
     return call(final_kernel, shape(128, 640), [VMEM], VMEM, [pltpu.VMEM((640, 128), F32)])(summands)

time: 115 us -> 110 us (0.957)
  waiting for transfers between devices: 25.8 us -> 14.3 us
  starting transfers between devices: 57.4 us -> 68.3 us
  blocking collectives: 18.5 us -> 15.9 us
  Pallas kernels: 11.5 us -> 9.97 us
    ppermute x0 -> x6, starting transfers between devices: none -> 31.4 us  [the longest x3 20.6 us: from_either(): return lax.ppermute(value, ('z', 'c'), pairs)]
    ppermute x7 -> x6, starting transfers between devices: 38.6 us -> 18.3 us  [from_plane(): return lax.ppermute(value, 'z', [((i + step) % NZ, i) for i in range(NZ)])]
    ppermute x7 -> x6, waiting for transfers between devices: 21.9 us -> 3.98 us  [from_plane(): return lax.ppermute(value, 'z', [((i + step) % NZ, i) for i in range(NZ)])]
    ppermute x0 -> x6, waiting for transfers between devices: none -> 9.35 us  [the longest x3 9.34 us: from_either(): return lax.ppermute(value, ('z', 'c'), pairs)]
    all_to_all x1 -> x0, starting transfers between devices: 3.52 us -> none  [per_device(): lax.all_to_all(attended, 'x', split_axis=0, concat_axis=0, tiled=True)]
    ppermute x1, starting transfers between devices: 4.67 us -> 8.08 us  [per_device(): other = lax.ppermute(give, 'c', [(0, 1), (1, 0)])]
    all_to_all x1, blocking collectives: 18.5 us -> 15.9 us  [per_device(): lax.all_to_all(terms, ('x', 'y'), split_axis=0, concat_axis=0, tiled=True)]
    all_to_all x1, waiting for transfers between devices: 2.22 us -> 0.01 us  [per_device(): lax.all_to_all(packed, plane, split_axis=0, concat_axis=0, tiled=True)]
  transfers between devices with their start and end apart: 10 -> 14, of which waited for: 7 -> 6; matrix products, arithmetic and copies ran while one was open for 0% -> 0% of each run, Pallas kernels for 2% -> 4%
where the time goes in v4:
time: 110 us; the launch traced here: 109 us
  starting transfers between devices  68.3 us (62%)
  blocking collectives  15.9 us (14%)
  waiting for transfers between devices  14.3 us (13%)
  Pallas kernels  9.97 us (9%)
    ppermute x3, starting transfers between devices, from_either(): return lax.ppermute(value, ('z', 'c'), pairs)  20.6 us
    ppermute x6, starting transfers between devices, from_plane(): return lax.ppermute(value, 'z', [((i + step) % NZ, i) for i in range(NZ)])  18.3 us
    all_to_all x1, blocking collectives, per_device(): lax.all_to_all(terms, ('x', 'y'), split_axis=0, concat_axis=0, tiled=True)  15.9 us
    ppermute x3, starting transfers between devices, per_device(): lax.ppermute(attended, 'x', [((i + step) % NX, i) for i in range(NX)])  10.7 us
    all_to_all x1, starting transfers between devices, per_device(): lax.all_to_all(packed, plane, split_axis=0, concat_axis=0, tiled=True)  10.6 us
    ppermute x3, waiting for transfers between devices, from_either(): return lax.ppermute(value, ('z', 'c'), pairs)  9.34 us
    ppermute x1, starting transfers between devices, per_device(): other = lax.ppermute(give, 'c', [(0, 1), (1, 0)])  8.08 us
    ppermute x6, waiting for transfers between devices, from_plane(): return lax.ppermute(value, 'z', [((i + step) % NZ, i) for i in range(NZ)])  3.98 us
  transfers between devices with their start and end apart: 14, of which 6 were waited for; matrix products, arithmetic and copies ran while one was open for 0% of the time, Pallas kernels for 4%

profile of v4, /device:TPU:1, one launch (start us, length us, event | category | flops | bytes accessed | tf_op | source)
XLA Modules:
  0.0 109.3 jit_solution(2648301849144142559)
XLA Ops:
  0.0 2.8 %shard_map.73 = bf16[32,192,128]{2,1,0:T(8,128)(2,1)} custom-call(bf16[16,5120]{1,0:T(8,128)(2,1)} %q_hbm.1, bf16[64,5120]{1,0:T(8,128)(2,1)} %k_hbm.1, bf16[64,5120]{1,0:T(8,128)(2,1)} %v_hbm.1, f32[1,5120]{1,0:T(1,128)} %bitcast.15, f32[1,5120]{1,0:T(1,128)} %bitcast.16), custom_call_target="tpu_custom_call" | custom-call | tf_op jit(solution)/shard_map/pallas_call | solution.py:278
  2.8 0.0 copy-start
  2.9 0.0 copy-start.1
  2.9 10.6 %all-to-all-start = ((bf16[32,192,128]{2,1,0:T(8,128)(2,1)}), bf16[32,192,128]{2,1,0:T(8,128)(2,1)S(1)}, u32[]{:S(2)}, u32[]{:S(2)}) async-start(bf16[32,192,128]{2,1,0:T(8,128)(2,1)} %shard_map.73), calls=%async_computation | async-start | bytes 3145728 | tf_op jit(solution)/shard_map/all_to_all | solution.py:297
  13.5 0.0 copy-done
  13.5 0.1 reshape.30
  13.7 10.1 %collective-permute-start.2 = (bf16[400,128]{1,0:T(8,128)(2,1)S(1)}, bf16[400,128]{1,0:T(8,128)(2,1)S(1)}, u32[]{:S(2)}, u32[]{:S(2)}) collective-permute-start(bf16[400,128]{1,0:T(8,128)(2,1)S(1)} %bitcast.9), channel_id=1, source_target_pairs={{416,0},{97,1},{448,32},{129,33},{480,64},{161,65},{0,96},{193,97}... | collective-permute-start | bytes 307208 | tf_op jit(solution)/shard_map/ppermute | solution.py:270
  23.8 5.2 %collective-permute-start.1 = (bf16[400,128]{1,0:T(8,128)(2,1)S(1)}, bf16[400,128]{1,0:T(8,128)(2,1)S(1)}, u32[]{:S(2)}, u32[]{:S(2)}) collective-permute-start(bf16[400,128]{1,0:T(8,128)(2,1)S(1)} %bitcast.10), channel_id=1, source_target_pairs={{320,0},{193,1},{352,32},{225,33},{384,64},{257,65},{416,96},{289,... | collective-permute-start | bytes 307208 | tf_op jit(solution)/shard_map/ppermute | solution.py:270
  29.0 5.4 %collective-permute-start = (bf16[400,128]{1,0:T(8,128)(2,1)S(1)}, bf16[400,128]{1,0:T(8,128)(2,1)S(1)}, u32[]{:S(2)}, u32[]{:S(2)}) collective-permute-start(bf16[400,128]{1,0:T(8,128)(2,1)S(1)} %bitcast.11), channel_id=1, source_target_pairs={{160,0},{353,1},{192,32},{385,33},{224,64},{417,65},{256,96},{449,... | collective-permute-start | bytes 307208 | tf_op jit(solution)/shard_map/ppermute | solution.py:270
  34.4 0.0 copy-done.1
  34.4 0.1 copy.9
  34.5 0.1 reshape.27.lists
  34.5 0.0 collective-permute-done.2.rest_3_.last
  34.6 4.0 %collective-permute-done.1.rest_2_.down6 = bf16[400,128]{1,0:T(8,128)(2,1)S(1)} collective-permute-done((bf16[400,128]{1,0:T(8,128)(2,1)S(1)}, bf16[400,128]{1,0:T(8,128)(2,1)S(1)}, u32[]{:S(2)}, u32[]{:S(2)}) %collective-permute-start.1) | collective-permute-done | bytes 102432 | tf_op jit(solution)/shard_map/ppermute | solution.py:270
  38.6 5.3 %collective-permute-done.rest_1_.up5 = bf16[400,128]{1,0:T(8,128)(2,1)S(1)} collective-permute-done((bf16[400,128]{1,0:T(8,128)(2,1)S(1)}, bf16[400,128]{1,0:T(8,128)(2,1)S(1)}, u32[]{:S(2)}, u32[]{:S(2)}) %collective-permute-start) | collective-permute-done | bytes 102432 | tf_op jit(solution)/shard_map/ppermute | solution.py:270
  43.9 0.0 all-to-all-done.r_ref
  43.9 0.8 shard_map.74
  44.7 3.7 %collective-permute-start.3 = (bf16[1280,128]{1,0:T(8,128)(2,1)S(1)}, bf16[1280,128]{1,0:T(8,128)(2,1)S(1)}, u32[]{:S(2)}, u32[]{:S(2)}) collective-permute-start(bf16[1280,128]{1,0:T(8,128)(2,1)S(1)} %get-tuple-element.19), channel_id=1, source_target_pairs={{480,0},{0,32},{32,64},{64,96},{96,128},{128,160},{160,192},{192,2... | collective-permute-start | bytes 983048 | tf_op jit(solution)/shard_map/ppermute | solution.py:265
  48.3 2.8 %collective-permute-start.4 = (bf16[1280,128]{1,0:T(8,128)(2,1)S(1)}, bf16[1280,128]{1,0:T(8,128)(2,1)S(1)}, u32[]{:S(2)}, u32[]{:S(2)}) collective-permute-start(bf16[1280,128]{1,0:T(8,128)(2,1)S(1)} %get-tuple-element.20), channel_id=1, source_target_pairs={{32,0},{64,32},{96,64},{128,96},{160,128},{192,160},{224,192},{256... | collective-permute-start | bytes 983048 | tf_op jit(solution)/shard_map/ppermute | solution.py:265
  51.2 1.9 %collective-permute-start.9 = (bf16[1200,128]{1,0:T(8,128)(2,1)S(1)}, bf16[1200,128]{1,0:T(8,128)(2,1)S(1)}, u32[]{:S(2)}, u32[]{:S(2)}) collective-permute-start(bf16[1200,128]{1,0:T(8,128)(2,1)S(1)} %get-tuple-element.23), channel_id=1, source_target_pairs={{32,0},{64,32},{96,64},{128,96},{160,128},{192,160},{224,192},{256... | collective-permute-start | bytes 921608 | tf_op jit(solution)/shard_map/ppermute | solution.py:265
  53.1 3.4 %collective-permute-start.8 = (bf16[1200,128]{1,0:T(8,128)(2,1)S(1)}, bf16[1200,128]{1,0:T(8,128)(2,1)S(1)}, u32[]{:S(2)}, u32[]{:S(2)}) collective-permute-start(bf16[1200,128]{1,0:T(8,128)(2,1)S(1)} %get-tuple-element.23), channel_id=1, source_target_pairs={{480,0},{0,32},{32,64},{64,96},{96,128},{128,160},{160,192},{192,2... | collective-permute-start | bytes 921608 | tf_op jit(solution)/shard_map/ppermute | solution.py:265
  56.5 2.3 %shard_map.75 = (f32[256,512]{1,0:T(8,128)S(1)}, f32[8,512]{1,0:T(8,128)S(1)}) custom-call(s32[512]{0:T(512)S(1)} %reshape.27.lists, s32[1]{0:T(128)} %bitcast.1.zi, bf16[32,192,128]{2,1,0:T(8,128)(2,1)S(1)} %all-to-all-done.r_ref), custom_call_target="tpu_custom_call" | custom-call | tf_op jit(solution)/shard_map/pallas_call | solution.py:302
  58.8 0.0 collective-permute-done.3.prev_ref
  58.8 0.2 collective-permute-done.4.next_ref
  59.0 1.2 %shard_map.76.attended.g0 = bf16[304,512]{1,0:T(8,128)(2,1)S(1)} custom-call(s32[512]{0:T(512)S(1)} %reshape.27.lists, s32[1]{0:T(128)} %bitcast.1.zi, bf16[32,192,128]{2,1,0:T(8,128)(2,1)S(1)} %all-to-all-done.r_ref, bf16[1280,128]{1,0:T(8,128)(2,1)S(1)} %collective-permute-done.3.prev_ref, bf16[1280,128]{1,0:T(8,128)(2,1)S(1)} %collective-permute-done.4.next_ref, ...), custom_call_target="tpu_custom_call" | custom-call | tf_op jit(solution)/shard_map/pallas_call | solution.py:309
  60.1 3.3 %collective-permute-start.7 = (bf16[304,512]{1,0:T(8,128)(2,1)S(1)}, bf16[304,512]{1,0:T(8,128)(2,1)S(1)}, u32[]{:S(2)}, u32[]{:S(2)}) collective-permute-start(bf16[304,512]{1,0:T(8,128)(2,1)S(1)} %shard_map.76.attended.g0), channel_id=1, source_target_pairs={{24,0},{0,8},{8,16},{16,24},{25,1},{1,9},{9,17},{17,25},{26,2},{2,... | collective-permute-start | bytes 933896 | tf_op jit(solution)/shard_map/ppermute | solution.py:318
  63.5 4.3 %collective-permute-start.6 = (bf16[304,512]{1,0:T(8,128)(2,1)S(1)}, bf16[304,512]{1,0:T(8,128)(2,1)S(1)}, u32[]{:S(2)}, u32[]{:S(2)}) collective-permute-start(bf16[304,512]{1,0:T(8,128)(2,1)S(1)} %shard_map.76.attended.g0), channel_id=1, source_target_pairs={{16,0},{24,8},{0,16},{8,24},{17,1},{25,9},{1,17},{9,25},{18,2},{26... | collective-permute-start | bytes 933896 | tf_op jit(solution)/shard_map/ppermute | solution.py:318
  67.8 3.0 %collective-permute-start.5 = (bf16[304,512]{1,0:T(8,128)(2,1)S(1)}, bf16[304,512]{1,0:T(8,128)(2,1)S(1)}, u32[]{:S(2)}, u32[]{:S(2)}) collective-permute-start(bf16[304,512]{1,0:T(8,128)(2,1)S(1)} %shard_map.76.attended.g0), channel_id=1, source_target_pairs={{8,0},{16,8},{24,16},{0,24},{9,1},{17,9},{25,17},{1,25},{10,2},{18... | collective-permute-start | bytes 933896 | tf_op jit(solution)/shard_map/ppermute | solution.py:318
  70.9 0.0 collective-permute-done.9.above_w.after
  70.9 0.0 collective-permute-done.8.below_w.before
  71.0 2.3 %collective-permute-start.10 = (bf16[1200,128]{1,0:T(8,128)(2,1)S(1)}, bf16[1200,128]{1,0:T(8,128)(2,1)S(1)}, u32[]{:S(2)}, u32[]{:S(2)}) collective-permute-start(bf16[1200,128]{1,0:T(8,128)(2,1)S(1)} %get-tuple-element.24), channel_id=1, source_target_pairs={{480,0},{0,32},{32,64},{64,96},{96,128},{128,160},{160,192},{192,2... | collective-permute-start | bytes 921608 | tf_op jit(solution)/shard_map/ppermute | solution.py:265
  73.2 4.2 %collective-permute-start.11 = (bf16[1200,128]{1,0:T(8,128)(2,1)S(1)}, bf16[1200,128]{1,0:T(8,128)(2,1)S(1)}, u32[]{:S(2)}, u32[]{:S(2)}) collective-permute-start(bf16[1200,128]{1,0:T(8,128)(2,1)S(1)} %get-tuple-element.25), channel_id=1, source_target_pairs={{32,0},{64,32},{96,64},{128,96},{160,128},{192,160},{224,192},{256... | collective-permute-start | bytes 921608 | tf_op jit(solution)/shard_map/ppermute | solution.py:265
  77.5 2.6 %collective-permute-done.10.before2 = bf16[1200,128]{1,0:T(8,128)(2,1)S(1)} collective-permute-done((bf16[1200,128]{1,0:T(8,128)(2,1)S(1)}, bf16[1200,128]{1,0:T(8,128)(2,1)S(1)}, u32[]{:S(2)}, u32[]{:S(2)}) %collective-permute-start.10) | collective-permute-done | bytes 307232 | tf_op jit(solution)/shard_map/ppermute | solution.py:265
  80.1 1.2 %collective-permute-done.11.after2 = bf16[1200,128]{1,0:T(8,128)(2,1)S(1)} collective-permute-done((bf16[1200,128]{1,0:T(8,128)(2,1)S(1)}, bf16[1200,128]{1,0:T(8,128)(2,1)S(1)}, u32[]{:S(2)}, u32[]{:S(2)}) %collective-permute-start.11) | collective-permute-done | bytes 307232 | tf_op jit(solution)/shard_map/ppermute | solution.py:265
  81.2 0.0 collective-permute-done.7.g3
  81.2 0.0 collective-permute-done.6.g2
  81.2 0.0 collective-permute-done.5.g1
  81.3 1.4 %shard_map.78 = (bf16[16,160,128]{2,1,0:T(8,128)(2,1)S(1)}, bf16[640,512]{1,0:T(8,128)(2,1)S(1)}, bf16[640,640]{1,0:T(8,128)(2,1)S(1)}) custom-call(s32[1]{0:T(128)} %bitcast.ci, s32[1]{0:T(128)} %bitcast.1.zi, s32[1]{0:T(128)} %bitcast.2.xi, bf16[304,512]{1,0:T(8,128)(2,1)S(1)} %shard_map.76.attended.g0, bf16[304,512]{1,0:T(8,128)(2,1)S(1)} %collective-permute-done.5.g1, ...), custom_call_target="tpu_custom_call" | custom-call | tf_op jit(solution)/shard_map/pallas_call | solution.py:321
  82.6 8.1 %collective-permute-start.12 = (bf16[16,160,128]{2,1,0:T(8,128)(2,1)S(1)}, bf16[16,160,128]{2,1,0:T(8,128)(2,1)S(1)}, u32[]{:S(2)}, u32[]{:S(2)}) collective-permute-start(bf16[16,160,128]{2,1,0:T(8,128)(2,1)S(1)} %get-tuple-element.28), channel_id=1, source_target_pairs={{0,1},{1,0},{2,3},{3,2},{4,5},{5,4},{6,7},{7,6},{8,9},{9,8},{10,11... | collective-permute-start | bytes 1966088 | tf_op jit(solution)/shard_map/ppermute | solution.py:328
  90.7 0.7 shard_map.79
  91.4 1.0 collective-permute-done.12
  92.4 0.2 add_convert_fusion
  92.6 15.9 %all_to_all.10.r_ref = bf16[16,160,128]{2,1,0:T(8,128)(2,1)S(1)} all-to-all(bf16[16,160,128]{2,1,0:T(8,128)(2,1)S(1)} %add_convert_fusion), channel_id=1, replica_groups=mesh['z'=16,'x'=4,'y'=4,'c'=2] {'x','y'}, dimensions={0} | all-to-all | bytes 1310720 | tf_op jit(solution)/shard_map/all_to_all | solution.py:331
  108.5 0.8 shard_map.80
  (2 shorter events, 0.1 us)
Async XLA Ops:
  2.8 10.7 %copy-start = (bf16[640,80]{0,1:T(8,128)(2,1)S(1)}, bf16[640,80]{0,1:T(8,128)(2,1)}, u32[]{:S(2)}) copy-start(bf16[640,80]{0,1:T(8,128)(2,1)} %param.13) | copy-start | bytes 307204
  2.9 31.5 %copy-start.1 = (s32[64,8]{0,1:T(8,128)S(1)}, s32[64,8]{0,1:T(8,128)}, u32[]{:S(2)}) copy-start(s32[64,8]{0,1:T(8,128)} %param.12) | copy-start | bytes 6148
  2.9 41.0 %all-to-all-start = ((bf16[32,192,128]{2,1,0:T(8,128)(2,1)}), bf16[32,192,128]{2,1,0:T(8,128)(2,1)S(1)}, u32[]{:S(2)}, u32[]{:S(2)}) async-start(bf16[32,192,128]{2,1,0:T(8,128)(2,1)} %shard_map.73), calls=%async_computation | async-start | bytes 3145728 | tf_op jit(solution)/shard_map/all_to_all | solution.py:297
  13.7 20.9 %collective-permute-start.2 = (bf16[400,128]{1,0:T(8,128)(2,1)S(1)}, bf16[400,128]{1,0:T(8,128)(2,1)S(1)}, u32[]{:S(2)}, u32[]{:S(2)}) collective-permute-start(bf16[400,128]{1,0:T(8,128)(2,1)S(1)} %bitcast.9), channel_id=1, source_target_pairs={{416,0},{97,1},{448,32},{129,33},{480,64},{161,65},{0,96},{193,97}... | collective-permute-start | bytes 307208 | tf_op jit(solution)/shard_map/ppermute | solution.py:270
  23.8 14.8 %collective-permute-start.1 = (bf16[400,128]{1,0:T(8,128)(2,1)S(1)}, bf16[400,128]{1,0:T(8,128)(2,1)S(1)}, u32[]{:S(2)}, u32[]{:S(2)}) collective-permute-start(bf16[400,128]{1,0:T(8,128)(2,1)S(1)} %bitcast.10), channel_id=1, source_target_pairs={{320,0},{193,1},{352,32},{225,33},{384,64},{257,65},{416,96},{289,... | collective-permute-start | bytes 307208 | tf_op jit(solution)/shard_map/ppermute | solution.py:270
  29.0 14.9 %collective-permute-start = (bf16[400,128]{1,0:T(8,128)(2,1)S(1)}, bf16[400,128]{1,0:T(8,128)(2,1)S(1)}, u32[]{:S(2)}, u32[]{:S(2)}) collective-permute-start(bf16[400,128]{1,0:T(8,128)(2,1)S(1)} %bitcast.11), channel_id=1, source_target_pairs={{160,0},{353,1},{192,32},{385,33},{224,64},{417,65},{256,96},{449,... | collective-permute-start | bytes 307208 | tf_op jit(solution)/shard_map/ppermute | solution.py:270
  44.7 14.1 %collective-permute-start.3 = (bf16[1280,128]{1,0:T(8,128)(2,1)S(1)}, bf16[1280,128]{1,0:T(8,128)(2,1)S(1)}, u32[]{:S(2)}, u32[]{:S(2)}) collective-permute-start(bf16[1280,128]{1,0:T(8,128)(2,1)S(1)} %get-tuple-element.19), channel_id=1, source_target_pairs={{480,0},{0,32},{32,64},{64,96},{96,128},{128,160},{160,192},{192,2... | collective-permute-start | bytes 983048 | tf_op jit(solution)/shard_map/ppermute | solution.py:265
  48.3 10.6 %collective-permute-start.4 = (bf16[1280,128]{1,0:T(8,128)(2,1)S(1)}, bf16[1280,128]{1,0:T(8,128)(2,1)S(1)}, u32[]{:S(2)}, u32[]{:S(2)}) collective-permute-start(bf16[1280,128]{1,0:T(8,128)(2,1)S(1)} %get-tuple-element.20), channel_id=1, source_target_pairs={{32,0},{64,32},{96,64},{128,96},{160,128},{192,160},{224,192},{256... | collective-permute-start | bytes 983048 | tf_op jit(solution)/shard_map/ppermute | solution.py:265
  51.2 19.7 %collective-permute-start.9 = (bf16[1200,128]{1,0:T(8,128)(2,1)S(1)}, bf16[1200,128]{1,0:T(8,128)(2,1)S(1)}, u32[]{:S(2)}, u32[]{:S(2)}) collective-permute-start(bf16[1200,128]{1,0:T(8,128)(2,1)S(1)} %get-tuple-element.23), channel_id=1, source_target_pairs={{32,0},{64,32},{96,64},{128,96},{160,128},{192,160},{224,192},{256... | collective-permute-start | bytes 921608 | tf_op jit(solution)/shard_map/ppermute | solution.py:265
  53.1 17.8 %collective-permute-start.8 = (bf16[1200,128]{1,0:T(8,128)(2,1)S(1)}, bf16[1200,128]{1,0:T(8,128)(2,1)S(1)}, u32[]{:S(2)}, u32[]{:S(2)}) collective-permute-start(bf16[1200,128]{1,0:T(8,128)(2,1)S(1)} %get-tuple-element.23), channel_id=1, source_target_pairs={{480,0},{0,32},{32,64},{64,96},{96,128},{128,160},{160,192},{192,2... | collective-permute-start | bytes 921608 | tf_op jit(solution)/shard_map/ppermute | solution.py:265
  60.1 21.1 %collective-permute-start.7 = (bf16[304,512]{1,0:T(8,128)(2,1)S(1)}, bf16[304,512]{1,0:T(8,128)(2,1)S(1)}, u32[]{:S(2)}, u32[]{:S(2)}) collective-permute-start(bf16[304,512]{1,0:T(8,128)(2,1)S(1)} %shard_map.76.attended.g0), channel_id=1, source_target_pairs={{24,0},{0,8},{8,16},{16,24},{25,1},{1,9},{9,17},{17,25},{26,2},{2,... | collective-permute-start | bytes 933896 | tf_op jit(solution)/shard_map/ppermute | solution.py:318
  63.5 17.8 %collective-permute-start.6 = (bf16[304,512]{1,0:T(8,128)(2,1)S(1)}, bf16[304,512]{1,0:T(8,128)(2,1)S(1)}, u32[]{:S(2)}, u32[]{:S(2)}) collective-permute-start(bf16[304,512]{1,0:T(8,128)(2,1)S(1)} %shard_map.76.attended.g0), channel_id=1, source_target_pairs={{16,0},{24,8},{0,16},{8,24},{17,1},{25,9},{1,17},{9,25},{18,2},{26... | collective-permute-start | bytes 933896 | tf_op jit(solution)/shard_map/ppermute | solution.py:318
  67.8 13.4 %collective-permute-start.5 = (bf16[304,512]{1,0:T(8,128)(2,1)S(1)}, bf16[304,512]{1,0:T(8,128)(2,1)S(1)}, u32[]{:S(2)}, u32[]{:S(2)}) collective-permute-start(bf16[304,512]{1,0:T(8,128)(2,1)S(1)} %shard_map.76.attended.g0), channel_id=1, source_target_pairs={{8,0},{16,8},{24,16},{0,24},{9,1},{17,9},{25,17},{1,25},{10,2},{18... | collective-permute-start | bytes 933896 | tf_op jit(solution)/shard_map/ppermute | solution.py:318
  71.0 9.1 %collective-permute-start.10 = (bf16[1200,128]{1,0:T(8,128)(2,1)S(1)}, bf16[1200,128]{1,0:T(8,128)(2,1)S(1)}, u32[]{:S(2)}, u32[]{:S(2)}) collective-permute-start(bf16[1200,128]{1,0:T(8,128)(2,1)S(1)} %get-tuple-element.24), channel_id=1, source_target_pairs={{480,0},{0,32},{32,64},{64,96},{96,128},{128,160},{160,192},{192,2... | collective-permute-start | bytes 921608 | tf_op jit(solution)/shard_map/ppermute | solution.py:265
  73.2 8.0 %collective-permute-start.11 = (bf16[1200,128]{1,0:T(8,128)(2,1)S(1)}, bf16[1200,128]{1,0:T(8,128)(2,1)S(1)}, u32[]{:S(2)}, u32[]{:S(2)}) collective-permute-start(bf16[1200,128]{1,0:T(8,128)(2,1)S(1)} %get-tuple-element.25), channel_id=1, source_target_pairs={{32,0},{64,32},{96,64},{128,96},{160,128},{192,160},{224,192},{256... | collective-permute-start | bytes 921608 | tf_op jit(solution)/shard_map/ppermute | solution.py:265
  82.6 9.8 %collective-permute-start.12 = (bf16[16,160,128]{2,1,0:T(8,128)(2,1)S(1)}, bf16[16,160,128]{2,1,0:T(8,128)(2,1)S(1)}, u32[]{:S(2)}, u32[]{:S(2)}) collective-permute-start(bf16[16,160,128]{2,1,0:T(8,128)(2,1)S(1)} %get-tuple-element.28), channel_id=1, source_target_pairs={{0,1},{1,0},{2,3},{3,2},{4,5},{5,4},{6,7},{7,6},{8,9},{9,8},{10,11... | collective-permute-start | bytes 1966088 | tf_op jit(solution)/shard_map/ppermute | solution.py:328

commit v5 on v4

--- a/solution.py
+++ b/solution.py
@@ -100,10 +100,12 @@
     )
 
 
-def select_kernel(lists, zi, r_ref, *rest):
-    held, (up_ref, down_ref, joined_ref) = rest[:3], rest[4:]
-    for i, ref in enumerate(held):
-        joined_ref[i * BLOCK : i * BLOCK + BLOCK] = ref[...]
+def join_kernel(*refs):
+    for i, ref in enumerate(refs[:3]):
+        refs[-1][i * BLOCK : i * BLOCK + BLOCK] = ref[...]
+
+
+def select_kernel(lists, zi, r_ref, up_ref, down_ref):
     z = zi[0]
     for blocks, target in ((listed_above(lists, z), up_ref), (listed_below(lists, z), down_ref)):
         for slot, block in enumerate(blocks):
@@ -155,6 +157,7 @@
 def attend_rest_kernel(lists, zi, r_ref, prev_ref, next_ref, sum_ref, stat_ref, out_ref):
     z = zi[0]
     near = listed_above(lists, z - 1), listed_below(lists, z + 1)
+    out_ref[272:] = jnp.zeros((32, 512), BF)
     parts = []
     for x in range(NX):
         ref, side = ((prev_ref, 0), (next_ref, 1))[x // 2]
@@ -295,9 +298,8 @@
     held = [columns] + [from_either(columns, step) for step in HELD[1:]]
     last = from_either(columns, LAST)
     mine = lax.all_to_all(packed, plane, split_axis=0, concat_axis=0, tiled=True)
-    up, down, joined = call(
-        select_kernel, (shape(SENT, HD), shape(SENT, HD), shape(3 * BLOCK, HD)), [SMEM, SMEM] + [VMEM] * 4 + [ANY], (VMEM,) * 3
-    )(lists, zi, mine, *held, last)
+    up, down = call(select_kernel, (shape(SENT, HD),) * 2, [SMEM, SMEM, VMEM], (VMEM, VMEM))(lists, zi, mine)
+    joined = call(join_kernel, shape(3 * BLOCK, HD), [VMEM] * 3 + [ANY])(*held, last)
     before, after = from_plane(up, -1), from_plane(down, 1)
     sums, stats = call(
         attend_own_kernel,

time: 110 us -> 103 us (0.936)
  waiting for transfers between devices: 14.3 us -> 7.8 us
    ppermute x3, waiting for transfers between devices: 9.34 us -> 0.01 us  [from_either(): return lax.ppermute(value, ('z', 'c'), pairs)]
    ppermute x6, starting transfers between devices: 18.3 us -> 23 us  [from_plane(): return lax.ppermute(value, 'z', [((i + step) % NZ, i) for i in range(NZ)])]
    ppermute x1, starting transfers between devices: 8.08 us -> 4.37 us  [per_device(): other = lax.ppermute(give, 'c', [(0, 1), (1, 0)])]
    ppermute x3, starting transfers between devices: 10.7 us -> 8.76 us  [per_device(): lax.ppermute(attended, 'x', [((i + step) % NX, i) for i in range(NX)])]
    all_to_all x1, waiting for transfers between devices: 0.01 us -> 1.75 us  [per_device(): lax.all_to_all(packed, plane, split_axis=0, concat_axis=0, tiled=True)]
  transfers between devices with their start and end apart: 14 -> 14, of which waited for: 6 -> 5; matrix products, arithmetic and copies ran while one was open for 0% -> 0% of each run, Pallas kernels for 4% -> 5%
where the time goes in v5:
time: 103 us; the launch traced here: 102 us
  starting transfers between devices  67.4 us (65%)
  blocking collectives  15.7 us (15%)
  Pallas kernels  9.96 us (10%)
  waiting for transfers between devices  7.8 us (8%)
    ppermute x6, starting transfers between devices, from_plane(): return lax.ppermute(value, 'z', [((i + step) % NZ, i) for i in range(NZ)])  23 us
    ppermute x3, starting transfers between devices, from_either(): return lax.ppermute(value, ('z', 'c'), pairs)  20.6 us
    all_to_all x1, blocking collectives, per_device(): lax.all_to_all(terms, ('x', 'y'), split_axis=0, concat_axis=0, tiled=True)  15.7 us
    all_to_all x1, starting transfers between devices, per_device(): lax.all_to_all(packed, plane, split_axis=0, concat_axis=0, tiled=True)  10.6 us
    ppermute x3, starting transfers between devices, per_device(): lax.ppermute(attended, 'x', [((i + step) % NX, i) for i in range(NX)])  8.76 us
    ppermute x1, starting transfers between devices, per_device(): other = lax.ppermute(give, 'c', [(0, 1), (1, 0)])  4.37 us
    ppermute x6, waiting for transfers between devices, from_plane(): return lax.ppermute(value, 'z', [((i + step) % NZ, i) for i in range(NZ)])  4.34 us
    pallas_call x1, Pallas kernels, per_device(): call(pack_kernel, shape(32, CHUNK, HD), [ANY] * 5, VMEM, [pltpu.VMEM((QRO...  2.84 us
  transfers between devices with their start and end apart: 14, of which 5 were waited for; matrix products, arithmetic and copies ran while one was open for 0% of the time, Pallas kernels for 5%

profile of v5, /device:TPU:1, one launch (start us, length us, event | category | flops | bytes accessed | tf_op | source)
XLA Modules:
  0.0 101.6 jit_solution(8130013445084064409)
XLA Ops:
  0.0 2.8 %shard_map.73 = bf16[32,192,128]{2,1,0:T(8,128)(2,1)} custom-call(bf16[16,5120]{1,0:T(8,128)(2,1)} %q_hbm.1, bf16[64,5120]{1,0:T(8,128)(2,1)} %k_hbm.1, bf16[64,5120]{1,0:T(8,128)(2,1)} %v_hbm.1, f32[1,5120]{1,0:T(1,128)} %bitcast.15, f32[1,5120]{1,0:T(1,128)} %bitcast.16), custom_call_target="tpu_custom_call" | custom-call | tf_op jit(solution)/shard_map/pallas_call | solution.py:281
  2.8 0.0 copy-start
  2.9 0.0 copy-start.1
  2.9 10.6 %all-to-all-start = ((bf16[32,192,128]{2,1,0:T(8,128)(2,1)}), bf16[32,192,128]{2,1,0:T(8,128)(2,1)S(1)}, u32[]{:S(2)}, u32[]{:S(2)}) async-start(bf16[32,192,128]{2,1,0:T(8,128)(2,1)} %shard_map.73), calls=%async_computation | async-start | bytes 3145728 | tf_op jit(solution)/shard_map/all_to_all | solution.py:300
  13.5 0.0 copy-done
  13.5 0.1 reshape.30
  13.7 10.1 %collective-permute-start.7 = (bf16[400,128]{1,0:T(8,128)(2,1)S(1)}, bf16[400,128]{1,0:T(8,128)(2,1)S(1)}, u32[]{:S(2)}, u32[]{:S(2)}) collective-permute-start(bf16[400,128]{1,0:T(8,128)(2,1)S(1)} %bitcast.9), channel_id=1, source_target_pairs={{416,0},{97,1},{448,32},{129,33},{480,64},{161,65},{0,96},{193,97}... | collective-permute-start | bytes 307208 | tf_op jit(solution)/shard_map/ppermute | solution.py:273
  23.8 5.2 %collective-permute-start.6 = (bf16[400,128]{1,0:T(8,128)(2,1)S(1)}, bf16[400,128]{1,0:T(8,128)(2,1)S(1)}, u32[]{:S(2)}, u32[]{:S(2)}) collective-permute-start(bf16[400,128]{1,0:T(8,128)(2,1)S(1)} %bitcast.10), channel_id=1, source_target_pairs={{320,0},{193,1},{352,32},{225,33},{384,64},{257,65},{416,96},{289,... | collective-permute-start | bytes 307208 | tf_op jit(solution)/shard_map/ppermute | solution.py:273
  29.0 5.4 %collective-permute-start.5 = (bf16[400,128]{1,0:T(8,128)(2,1)S(1)}, bf16[400,128]{1,0:T(8,128)(2,1)S(1)}, u32[]{:S(2)}, u32[]{:S(2)}) collective-permute-start(bf16[400,128]{1,0:T(8,128)(2,1)S(1)} %bitcast.11), channel_id=1, source_target_pairs={{160,0},{353,1},{192,32},{385,33},{224,64},{417,65},{256,96},{449,... | collective-permute-start | bytes 307208 | tf_op jit(solution)/shard_map/ppermute | solution.py:273
  34.4 0.0 copy-done.1
  34.4 0.1 copy.9
  34.5 0.1 reshape.27.lists
  34.5 1.7 %all-to-all-done.r_ref = bf16[32,192,128]{2,1,0:T(8,128)(2,1)S(1)} async-done(((bf16[32,192,128]{2,1,0:T(8,128)(2,1)}), bf16[32,192,128]{2,1,0:T(8,128)(2,1)S(1)}, u32[]{:S(2)}, u32[]{:S(2)}) %all-to-all-start) | async-done | bytes 1572896 | tf_op jit(solution)/shard_map/all_to_all | solution.py:300
  36.3 0.7 shard_map.74
  37.0 1.9 %collective-permute-start = (bf16[1280,128]{1,0:T(8,128)(2,1)S(1)}, bf16[1280,128]{1,0:T(8,128)(2,1)S(1)}, u32[]{:S(2)}, u32[]{:S(2)}) collective-permute-start(bf16[1280,128]{1,0:T(8,128)(2,1)S(1)} %get-tuple-element.17), channel_id=1, source_target_pairs={{480,0},{0,32},{32,64},{64,96},{96,128},{128,160},{160,192},{192,2... | collective-permute-start | bytes 983048 | tf_op jit(solution)/shard_map/ppermute | solution.py:268
  39.0 9.1 %collective-permute-start.1 = (bf16[1280,128]{1,0:T(8,128)(2,1)S(1)}, bf16[1280,128]{1,0:T(8,128)(2,1)S(1)}, u32[]{:S(2)}, u32[]{:S(2)}) collective-permute-start(bf16[1280,128]{1,0:T(8,128)(2,1)S(1)} %get-tuple-element.18), channel_id=1, source_target_pairs={{32,0},{64,32},{96,64},{128,96},{160,128},{192,160},{224,192},{256... | collective-permute-start | bytes 983048 | tf_op jit(solution)/shard_map/ppermute | solution.py:268
  48.1 0.0 collective-permute-done.7.refs_3_.last
  48.1 0.0 collective-permute-done.6.refs_2_.down6
  48.1 0.0 collective-permute-done.5.refs_1_.up5
  48.2 3.4 %collective-permute-start.9 = (bf16[1200,128]{1,0:T(8,128)(2,1)S(1)}, bf16[1200,128]{1,0:T(8,128)(2,1)S(1)}, u32[]{:S(2)}, u32[]{:S(2)}) collective-permute-start(bf16[1200,128]{1,0:T(8,128)(2,1)S(1)} %shard_map.77), channel_id=1, source_target_pairs={{32,0},{64,32},{96,64},{128,96},{160,128},{192,160},{224,192},{256... | collective-permute-start | bytes 921608 | tf_op jit(solution)/shard_map/ppermute | solution.py:268
  51.5 1.9 %collective-permute-start.8 = (bf16[1200,128]{1,0:T(8,128)(2,1)S(1)}, bf16[1200,128]{1,0:T(8,128)(2,1)S(1)}, u32[]{:S(2)}, u32[]{:S(2)}) collective-permute-start(bf16[1200,128]{1,0:T(8,128)(2,1)S(1)} %shard_map.77), channel_id=1, source_target_pairs={{480,0},{0,32},{32,64},{64,96},{96,128},{128,160},{160,192},{192,2... | collective-permute-start | bytes 921608 | tf_op jit(solution)/shard_map/ppermute | solution.py:268
  53.5 2.3 %shard_map.75 = (f32[256,512]{1,0:T(8,128)S(1)}, f32[8,512]{1,0:T(8,128)S(1)}) custom-call(s32[512]{0:T(512)S(1)} %reshape.27.lists, s32[1]{0:T(128)} %bitcast.1.zi, bf16[32,192,128]{2,1,0:T(8,128)(2,1)S(1)} %all-to-all-done.r_ref), custom_call_target="tpu_custom_call" | custom-call | tf_op jit(solution)/shard_map/pallas_call | solution.py:304
  55.8 0.0 collective-permute-done.prev_ref
  55.8 0.0 collective-permute-done.1.next_ref
  55.8 1.2 %shard_map.76.attended.g0 = bf16[304,512]{1,0:T(8,128)(2,1)S(1)} custom-call(s32[512]{0:T(512)S(1)} %reshape.27.lists, s32[1]{0:T(128)} %bitcast.1.zi, bf16[32,192,128]{2,1,0:T(8,128)(2,1)S(1)} %all-to-all-done.r_ref, bf16[1280,128]{1,0:T(8,128)(2,1)S(1)} %collective-permute-done.prev_ref, bf16[1280,128]{1,0:T(8,128)(2,1)S(1)} %collective-permute-done.1.next_ref, ...), custom_call_target="tpu_custom_call" | custom-call | tf_op jit(solution)/shard_map/pallas_call | solution.py:311
  56.9 1.9 %collective-permute-start.4 = (bf16[304,512]{1,0:T(8,128)(2,1)S(1)}, bf16[304,512]{1,0:T(8,128)(2,1)S(1)}, u32[]{:S(2)}, u32[]{:S(2)}) collective-permute-start(bf16[304,512]{1,0:T(8,128)(2,1)S(1)} %shard_map.76.attended.g0), channel_id=1, source_target_pairs={{24,0},{0,8},{8,16},{16,24},{25,1},{1,9},{9,17},{17,25},{26,2},{2,... | collective-permute-start | bytes 933896 | tf_op jit(solution)/shard_map/ppermute | solution.py:320
  58.9 3.6 %collective-permute-start.3 = (bf16[304,512]{1,0:T(8,128)(2,1)S(1)}, bf16[304,512]{1,0:T(8,128)(2,1)S(1)}, u32[]{:S(2)}, u32[]{:S(2)}) collective-permute-start(bf16[304,512]{1,0:T(8,128)(2,1)S(1)} %shard_map.76.attended.g0), channel_id=1, source_target_pairs={{16,0},{24,8},{0,16},{8,24},{17,1},{25,9},{1,17},{9,25},{18,2},{26... | collective-permute-start | bytes 933896 | tf_op jit(solution)/shard_map/ppermute | solution.py:320
  62.5 3.2 %collective-permute-start.2 = (bf16[304,512]{1,0:T(8,128)(2,1)S(1)}, bf16[304,512]{1,0:T(8,128)(2,1)S(1)}, u32[]{:S(2)}, u32[]{:S(2)}) collective-permute-start(bf16[304,512]{1,0:T(8,128)(2,1)S(1)} %shard_map.76.attended.g0), channel_id=1, source_target_pairs={{8,0},{16,8},{24,16},{0,24},{9,1},{17,9},{25,17},{1,25},{10,2},{18... | collective-permute-start | bytes 933896 | tf_op jit(solution)/shard_map/ppermute | solution.py:320
  65.7 0.0 collective-permute-done.9.above_w.after
  65.7 0.0 collective-permute-done.8.below_w.before
  65.8 1.9 %collective-permute-start.10 = (bf16[1200,128]{1,0:T(8,128)(2,1)S(1)}, bf16[1200,128]{1,0:T(8,128)(2,1)S(1)}, u32[]{:S(2)}, u32[]{:S(2)}) collective-permute-start(bf16[1200,128]{1,0:T(8,128)(2,1)S(1)} %get-tuple-element.22), channel_id=1, source_target_pairs={{480,0},{0,32},{32,64},{64,96},{96,128},{128,160},{160,192},{192,2... | collective-permute-start | bytes 921608 | tf_op jit(solution)/shard_map/ppermute | solution.py:268
  67.7 4.7 %collective-permute-start.11 = (bf16[1200,128]{1,0:T(8,128)(2,1)S(1)}, bf16[1200,128]{1,0:T(8,128)(2,1)S(1)}, u32[]{:S(2)}, u32[]{:S(2)}) collective-permute-start(bf16[1200,128]{1,0:T(8,128)(2,1)S(1)} %get-tuple-element.23), channel_id=1, source_target_pairs={{32,0},{64,32},{96,64},{128,96},{160,128},{192,160},{224,192},{256... | collective-permute-start | bytes 921608 | tf_op jit(solution)/shard_map/ppermute | solution.py:268
  72.4 3.4 %collective-permute-done.10.before2 = bf16[1200,128]{1,0:T(8,128)(2,1)S(1)} collective-permute-done((bf16[1200,128]{1,0:T(8,128)(2,1)S(1)}, bf16[1200,128]{1,0:T(8,128)(2,1)S(1)}, u32[]{:S(2)}, u32[]{:S(2)}) %collective-permute-start.10) | collective-permute-done | bytes 307232 | tf_op jit(solution)/shard_map/ppermute | solution.py:268
  75.9 0.9 collective-permute-done.11.after2
  76.8 0.0 collective-permute-done.4.g3
  76.8 0.0 collective-permute-done.3.g2
  76.8 0.7 collective-permute-done.2.g1
  77.5 1.4 %shard_map.79 = (bf16[16,160,128]{2,1,0:T(8,128)(2,1)S(1)}, bf16[640,512]{1,0:T(8,128)(2,1)S(1)}, bf16[640,640]{1,0:T(8,128)(2,1)S(1)}) custom-call(s32[1]{0:T(128)} %bitcast.ci, s32[1]{0:T(128)} %bitcast.1.zi, s32[1]{0:T(128)} %bitcast.2.xi, bf16[304,512]{1,0:T(8,128)(2,1)S(1)} %shard_map.76.attended.g0, bf16[304,512]{1,0:T(8,128)(2,1)S(1)} %collective-permute-done.2.g1, ...), custom_call_target="tpu_custom_call" | custom-call | tf_op jit(solution)/shard_map/pallas_call | solution.py:323
  78.8 4.4 %collective-permute-start.12 = (bf16[16,160,128]{2,1,0:T(8,128)(2,1)S(1)}, bf16[16,160,128]{2,1,0:T(8,128)(2,1)S(1)}, u32[]{:S(2)}, u32[]{:S(2)}) collective-permute-start(bf16[16,160,128]{2,1,0:T(8,128)(2,1)S(1)} %get-tuple-element.26), channel_id=1, source_target_pairs={{0,1},{1,0},{2,3},{3,2},{4,5},{5,4},{6,7},{7,6},{8,9},{9,8},{10,11... | collective-permute-start | bytes 1966088 | tf_op jit(solution)/shard_map/ppermute | solution.py:330
  83.2 0.7 shard_map.80
  83.9 1.0 collective-permute-done.12
  84.9 0.2 add_convert_fusion
  85.1 15.7 %all_to_all.10.r_ref = bf16[16,160,128]{2,1,0:T(8,128)(2,1)S(1)} all-to-all(bf16[16,160,128]{2,1,0:T(8,128)(2,1)S(1)} %add_convert_fusion), channel_id=1, replica_groups=mesh['z'=16,'x'=4,'y'=4,'c'=2] {'x','y'}, dimensions={0} | all-to-all | bytes 1310720 | tf_op jit(solution)/shard_map/all_to_all | solution.py:333
  100.8 0.8 shard_map.81
  (3 shorter events, 0.1 us)
Async XLA Ops:
  2.8 10.7 %copy-start = (bf16[640,80]{0,1:T(8,128)(2,1)S(1)}, bf16[640,80]{0,1:T(8,128)(2,1)}, u32[]{:S(2)}) copy-start(bf16[640,80]{0,1:T(8,128)(2,1)} %param.13) | copy-start | bytes 307204
  2.9 31.5 %copy-start.1 = (s32[64,8]{0,1:T(8,128)S(1)}, s32[64,8]{0,1:T(8,128)}, u32[]{:S(2)}) copy-start(s32[64,8]{0,1:T(8,128)} %param.12) | copy-start | bytes 6148
  2.9 33.4 %all-to-all-start = ((bf16[32,192,128]{2,1,0:T(8,128)(2,1)}), bf16[32,192,128]{2,1,0:T(8,128)(2,1)S(1)}, u32[]{:S(2)}, u32[]{:S(2)}) async-start(bf16[32,192,128]{2,1,0:T(8,128)(2,1)} %shard_map.73), calls=%async_computation | async-start | bytes 3145728 | tf_op jit(solution)/shard_map/all_to_all | solution.py:300
  13.7 34.4 %collective-permute-start.7 = (bf16[400,128]{1,0:T(8,128)(2,1)S(1)}, bf16[400,128]{1,0:T(8,128)(2,1)S(1)}, u32[]{:S(2)}, u32[]{:S(2)}) collective-permute-start(bf16[400,128]{1,0:T(8,128)(2,1)S(1)} %bitcast.9), channel_id=1, source_target_pairs={{416,0},{97,1},{448,32},{129,33},{480,64},{161,65},{0,96},{193,97}... | collective-permute-start | bytes 307208 | tf_op jit(solution)/shard_map/ppermute | solution.py:273
  23.8 24.3 %collective-permute-start.6 = (bf16[400,128]{1,0:T(8,128)(2,1)S(1)}, bf16[400,128]{1,0:T(8,128)(2,1)S(1)}, u32[]{:S(2)}, u32[]{:S(2)}) collective-permute-start(bf16[400,128]{1,0:T(8,128)(2,1)S(1)} %bitcast.10), channel_id=1, source_target_pairs={{320,0},{193,1},{352,32},{225,33},{384,64},{257,65},{416,96},{289,... | collective-permute-start | bytes 307208 | tf_op jit(solution)/shard_map/ppermute | solution.py:273
  29.0 19.1 %collective-permute-start.5 = (bf16[400,128]{1,0:T(8,128)(2,1)S(1)}, bf16[400,128]{1,0:T(8,128)(2,1)S(1)}, u32[]{:S(2)}, u32[]{:S(2)}) collective-permute-start(bf16[400,128]{1,0:T(8,128)(2,1)S(1)} %bitcast.11), channel_id=1, source_target_pairs={{160,0},{353,1},{192,32},{385,33},{224,64},{417,65},{256,96},{449,... | collective-permute-start | bytes 307208 | tf_op jit(solution)/shard_map/ppermute | solution.py:273
  37.0 18.7 %collective-permute-start = (bf16[1280,128]{1,0:T(8,128)(2,1)S(1)}, bf16[1280,128]{1,0:T(8,128)(2,1)S(1)}, u32[]{:S(2)}, u32[]{:S(2)}) collective-permute-start(bf16[1280,128]{1,0:T(8,128)(2,1)S(1)} %get-tuple-element.17), channel_id=1, source_target_pairs={{480,0},{0,32},{32,64},{64,96},{96,128},{128,160},{160,192},{192,2... | collective-permute-start | bytes 983048 | tf_op jit(solution)/shard_map/ppermute | solution.py:268
  39.0 16.8 %collective-permute-start.1 = (bf16[1280,128]{1,0:T(8,128)(2,1)S(1)}, bf16[1280,128]{1,0:T(8,128)(2,1)S(1)}, u32[]{:S(2)}, u32[]{:S(2)}) collective-permute-start(bf16[1280,128]{1,0:T(8,128)(2,1)S(1)} %get-tuple-element.18), channel_id=1, source_target_pairs={{32,0},{64,32},{96,64},{128,96},{160,128},{192,160},{224,192},{256... | collective-permute-start | bytes 983048 | tf_op jit(solution)/shard_map/ppermute | solution.py:268
  48.2 17.6 %collective-permute-start.9 = (bf16[1200,128]{1,0:T(8,128)(2,1)S(1)}, bf16[1200,128]{1,0:T(8,128)(2,1)S(1)}, u32[]{:S(2)}, u32[]{:S(2)}) collective-permute-start(bf16[1200,128]{1,0:T(8,128)(2,1)S(1)} %shard_map.77), channel_id=1, source_target_pairs={{32,0},{64,32},{96,64},{128,96},{160,128},{192,160},{224,192},{256... | collective-permute-start | bytes 921608 | tf_op jit(solution)/shard_map/ppermute | solution.py:268
  51.5 14.2 %collective-permute-start.8 = (bf16[1200,128]{1,0:T(8,128)(2,1)S(1)}, bf16[1200,128]{1,0:T(8,128)(2,1)S(1)}, u32[]{:S(2)}, u32[]{:S(2)}) collective-permute-start(bf16[1200,128]{1,0:T(8,128)(2,1)S(1)} %shard_map.77), channel_id=1, source_target_pairs={{480,0},{0,32},{32,64},{64,96},{96,128},{128,160},{160,192},{192,2... | collective-permute-start | bytes 921608 | tf_op jit(solution)/shard_map/ppermute | solution.py:268
  56.9 19.8 %collective-permute-start.4 = (bf16[304,512]{1,0:T(8,128)(2,1)S(1)}, bf16[304,512]{1,0:T(8,128)(2,1)S(1)}, u32[]{:S(2)}, u32[]{:S(2)}) collective-permute-start(bf16[304,512]{1,0:T(8,128)(2,1)S(1)} %shard_map.76.attended.g0), channel_id=1, source_target_pairs={{24,0},{0,8},{8,16},{16,24},{25,1},{1,9},{9,17},{17,25},{26,2},{2,... | collective-permute-start | bytes 933896 | tf_op jit(solution)/shard_map/ppermute | solution.py:320
  58.9 17.9 %collective-permute-start.3 = (bf16[304,512]{1,0:T(8,128)(2,1)S(1)}, bf16[304,512]{1,0:T(8,128)(2,1)S(1)}, u32[]{:S(2)}, u32[]{:S(2)}) collective-permute-start(bf16[304,512]{1,0:T(8,128)(2,1)S(1)} %shard_map.76.attended.g0), channel_id=1, source_target_pairs={{16,0},{24,8},{0,16},{8,24},{17,1},{25,9},{1,17},{9,25},{18,2},{26... | collective-permute-start | bytes 933896 | tf_op jit(solution)/shard_map/ppermute | solution.py:320
  62.5 15.0 %collective-permute-start.2 = (bf16[304,512]{1,0:T(8,128)(2,1)S(1)}, bf16[304,512]{1,0:T(8,128)(2,1)S(1)}, u32[]{:S(2)}, u32[]{:S(2)}) collective-permute-start(bf16[304,512]{1,0:T(8,128)(2,1)S(1)} %shard_map.76.attended.g0), channel_id=1, source_target_pairs={{8,0},{16,8},{24,16},{0,24},{9,1},{17,9},{25,17},{1,25},{10,2},{18... | collective-permute-start | bytes 933896 | tf_op jit(solution)/shard_map/ppermute | solution.py:320
  65.8 10.1 %collective-permute-start.10 = (bf16[1200,128]{1,0:T(8,128)(2,1)S(1)}, bf16[1200,128]{1,0:T(8,128)(2,1)S(1)}, u32[]{:S(2)}, u32[]{:S(2)}) collective-permute-start(bf16[1200,128]{1,0:T(8,128)(2,1)S(1)} %get-tuple-element.22), channel_id=1, source_target_pairs={{480,0},{0,32},{32,64},{64,96},{96,128},{128,160},{160,192},{192,2... | collective-permute-start | bytes 921608 | tf_op jit(solution)/shard_map/ppermute | solution.py:268
  67.7 9.0 %collective-permute-start.11 = (bf16[1200,128]{1,0:T(8,128)(2,1)S(1)}, bf16[1200,128]{1,0:T(8,128)(2,1)S(1)}, u32[]{:S(2)}, u32[]{:S(2)}) collective-permute-start(bf16[1200,128]{1,0:T(8,128)(2,1)S(1)} %get-tuple-element.23), channel_id=1, source_target_pairs={{32,0},{64,32},{96,64},{128,96},{160,128},{192,160},{224,192},{256... | collective-permute-start | bytes 921608 | tf_op jit(solution)/shard_map/ppermute | solution.py:268
  78.8 6.1 %collective-permute-start.12 = (bf16[16,160,128]{2,1,0:T(8,128)(2,1)S(1)}, bf16[16,160,128]{2,1,0:T(8,128)(2,1)S(1)}, u32[]{:S(2)}, u32[]{:S(2)}) collective-permute-start(bf16[16,160,128]{2,1,0:T(8,128)(2,1)S(1)} %get-tuple-element.26), channel_id=1, source_target_pairs={{0,1},{1,0},{2,3},{3,2},{4,5},{5,4},{6,7},{7,6},{8,9},{9,8},{10,11... | collective-permute-start | bytes 1966088 | tf_op jit(solution)/shard_map/ppermute | solution.py:330

commit v6 on v5

--- a/solution.py
+++ b/solution.py
@@ -33,7 +33,7 @@
     return lax.dot_general(a, b, ((contract[:1], contract[1:]), ((), ())), preferred_element_type=F32)
 
 
-def pack_kernel(q_hbm, k_hbm, v_hbm, qg_hbm, kg_hbm, out_ref, q_ref, k_ref, v_ref, qg_ref, kg_ref, sems):
+def pack_kernel(q_hbm, k_hbm, v_hbm, qg_hbm, kg_hbm, out_hbm, q_ref, k_ref, v_ref, qg_ref, kg_ref, out_ref, sems, out_sems):
     pairs = ((k_hbm, k_ref), (kg_hbm, kg_ref), (q_hbm, q_ref), (qg_hbm, qg_ref), (v_hbm, v_ref))
     copies = [pltpu.make_async_copy(*pair, sems.at[i]) for i, pair in enumerate(pairs)]
     for copy in copies:
@@ -46,29 +46,32 @@
         return lax.rsqrt(jnp.mean(wide * wide, axis=-1, keepdims=True) + 1e-06)
 
     k_inv, q_inv = inverse(k_ref), inverse(q_ref)
-
-    def heads():
+    copies[4].wait()
+    leaving = []
+    for at in (4, 0, 1, 2, 3):
         for group in range(NH):
-            for at in range(GROUP):
-                yield group, at, slice((group * GROUP + at) * HD, (group * GROUP + at + 1) * HD)
-
-    for group, at, cols in heads():
-        k = (k_ref[:, cols].astype(F32) * k_inv * kg_ref[:, cols]).astype(BF)
-        q = (q_ref[:, cols].astype(F32) * q_inv * qg_ref[:, cols]).astype(BF)
+            cols = slice((group * GROUP + at) * HD, (group * GROUP + at + 1) * HD)
+            k = (k_ref[:, cols].astype(F32) * k_inv * kg_ref[:, cols]).astype(BF)
+            q = (q_ref[:, cols].astype(F32) * q_inv * qg_ref[:, cols]).astype(BF)
+            v = v_ref[:, cols]
+            if at < NX:
+                chunk = at * NH + group
+                out_ref[chunk, K0 : K0 + HALF] = k
+                out_ref[chunk, V0 : V0 + HALF] = v
+                out_ref[chunk, Q0 : Q0 + QROWS] = q
+            else:
+                for x in range(NX):
+                    chunk = x * NH + group
+                    rows = slice(x * 16, x * 16 + 16)
+                    out_ref[chunk, K5 : K5 + 16] = k[rows]
+                    out_ref[chunk, V5 : V5 + 16] = v[rows]
+                    out_ref[chunk, Q5 : Q5 + QROWS] = q
         if at < NX:
-            out_ref[at * NH + group, K0 : K0 + HALF] = k
-            out_ref[at * NH + group, Q0 : Q0 + QROWS] = q
-        else:
-            for x in range(NX):
-                out_ref[x * NH + group, K5 : K5 + 16] = k[x * 16 : x * 16 + 16]
-                out_ref[x * NH + group, Q5 : Q5 + QROWS] = q
-    copies[4].wait()
-    for group, at, cols in heads():
-        if at < NX:
-            out_ref[at * NH + group, V0 : V0 + HALF] = v_ref[:, cols]
-        else:
-            for x in range(NX):
-                out_ref[x * NH + group, V5 : V5 + 16] = v_ref[x * 16 : x * 16 + 16, cols]
+            part = pl.ds(at * NH, NH)
+            leaving.append(pltpu.make_async_copy(out_ref.at[part], out_hbm.at[part], out_sems.at[at]))
+            leaving[-1].start()
+    for copy in leaving:
+        copy.wait()
 
 
 def listed_of(lists, block, seq, count):
@@ -223,9 +226,7 @@
 
 
 def hand_on_kernel(below_w, above_w, attended, below_ref, above_ref):
-    del attended
-    below_ref[...] = below_w[...]
-    above_ref[...] = above_w[...]
+    del below_w, above_w, attended, below_ref, above_ref
 
 
 def multiply(w_ref, a_ref, out_ref):
@@ -249,13 +250,14 @@
     out_ref[...] = t_ref[...].T.astype(BF)
 
 
-def call(kernel, out, specs, out_specs=VMEM, scratch=(), limit=LIMIT):
+def call(kernel, out, specs, out_specs=VMEM, scratch=(), limit=LIMIT, aliases=None):
     return pl.pallas_call(
         kernel,
         out_shape=out,
         in_specs=specs,
         out_specs=out_specs,
         scratch_shapes=list(scratch),
+        input_output_aliases=aliases or {},
         compiler_params=pltpu.CompilerParams(vmem_limit_bytes=limit),
     )
 
@@ -282,14 +284,16 @@
         pack_kernel,
         shape(32, CHUNK, HD),
         [ANY] * 5,
-        VMEM,
+        ANY,
         [
             pltpu.VMEM((QROWS, D), BF),
             pltpu.VMEM((HALF, D), BF),
             pltpu.VMEM((HALF, D), BF),
             pltpu.VMEM((1, D), F32),
             pltpu.VMEM((1, D), F32),
+            pltpu.VMEM((32, CHUNK, HD), BF),
             pltpu.SemaphoreType.DMA((5,)),
+            pltpu.SemaphoreType.DMA((NX,)),
         ],
         ALL,
     )(query_input, key_input, value_input, query_gain.reshape(1, -1), key_gain.reshape(1, -1))
@@ -299,7 +303,6 @@
     last = from_either(columns, LAST)
     mine = lax.all_to_all(packed, plane, split_axis=0, concat_axis=0, tiled=True)
     up, down = call(select_kernel, (shape(SENT, HD),) * 2, [SMEM, SMEM, VMEM], (VMEM, VMEM))(lists, zi, mine)
-    joined = call(join_kernel, shape(3 * BLOCK, HD), [VMEM] * 3 + [ANY])(*held, last)
     before, after = from_plane(up, -1), from_plane(down, 1)
     sums, stats = call(
         attend_own_kernel,
@@ -308,12 +311,13 @@
         (VMEM, VMEM),
         [pltpu.VMEM((1024, HD), BF), pltpu.VMEM((1024, HD), BF), pltpu.VMEM((256, HD), BF), pltpu.VMEM((256, HD), BF)],
     )(lists, zi, mine)
+    joined = call(join_kernel, shape(3 * BLOCK, HD), [VMEM] * 3 + [ANY] * 2)(*held, last, stats)
     attended = call(attend_rest_kernel, shape(304, 512), [SMEM, SMEM] + [VMEM] * 5)(
         lists, zi, mine, before, after, sums, stats
     )
     above_w, below_w = from_plane(joined, 1), from_plane(joined, -1)
     below_again, above_again = call(
-        hand_on_kernel, (shape(3 * BLOCK, HD),) * 2, [VMEM, VMEM, ANY], (VMEM, VMEM)
+        hand_on_kernel, (shape(3 * BLOCK, HD),) * 2, [ANY] * 3, (ANY, ANY), aliases={0: 0, 1: 1}
     )(below_w, above_w, attended)
     below2, above2 = from_plane(below_again, -1), from_plane(above_again, 1)
     gathered = [attended] + [
@@ -326,7 +330,7 @@
         [SMEM, SMEM, SMEM] + [VMEM] * 12,
         (VMEM, VMEM, VMEM),
         [pltpu.VMEM((640, 640), BF)],
-    )(ci, zi, xi, *gathered, *held, last, below_w, above_w, below2, above2)
+    )(ci, zi, xi, *gathered, *held, last, below_again, above_again, below2, above2)
     other = lax.ppermute(give, "c", [(0, 1), (1, 0)])
     keep = call(keep_kernel, shape(16, 160, 128), [VMEM, VMEM])(a, keep_w)
     terms = (keep.astype(F32) + other.astype(F32)).astype(BF)

time: 103 us -> 102 us (level)
  no operation moved by 1% of the time
where the time goes in v6:
time: 102 us; the launch traced here: 101 us
  starting transfers between devices  67.3 us (66%)
  blocking collectives  15.7 us (15%)
  Pallas kernels  9.82 us (10%)
  waiting for transfers between devices  7.84 us (8%)
    ppermute x6, starting transfers between devices, from_plane(): return lax.ppermute(value, 'z', [((i + step) % NZ, i) for i in range(NZ)])  23 us
    ppermute x3, starting transfers between devices, from_either(): return lax.ppermute(value, ('z', 'c'), pairs)  20.6 us
    all_to_all x1, blocking collectives, per_device(): lax.all_to_all(terms, ('x', 'y'), split_axis=0, concat_axis=0, tiled=True)  15.7 us
    all_to_all x1, starting transfers between devices, per_device(): lax.all_to_all(packed, plane, split_axis=0, concat_axis=0, tiled=True)  10.6 us
    ppermute x3, starting transfers between devices, per_device(): lax.ppermute(attended, 'x', [((i + step) % NX, i) for i in range(NX)])  8.76 us
    ppermute x6, waiting for transfers between devices, from_plane(): return lax.ppermute(value, 'z', [((i + step) % NZ, i) for i in range(NZ)])  4.34 us
    ppermute x1, starting transfers between devices, per_device(): other = lax.ppermute(give, 'c', [(0, 1), (1, 0)])  4.33 us
    pallas_call x1, Pallas kernels, per_device(): call(pack_kernel, shape(32, CHUNK, HD), [ANY] * 5, ANY, [pltpu.VMEM((QROW...  2.74 us
  transfers between devices with their start and end apart: 14, of which 5 were waited for; matrix products, arithmetic and copies ran while one was open for 0% of the time, Pallas kernels for 5%

profile of v6, /device:TPU:1, one launch (start us, length us, event | category | flops | bytes accessed | tf_op | source)
XLA Modules:
  0.0 101.5 jit_solution(10057457215258870552)
XLA Ops:
  0.0 2.7 %shard_map.73 = bf16[32,192,128]{2,1,0:T(8,128)(2,1)} custom-call(bf16[16,5120]{1,0:T(8,128)(2,1)} %q_hbm.1, bf16[64,5120]{1,0:T(8,128)(2,1)} %k_hbm.1, bf16[64,5120]{1,0:T(8,128)(2,1)} %v_hbm.1, f32[1,5120]{1,0:T(1,128)} %bitcast.15, f32[1,5120]{1,0:T(1,128)} %bitcast.16), custom_call_target="tpu_custom_call" | custom-call | tf_op jit(solution)/shard_map/pallas_call | solution.py:283
  2.8 0.0 copy-start
  2.8 0.0 copy-start.1
  2.8 10.6 %all-to-all-start = ((bf16[32,192,128]{2,1,0:T(8,128)(2,1)}), bf16[32,192,128]{2,1,0:T(8,128)(2,1)S(1)}, u32[]{:S(2)}, u32[]{:S(2)}) async-start(bf16[32,192,128]{2,1,0:T(8,128)(2,1)} %shard_map.73), calls=%async_computation | async-start | bytes 3145728 | tf_op jit(solution)/shard_map/all_to_all | solution.py:304
  13.4 0.0 copy-done
  13.4 0.1 reshape.30
  13.6 10.1 %collective-permute-start.7 = (bf16[400,128]{1,0:T(8,128)(2,1)S(1)}, bf16[400,128]{1,0:T(8,128)(2,1)S(1)}, u32[]{:S(2)}, u32[]{:S(2)}) collective-permute-start(bf16[400,128]{1,0:T(8,128)(2,1)S(1)} %bitcast.9), channel_id=1, source_target_pairs={{416,0},{97,1},{448,32},{129,33},{480,64},{161,65},{0,96},{193,97}... | collective-permute-start | bytes 307208 | tf_op jit(solution)/shard_map/ppermute | solution.py:275
  23.7 5.2 %collective-permute-start.6 = (bf16[400,128]{1,0:T(8,128)(2,1)S(1)}, bf16[400,128]{1,0:T(8,128)(2,1)S(1)}, u32[]{:S(2)}, u32[]{:S(2)}) collective-permute-start(bf16[400,128]{1,0:T(8,128)(2,1)S(1)} %bitcast.10), channel_id=1, source_target_pairs={{320,0},{193,1},{352,32},{225,33},{384,64},{257,65},{416,96},{289,... | collective-permute-start | bytes 307208 | tf_op jit(solution)/shard_map/ppermute | solution.py:275
  28.9 5.4 %collective-permute-start.5 = (bf16[400,128]{1,0:T(8,128)(2,1)S(1)}, bf16[400,128]{1,0:T(8,128)(2,1)S(1)}, u32[]{:S(2)}, u32[]{:S(2)}) collective-permute-start(bf16[400,128]{1,0:T(8,128)(2,1)S(1)} %bitcast.11), channel_id=1, source_target_pairs={{160,0},{353,1},{192,32},{385,33},{224,64},{417,65},{256,96},{449,... | collective-permute-start | bytes 307208 | tf_op jit(solution)/shard_map/ppermute | solution.py:275
  34.3 0.0 copy-done.1
  34.3 0.1 copy.11
  34.4 0.1 reshape.27.lists
  34.5 1.7 %all-to-all-done.r_ref = bf16[32,192,128]{2,1,0:T(8,128)(2,1)S(1)} async-done(((bf16[32,192,128]{2,1,0:T(8,128)(2,1)}), bf16[32,192,128]{2,1,0:T(8,128)(2,1)S(1)}, u32[]{:S(2)}, u32[]{:S(2)}) %all-to-all-start) | async-done | bytes 1572896 | tf_op jit(solution)/shard_map/all_to_all | solution.py:304
  36.2 0.7 shard_map.74
  37.0 1.9 %collective-permute-start = (bf16[1280,128]{1,0:T(8,128)(2,1)S(1)}, bf16[1280,128]{1,0:T(8,128)(2,1)S(1)}, u32[]{:S(2)}, u32[]{:S(2)}) collective-permute-start(bf16[1280,128]{1,0:T(8,128)(2,1)S(1)} %get-tuple-element.17), channel_id=1, source_target_pairs={{480,0},{0,32},{32,64},{64,96},{96,128},{128,160},{160,192},{192,2... | collective-permute-start | bytes 983048 | tf_op jit(solution)/shard_map/ppermute | solution.py:270
  38.9 9.1 %collective-permute-start.1 = (bf16[1280,128]{1,0:T(8,128)(2,1)S(1)}, bf16[1280,128]{1,0:T(8,128)(2,1)S(1)}, u32[]{:S(2)}, u32[]{:S(2)}) collective-permute-start(bf16[1280,128]{1,0:T(8,128)(2,1)S(1)} %get-tuple-element.18), channel_id=1, source_target_pairs={{32,0},{64,32},{96,64},{128,96},{160,128},{192,160},{224,192},{256... | collective-permute-start | bytes 983048 | tf_op jit(solution)/shard_map/ppermute | solution.py:270
  48.0 2.3 %shard_map.75 = (f32[256,512]{1,0:T(8,128)S(1)}, f32[8,512]{1,0:T(8,128)S(1)}) custom-call(s32[512]{0:T(512)S(1)} %reshape.27.lists, s32[1]{0:T(128)} %bitcast.1.zi, bf16[32,192,128]{2,1,0:T(8,128)(2,1)S(1)} %all-to-all-done.r_ref), custom_call_target="tpu_custom_call" | custom-call | tf_op jit(solution)/shard_map/pallas_call | solution.py:307
  50.3 0.0 collective-permute-done.7.refs_3_.last
  50.3 0.0 collective-permute-done.6.refs_2_.down6
  50.3 0.0 collective-permute-done.5.refs_1_.up5
  50.4 3.4 %collective-permute-start.9 = (bf16[1200,128]{1,0:T(8,128)(2,1)S(1)}, bf16[1200,128]{1,0:T(8,128)(2,1)S(1)}, u32[]{:S(2)}, u32[]{:S(2)}) collective-permute-start(bf16[1200,128]{1,0:T(8,128)(2,1)S(1)} %shard_map.77), channel_id=1, source_target_pairs={{32,0},{64,32},{96,64},{128,96},{160,128},{192,160},{224,192},{256... | collective-permute-start | bytes 921608 | tf_op jit(solution)/shard_map/ppermute | solution.py:270
  53.7 1.9 %collective-permute-start.8 = (bf16[1200,128]{1,0:T(8,128)(2,1)S(1)}, bf16[1200,128]{1,0:T(8,128)(2,1)S(1)}, u32[]{:S(2)}, u32[]{:S(2)}) collective-permute-start(bf16[1200,128]{1,0:T(8,128)(2,1)S(1)} %shard_map.77), channel_id=1, source_target_pairs={{480,0},{0,32},{32,64},{64,96},{96,128},{128,160},{160,192},{192,2... | collective-permute-start | bytes 921608 | tf_op jit(solution)/shard_map/ppermute | solution.py:270
  55.7 0.0 collective-permute-done.prev_ref
  55.7 0.0 collective-permute-done.1.next_ref
  55.7 1.2 %shard_map.76.attended.g0 = bf16[304,512]{1,0:T(8,128)(2,1)S(1)} custom-call(s32[512]{0:T(512)S(1)} %reshape.27.lists, s32[1]{0:T(128)} %bitcast.1.zi, bf16[32,192,128]{2,1,0:T(8,128)(2,1)S(1)} %all-to-all-done.r_ref, bf16[1280,128]{1,0:T(8,128)(2,1)S(1)} %collective-permute-done.prev_ref, bf16[1280,128]{1,0:T(8,128)(2,1)S(1)} %collective-permute-done.1.next_ref, ...), custom_call_target="tpu_custom_call" | custom-call | tf_op jit(solution)/shard_map/pallas_call | solution.py:315
  56.8 1.9 %collective-permute-start.4 = (bf16[304,512]{1,0:T(8,128)(2,1)S(1)}, bf16[304,512]{1,0:T(8,128)(2,1)S(1)}, u32[]{:S(2)}, u32[]{:S(2)}) collective-permute-start(bf16[304,512]{1,0:T(8,128)(2,1)S(1)} %shard_map.76.attended.g0), channel_id=1, source_target_pairs={{24,0},{0,8},{8,16},{16,24},{25,1},{1,9},{9,17},{17,25},{26,2},{2,... | collective-permute-start | bytes 933896 | tf_op jit(solution)/shard_map/ppermute | solution.py:324
  58.8 3.6 %collective-permute-start.3 = (bf16[304,512]{1,0:T(8,128)(2,1)S(1)}, bf16[304,512]{1,0:T(8,128)(2,1)S(1)}, u32[]{:S(2)}, u32[]{:S(2)}) collective-permute-start(bf16[304,512]{1,0:T(8,128)(2,1)S(1)} %shard_map.76.attended.g0), channel_id=1, source_target_pairs={{16,0},{24,8},{0,16},{8,24},{17,1},{25,9},{1,17},{9,25},{18,2},{26... | collective-permute-start | bytes 933896 | tf_op jit(solution)/shard_map/ppermute | solution.py:324
  62.4 3.2 %collective-permute-start.2 = (bf16[304,512]{1,0:T(8,128)(2,1)S(1)}, bf16[304,512]{1,0:T(8,128)(2,1)S(1)}, u32[]{:S(2)}, u32[]{:S(2)}) collective-permute-start(bf16[304,512]{1,0:T(8,128)(2,1)S(1)} %shard_map.76.attended.g0), channel_id=1, source_target_pairs={{8,0},{16,8},{24,16},{0,24},{9,1},{17,9},{25,17},{1,25},{10,2},{18... | collective-permute-start | bytes 933896 | tf_op jit(solution)/shard_map/ppermute | solution.py:324
  65.6 0.0 collective-permute-done.9.above_w
  65.6 0.0 collective-permute-done.8.below_w
  65.7 1.9 %collective-permute-start.10 = (bf16[1200,128]{1,0:T(8,128)(2,1)S(1)}, bf16[1200,128]{1,0:T(8,128)(2,1)S(1)}, u32[]{:S(2)}, u32[]{:S(2)}) collective-permute-start(bf16[1200,128]{1,0:T(8,128)(2,1)S(1)} %get-tuple-element.22.before), channel_id=1, source_target_pairs={{480,0},{0,32},{32,64},{64,96},{96,128},{128,160},{160,192},{192,2... | collective-permute-start | bytes 921608 | tf_op jit(solution)/shard_map/ppermute | solution.py:270
  67.6 4.7 %collective-permute-start.11 = (bf16[1200,128]{1,0:T(8,128)(2,1)S(1)}, bf16[1200,128]{1,0:T(8,128)(2,1)S(1)}, u32[]{:S(2)}, u32[]{:S(2)}) collective-permute-start(bf16[1200,128]{1,0:T(8,128)(2,1)S(1)} %get-tuple-element.23.after), channel_id=1, source_target_pairs={{32,0},{64,32},{96,64},{128,96},{160,128},{192,160},{224,192},{256... | collective-permute-start | bytes 921608 | tf_op jit(solution)/shard_map/ppermute | solution.py:270
  72.3 3.4 %collective-permute-done.10.before2 = bf16[1200,128]{1,0:T(8,128)(2,1)S(1)} collective-permute-done((bf16[1200,128]{1,0:T(8,128)(2,1)S(1)}, bf16[1200,128]{1,0:T(8,128)(2,1)S(1)}, u32[]{:S(2)}, u32[]{:S(2)}) %collective-permute-start.10) | collective-permute-done | bytes 307232 | tf_op jit(solution)/shard_map/ppermute | solution.py:270
  75.7 0.9 collective-permute-done.11.after2
  76.6 0.0 collective-permute-done.4.g3
  76.6 0.0 collective-permute-done.3.g2
  76.6 0.7 collective-permute-done.2.g1
  77.4 1.4 %shard_map.79 = (bf16[16,160,128]{2,1,0:T(8,128)(2,1)S(1)}, bf16[640,512]{1,0:T(8,128)(2,1)S(1)}, bf16[640,640]{1,0:T(8,128)(2,1)S(1)}) custom-call(s32[1]{0:T(128)} %bitcast.ci, s32[1]{0:T(128)} %bitcast.1.zi, s32[1]{0:T(128)} %bitcast.2.xi, bf16[304,512]{1,0:T(8,128)(2,1)S(1)} %shard_map.76.attended.g0, bf16[304,512]{1,0:T(8,128)(2,1)S(1)} %collective-permute-done.2.g1, ...), custom_call_target="tpu_custom_call" | custom-call | tf_op jit(solution)/shard_map/pallas_call | solution.py:327
  78.7 4.3 %collective-permute-start.12 = (bf16[16,160,128]{2,1,0:T(8,128)(2,1)S(1)}, bf16[16,160,128]{2,1,0:T(8,128)(2,1)S(1)}, u32[]{:S(2)}, u32[]{:S(2)}) collective-permute-start(bf16[16,160,128]{2,1,0:T(8,128)(2,1)S(1)} %get-tuple-element.26), channel_id=1, source_target_pairs={{0,1},{1,0},{2,3},{3,2},{4,5},{5,4},{6,7},{7,6},{8,9},{9,8},{10,11... | collective-permute-start | bytes 1966088 | tf_op jit(solution)/shard_map/ppermute | solution.py:334
  83.1 0.7 shard_map.80
  83.8 1.0 collective-permute-done.12
  84.8 0.2 add_convert_fusion
  85.0 15.7 %all_to_all.10.r_ref = bf16[16,160,128]{2,1,0:T(8,128)(2,1)S(1)} all-to-all(bf16[16,160,128]{2,1,0:T(8,128)(2,1)S(1)} %add_convert_fusion), channel_id=1, replica_groups=mesh['z'=16,'x'=4,'y'=4,'c'=2] {'x','y'}, dimensions={0} | all-to-all | bytes 1310720 | tf_op jit(solution)/shard_map/all_to_all | solution.py:337
  100.7 0.8 shard_map.81
  (3 shorter events, 0.0 us)
Async XLA Ops:
  2.8 10.7 %copy-start = (bf16[640,80]{0,1:T(8,128)(2,1)S(1)}, bf16[640,80]{0,1:T(8,128)(2,1)}, u32[]{:S(2)}) copy-start(bf16[640,80]{0,1:T(8,128)(2,1)} %param.13) | copy-start | bytes 307204
  2.8 31.5 %copy-start.1 = (s32[64,8]{0,1:T(8,128)S(1)}, s32[64,8]{0,1:T(8,128)}, u32[]{:S(2)}) copy-start(s32[64,8]{0,1:T(8,128)} %param.12) | copy-start | bytes 6148
  2.8 33.4 %all-to-all-start = ((bf16[32,192,128]{2,1,0:T(8,128)(2,1)}), bf16[32,192,128]{2,1,0:T(8,128)(2,1)S(1)}, u32[]{:S(2)}, u32[]{:S(2)}) async-start(bf16[32,192,128]{2,1,0:T(8,128)(2,1)} %shard_map.73), calls=%async_computation | async-start | bytes 3145728 | tf_op jit(solution)/shard_map/all_to_all | solution.py:304
  13.6 36.7 %collective-permute-start.7 = (bf16[400,128]{1,0:T(8,128)(2,1)S(1)}, bf16[400,128]{1,0:T(8,128)(2,1)S(1)}, u32[]{:S(2)}, u32[]{:S(2)}) collective-permute-start(bf16[400,128]{1,0:T(8,128)(2,1)S(1)} %bitcast.9), channel_id=1, source_target_pairs={{416,0},{97,1},{448,32},{129,33},{480,64},{161,65},{0,96},{193,97}... | collective-permute-start | bytes 307208 | tf_op jit(solution)/shard_map/ppermute | solution.py:275
  23.7 26.6 %collective-permute-start.6 = (bf16[400,128]{1,0:T(8,128)(2,1)S(1)}, bf16[400,128]{1,0:T(8,128)(2,1)S(1)}, u32[]{:S(2)}, u32[]{:S(2)}) collective-permute-start(bf16[400,128]{1,0:T(8,128)(2,1)S(1)} %bitcast.10), channel_id=1, source_target_pairs={{320,0},{193,1},{352,32},{225,33},{384,64},{257,65},{416,96},{289,... | collective-permute-start | bytes 307208 | tf_op jit(solution)/shard_map/ppermute | solution.py:275
  28.9 21.4 %collective-permute-start.5 = (bf16[400,128]{1,0:T(8,128)(2,1)S(1)}, bf16[400,128]{1,0:T(8,128)(2,1)S(1)}, u32[]{:S(2)}, u32[]{:S(2)}) collective-permute-start(bf16[400,128]{1,0:T(8,128)(2,1)S(1)} %bitcast.11), channel_id=1, source_target_pairs={{160,0},{353,1},{192,32},{385,33},{224,64},{417,65},{256,96},{449,... | collective-permute-start | bytes 307208 | tf_op jit(solution)/shard_map/ppermute | solution.py:275
  37.0 18.7 %collective-permute-start = (bf16[1280,128]{1,0:T(8,128)(2,1)S(1)}, bf16[1280,128]{1,0:T(8,128)(2,1)S(1)}, u32[]{:S(2)}, u32[]{:S(2)}) collective-permute-start(bf16[1280,128]{1,0:T(8,128)(2,1)S(1)} %get-tuple-element.17), channel_id=1, source_target_pairs={{480,0},{0,32},{32,64},{64,96},{96,128},{128,160},{160,192},{192,2... | collective-permute-start | bytes 983048 | tf_op jit(solution)/shard_map/ppermute | solution.py:270
  38.9 16.8 %collective-permute-start.1 = (bf16[1280,128]{1,0:T(8,128)(2,1)S(1)}, bf16[1280,128]{1,0:T(8,128)(2,1)S(1)}, u32[]{:S(2)}, u32[]{:S(2)}) collective-permute-start(bf16[1280,128]{1,0:T(8,128)(2,1)S(1)} %get-tuple-element.18), channel_id=1, source_target_pairs={{32,0},{64,32},{96,64},{128,96},{160,128},{192,160},{224,192},{256... | collective-permute-start | bytes 983048 | tf_op jit(solution)/shard_map/ppermute | solution.py:270
  50.4 15.3 %collective-permute-start.9 = (bf16[1200,128]{1,0:T(8,128)(2,1)S(1)}, bf16[1200,128]{1,0:T(8,128)(2,1)S(1)}, u32[]{:S(2)}, u32[]{:S(2)}) collective-permute-start(bf16[1200,128]{1,0:T(8,128)(2,1)S(1)} %shard_map.77), channel_id=1, source_target_pairs={{32,0},{64,32},{96,64},{128,96},{160,128},{192,160},{224,192},{256... | collective-permute-start | bytes 921608 | tf_op jit(solution)/shard_map/ppermute | solution.py:270
  53.7 11.9 %collective-permute-start.8 = (bf16[1200,128]{1,0:T(8,128)(2,1)S(1)}, bf16[1200,128]{1,0:T(8,128)(2,1)S(1)}, u32[]{:S(2)}, u32[]{:S(2)}) collective-permute-start(bf16[1200,128]{1,0:T(8,128)(2,1)S(1)} %shard_map.77), channel_id=1, source_target_pairs={{480,0},{0,32},{32,64},{64,96},{96,128},{128,160},{160,192},{192,2... | collective-permute-start | bytes 921608 | tf_op jit(solution)/shard_map/ppermute | solution.py:270
  56.8 19.8 %collective-permute-start.4 = (bf16[304,512]{1,0:T(8,128)(2,1)S(1)}, bf16[304,512]{1,0:T(8,128)(2,1)S(1)}, u32[]{:S(2)}, u32[]{:S(2)}) collective-permute-start(bf16[304,512]{1,0:T(8,128)(2,1)S(1)} %shard_map.76.attended.g0), channel_id=1, source_target_pairs={{24,0},{0,8},{8,16},{16,24},{25,1},{1,9},{9,17},{17,25},{26,2},{2,... | collective-permute-start | bytes 933896 | tf_op jit(solution)/shard_map/ppermute | solution.py:324
  58.8 17.9 %collective-permute-start.3 = (bf16[304,512]{1,0:T(8,128)(2,1)S(1)}, bf16[304,512]{1,0:T(8,128)(2,1)S(1)}, u32[]{:S(2)}, u32[]{:S(2)}) collective-permute-start(bf16[304,512]{1,0:T(8,128)(2,1)S(1)} %shard_map.76.attended.g0), channel_id=1, source_target_pairs={{16,0},{24,8},{0,16},{8,24},{17,1},{25,9},{1,17},{9,25},{18,2},{26... | collective-permute-start | bytes 933896 | tf_op jit(solution)/shard_map/ppermute | solution.py:324
  62.4 15.0 %collective-permute-start.2 = (bf16[304,512]{1,0:T(8,128)(2,1)S(1)}, bf16[304,512]{1,0:T(8,128)(2,1)S(1)}, u32[]{:S(2)}, u32[]{:S(2)}) collective-permute-start(bf16[304,512]{1,0:T(8,128)(2,1)S(1)} %shard_map.76.attended.g0), channel_id=1, source_target_pairs={{8,0},{16,8},{24,16},{0,24},{9,1},{17,9},{25,17},{1,25},{10,2},{18... | collective-permute-start | bytes 933896 | tf_op jit(solution)/shard_map/ppermute | solution.py:324
  65.7 10.1 %collective-permute-start.10 = (bf16[1200,128]{1,0:T(8,128)(2,1)S(1)}, bf16[1200,128]{1,0:T(8,128)(2,1)S(1)}, u32[]{:S(2)}, u32[]{:S(2)}) collective-permute-start(bf16[1200,128]{1,0:T(8,128)(2,1)S(1)} %get-tuple-element.22.before), channel_id=1, source_target_pairs={{480,0},{0,32},{32,64},{64,96},{96,128},{128,160},{160,192},{192,2... | collective-permute-start | bytes 921608 | tf_op jit(solution)/shard_map/ppermute | solution.py:270
  67.6 9.0 %collective-permute-start.11 = (bf16[1200,128]{1,0:T(8,128)(2,1)S(1)}, bf16[1200,128]{1,0:T(8,128)(2,1)S(1)}, u32[]{:S(2)}, u32[]{:S(2)}) collective-permute-start(bf16[1200,128]{1,0:T(8,128)(2,1)S(1)} %get-tuple-element.23.after), channel_id=1, source_target_pairs={{32,0},{64,32},{96,64},{128,96},{160,128},{192,160},{224,192},{256... | collective-permute-start | bytes 921608 | tf_op jit(solution)/shard_map/ppermute | solution.py:270
  78.7 6.0 %collective-permute-start.12 = (bf16[16,160,128]{2,1,0:T(8,128)(2,1)S(1)}, bf16[16,160,128]{2,1,0:T(8,128)(2,1)S(1)}, u32[]{:S(2)}, u32[]{:S(2)}) collective-permute-start(bf16[16,160,128]{2,1,0:T(8,128)(2,1)S(1)} %get-tuple-element.26), channel_id=1, source_target_pairs={{0,1},{1,0},{2,3},{3,2},{4,5},{5,4},{6,7},{7,6},{8,9},{9,8},{10,11... | collective-permute-start | bytes 1966088 | tf_op jit(solution)/shard_map/ppermute | solution.py:334

commit v7 on v6

--- a/solution.py
+++ b/solution.py
@@ -303,7 +303,8 @@
     last = from_either(columns, LAST)
     mine = lax.all_to_all(packed, plane, split_axis=0, concat_axis=0, tiled=True)
     up, down = call(select_kernel, (shape(SENT, HD),) * 2, [SMEM, SMEM, VMEM], (VMEM, VMEM))(lists, zi, mine)
-    before, after = from_plane(up, -1), from_plane(down, 1)
+    before = lax.ppermute(up, "z", [(i, i + 1) for i in range(NZ - 1)])
+    after = lax.ppermute(down, "z", [(i + 1, i) for i in range(NZ - 1)])
     sums, stats = call(
         attend_own_kernel,
         (jax.ShapeDtypeStruct((256, 512), F32), jax.ShapeDtypeStruct((8, 512), F32)),

time: 102 us -> 102 us (level)
  starting transfers between devices: 67.3 us -> 65.4 us
  waiting for transfers between devices: 7.84 us -> 9.64 us
    ppermute x6 -> x4, starting transfers between devices: 23 us -> 18.3 us  [from_plane(): return lax.ppermute(value, 'z', [((i + step) % NZ, i) for i in range(NZ)])]
    ppermute x0 -> x2, starting transfers between devices: none -> 2.85 us  [the longest x1 1.56 us: per_device(): before = lax.ppermute(up, 'z', [(i, i + 1) for i in range(NZ - 1)])]
    ppermute x3, waiting for transfers between devices: 0.01 us -> 1.67 us  [from_either(): return lax.ppermute(value, ('z', 'c'), pairs)]
    ppermute x6 -> x4, waiting for transfers between devices: 4.34 us -> 4.52 us  [from_plane(): return lax.ppermute(value, 'z', [((i + step) % NZ, i) for i in range(NZ)])]
  transfers between devices with their start and end apart: 14 -> 14, of which waited for: 5 -> 6; matrix products, arithmetic and copies ran while one was open for 0% -> 0% of each run, Pallas kernels for 5% -> 5%
where the time goes in v7:
time: 102 us; the launch traced here: 101 us
  starting transfers between devices  65.4 us (64%)
  blocking collectives  15.8 us (15%)
  Pallas kernels  9.82 us (10%)
  waiting for transfers between devices  9.64 us (9%)
    ppermute x3, starting transfers between devices, from_either(): return lax.ppermute(value, ('z', 'c'), pairs)  20.6 us
    ppermute x4, starting transfers between devices, from_plane(): return lax.ppermute(value, 'z', [((i + step) % NZ, i) for i in range(NZ)])  18.3 us
    all_to_all x1, blocking collectives, per_device(): lax.all_to_all(terms, ('x', 'y'), split_axis=0, concat_axis=0, tiled=True)  15.8 us
    all_to_all x1, starting transfers between devices, per_device(): lax.all_to_all(packed, plane, split_axis=0, concat_axis=0, tiled=True)  10.6 us
    ppermute x3, starting transfers between devices, per_device(): lax.ppermute(attended, 'x', [((i + step) % NX, i) for i in range(NX)])  8.76 us
    ppermute x4, waiting for transfers between devices, from_plane(): return lax.ppermute(value, 'z', [((i + step) % NZ, i) for i in range(NZ)])  4.52 us
    ppermute x1, starting transfers between devices, per_device(): other = lax.ppermute(give, 'c', [(0, 1), (1, 0)])  4.21 us
    pallas_call x1, Pallas kernels, per_device(): call(pack_kernel, shape(32, CHUNK, HD), [ANY] * 5, ANY, [pltpu.VMEM((QROW...  2.74 us
  transfers between devices with their start and end apart: 14, of which 6 were waited for; matrix products, arithmetic and copies ran while one was open for 0% of the time, Pallas kernels for 5%

profile of v7, /device:TPU:1, one launch (start us, length us, event | category | flops | bytes accessed | tf_op | source)
XLA Modules:
  0.0 101.5 jit_solution(8571647141438204684)
XLA Ops:
  0.0 2.7 %shard_map.73 = bf16[32,192,128]{2,1,0:T(8,128)(2,1)} custom-call(bf16[16,5120]{1,0:T(8,128)(2,1)} %q_hbm.1, bf16[64,5120]{1,0:T(8,128)(2,1)} %k_hbm.1, bf16[64,5120]{1,0:T(8,128)(2,1)} %v_hbm.1, f32[1,5120]{1,0:T(1,128)} %bitcast.15, f32[1,5120]{1,0:T(1,128)} %bitcast.16), custom_call_target="tpu_custom_call" | custom-call | tf_op jit(solution)/shard_map/pallas_call | solution.py:283
  2.8 0.0 copy-start
  2.8 0.0 copy-start.1
  2.8 10.6 %all-to-all-start = ((bf16[32,192,128]{2,1,0:T(8,128)(2,1)}), bf16[32,192,128]{2,1,0:T(8,128)(2,1)S(1)}, u32[]{:S(2)}, u32[]{:S(2)}) async-start(bf16[32,192,128]{2,1,0:T(8,128)(2,1)} %shard_map.73), calls=%async_computation | async-start | bytes 3145728 | tf_op jit(solution)/shard_map/all_to_all | solution.py:304
  13.4 0.0 copy-done
  13.4 0.1 reshape.30
  13.6 10.1 %collective-permute-start.7 = (bf16[400,128]{1,0:T(8,128)(2,1)S(1)}, bf16[400,128]{1,0:T(8,128)(2,1)S(1)}, u32[]{:S(2)}, u32[]{:S(2)}) collective-permute-start(bf16[400,128]{1,0:T(8,128)(2,1)S(1)} %bitcast.9), channel_id=1, source_target_pairs={{416,0},{97,1},{448,32},{129,33},{480,64},{161,65},{0,96},{193,97}... | collective-permute-start | bytes 307208 | tf_op jit(solution)/shard_map/ppermute | solution.py:275
  23.7 5.2 %collective-permute-start.6 = (bf16[400,128]{1,0:T(8,128)(2,1)S(1)}, bf16[400,128]{1,0:T(8,128)(2,1)S(1)}, u32[]{:S(2)}, u32[]{:S(2)}) collective-permute-start(bf16[400,128]{1,0:T(8,128)(2,1)S(1)} %bitcast.10), channel_id=1, source_target_pairs={{320,0},{193,1},{352,32},{225,33},{384,64},{257,65},{416,96},{289,... | collective-permute-start | bytes 307208 | tf_op jit(solution)/shard_map/ppermute | solution.py:275
  28.9 5.4 %collective-permute-start.5 = (bf16[400,128]{1,0:T(8,128)(2,1)S(1)}, bf16[400,128]{1,0:T(8,128)(2,1)S(1)}, u32[]{:S(2)}, u32[]{:S(2)}) collective-permute-start(bf16[400,128]{1,0:T(8,128)(2,1)S(1)} %bitcast.11), channel_id=1, source_target_pairs={{160,0},{353,1},{192,32},{385,33},{224,64},{417,65},{256,96},{449,... | collective-permute-start | bytes 307208 | tf_op jit(solution)/shard_map/ppermute | solution.py:275
  34.3 0.0 copy-done.1
  34.3 0.1 copy.11
  34.4 0.1 reshape.27.lists
  34.5 1.7 %all-to-all-done.r_ref = bf16[32,192,128]{2,1,0:T(8,128)(2,1)S(1)} async-done(((bf16[32,192,128]{2,1,0:T(8,128)(2,1)}), bf16[32,192,128]{2,1,0:T(8,128)(2,1)S(1)}, u32[]{:S(2)}, u32[]{:S(2)}) %all-to-all-start) | async-done | bytes 1572896 | tf_op jit(solution)/shard_map/all_to_all | solution.py:304
  36.2 0.7 shard_map.74
  37.0 1.6 %collective-permute-start = (bf16[1280,128]{1,0:T(8,128)(2,1)S(1)}, bf16[1280,128]{1,0:T(8,128)(2,1)S(1)}, u32[]{:S(2)}, u32[]{:S(2)}) collective-permute-start(bf16[1280,128]{1,0:T(8,128)(2,1)S(1)} %get-tuple-element.17), channel_id=1, source_target_pairs={{0,32},{32,64},{64,96},{96,128},{128,160},{160,192},{192,224},{224... | collective-permute-start | bytes 983048 | tf_op jit(solution)/shard_map/ppermute | solution.py:306
  38.5 1.3 %collective-permute-start.1 = (bf16[1280,128]{1,0:T(8,128)(2,1)S(1)}, bf16[1280,128]{1,0:T(8,128)(2,1)S(1)}, u32[]{:S(2)}, u32[]{:S(2)}) collective-permute-start(bf16[1280,128]{1,0:T(8,128)(2,1)S(1)} %get-tuple-element.18), channel_id=1, source_target_pairs={{32,0},{64,32},{96,64},{128,96},{160,128},{192,160},{224,192},{256... | collective-permute-start | bytes 983048 | tf_op jit(solution)/shard_map/ppermute | solution.py:307
  39.8 2.3 %shard_map.75 = (f32[256,512]{1,0:T(8,128)S(1)}, f32[8,512]{1,0:T(8,128)S(1)}) custom-call(s32[512]{0:T(512)S(1)} %reshape.27.lists, s32[1]{0:T(128)} %bitcast.1.zi, bf16[32,192,128]{2,1,0:T(8,128)(2,1)S(1)} %all-to-all-done.r_ref), custom_call_target="tpu_custom_call" | custom-call | tf_op jit(solution)/shard_map/pallas_call | solution.py:308
  42.1 0.0 collective-permute-done.7.refs_3_.last
  42.1 0.0 collective-permute-done.6.refs_2_.down6
  42.1 1.7 %collective-permute-done.5.refs_1_.up5 = bf16[400,128]{1,0:T(8,128)(2,1)S(1)} collective-permute-done((bf16[400,128]{1,0:T(8,128)(2,1)S(1)}, bf16[400,128]{1,0:T(8,128)(2,1)S(1)}, u32[]{:S(2)}, u32[]{:S(2)}) %collective-permute-start.5) | collective-permute-done | bytes 102432 | tf_op jit(solution)/shard_map/ppermute | solution.py:275
  43.8 9.9 %collective-permute-start.9 = (bf16[1200,128]{1,0:T(8,128)(2,1)S(1)}, bf16[1200,128]{1,0:T(8,128)(2,1)S(1)}, u32[]{:S(2)}, u32[]{:S(2)}) collective-permute-start(bf16[1200,128]{1,0:T(8,128)(2,1)S(1)} %shard_map.77), channel_id=1, source_target_pairs={{32,0},{64,32},{96,64},{128,96},{160,128},{192,160},{224,192},{256... | collective-permute-start | bytes 921608 | tf_op jit(solution)/shard_map/ppermute | solution.py:270
  53.8 1.9 %collective-permute-start.8 = (bf16[1200,128]{1,0:T(8,128)(2,1)S(1)}, bf16[1200,128]{1,0:T(8,128)(2,1)S(1)}, u32[]{:S(2)}, u32[]{:S(2)}) collective-permute-start(bf16[1200,128]{1,0:T(8,128)(2,1)S(1)} %shard_map.77), channel_id=1, source_target_pairs={{480,0},{0,32},{32,64},{64,96},{96,128},{128,160},{160,192},{192,2... | collective-permute-start | bytes 921608 | tf_op jit(solution)/shard_map/ppermute | solution.py:270
  55.7 0.0 collective-permute-done.prev_ref
  55.7 0.0 collective-permute-done.1.next_ref
  55.7 1.2 %shard_map.76.attended.g0 = bf16[304,512]{1,0:T(8,128)(2,1)S(1)} custom-call(s32[512]{0:T(512)S(1)} %reshape.27.lists, s32[1]{0:T(128)} %bitcast.1.zi, bf16[32,192,128]{2,1,0:T(8,128)(2,1)S(1)} %all-to-all-done.r_ref, bf16[1280,128]{1,0:T(8,128)(2,1)S(1)} %collective-permute-done.prev_ref, bf16[1280,128]{1,0:T(8,128)(2,1)S(1)} %collective-permute-done.1.next_ref, ...), custom_call_target="tpu_custom_call" | custom-call | tf_op jit(solution)/shard_map/pallas_call | solution.py:316
  56.9 1.9 %collective-permute-start.4 = (bf16[304,512]{1,0:T(8,128)(2,1)S(1)}, bf16[304,512]{1,0:T(8,128)(2,1)S(1)}, u32[]{:S(2)}, u32[]{:S(2)}) collective-permute-start(bf16[304,512]{1,0:T(8,128)(2,1)S(1)} %shard_map.76.attended.g0), channel_id=1, source_target_pairs={{24,0},{0,8},{8,16},{16,24},{25,1},{1,9},{9,17},{17,25},{26,2},{2,... | collective-permute-start | bytes 933896 | tf_op jit(solution)/shard_map/ppermute | solution.py:325
  58.8 3.6 %collective-permute-start.3 = (bf16[304,512]{1,0:T(8,128)(2,1)S(1)}, bf16[304,512]{1,0:T(8,128)(2,1)S(1)}, u32[]{:S(2)}, u32[]{:S(2)}) collective-permute-start(bf16[304,512]{1,0:T(8,128)(2,1)S(1)} %shard_map.76.attended.g0), channel_id=1, source_target_pairs={{16,0},{24,8},{0,16},{8,24},{17,1},{25,9},{1,17},{9,25},{18,2},{26... | collective-permute-start | bytes 933896 | tf_op jit(solution)/shard_map/ppermute | solution.py:325
  62.4 3.2 %collective-permute-start.2 = (bf16[304,512]{1,0:T(8,128)(2,1)S(1)}, bf16[304,512]{1,0:T(8,128)(2,1)S(1)}, u32[]{:S(2)}, u32[]{:S(2)}) collective-permute-start(bf16[304,512]{1,0:T(8,128)(2,1)S(1)} %shard_map.76.attended.g0), channel_id=1, source_target_pairs={{8,0},{16,8},{24,16},{0,24},{9,1},{17,9},{25,17},{1,25},{10,2},{18... | collective-permute-start | bytes 933896 | tf_op jit(solution)/shard_map/ppermute | solution.py:325
  65.6 0.0 collective-permute-done.9.above_w
  65.6 0.0 collective-permute-done.8.below_w
  65.7 1.9 %collective-permute-start.10 = (bf16[1200,128]{1,0:T(8,128)(2,1)S(1)}, bf16[1200,128]{1,0:T(8,128)(2,1)S(1)}, u32[]{:S(2)}, u32[]{:S(2)}) collective-permute-start(bf16[1200,128]{1,0:T(8,128)(2,1)S(1)} %get-tuple-element.22.before), channel_id=1, source_target_pairs={{480,0},{0,32},{32,64},{64,96},{96,128},{128,160},{160,192},{192,2... | collective-permute-start | bytes 921608 | tf_op jit(solution)/shard_map/ppermute | solution.py:270
  67.6 4.6 %collective-permute-start.11 = (bf16[1200,128]{1,0:T(8,128)(2,1)S(1)}, bf16[1200,128]{1,0:T(8,128)(2,1)S(1)}, u32[]{:S(2)}, u32[]{:S(2)}) collective-permute-start(bf16[1200,128]{1,0:T(8,128)(2,1)S(1)} %get-tuple-element.23.after), channel_id=1, source_target_pairs={{32,0},{64,32},{96,64},{128,96},{160,128},{192,160},{224,192},{256... | collective-permute-start | bytes 921608 | tf_op jit(solution)/shard_map/ppermute | solution.py:270
  72.2 3.6 %collective-permute-done.10.before2 = bf16[1200,128]{1,0:T(8,128)(2,1)S(1)} collective-permute-done((bf16[1200,128]{1,0:T(8,128)(2,1)S(1)}, bf16[1200,128]{1,0:T(8,128)(2,1)S(1)}, u32[]{:S(2)}, u32[]{:S(2)}) %collective-permute-start.10) | collective-permute-done | bytes 307232 | tf_op jit(solution)/shard_map/ppermute | solution.py:270
  75.8 0.9 collective-permute-done.11.after2
  76.7 0.0 collective-permute-done.4.g3
  76.7 0.0 collective-permute-done.3.g2
  76.7 0.7 collective-permute-done.2.g1
  77.4 1.4 %shard_map.79 = (bf16[16,160,128]{2,1,0:T(8,128)(2,1)S(1)}, bf16[640,512]{1,0:T(8,128)(2,1)S(1)}, bf16[640,640]{1,0:T(8,128)(2,1)S(1)}) custom-call(s32[1]{0:T(128)} %bitcast.ci, s32[1]{0:T(128)} %bitcast.1.zi, s32[1]{0:T(128)} %bitcast.2.xi, bf16[304,512]{1,0:T(8,128)(2,1)S(1)} %shard_map.76.attended.g0, bf16[304,512]{1,0:T(8,128)(2,1)S(1)} %collective-permute-done.2.g1, ...), custom_call_target="tpu_custom_call" | custom-call | tf_op jit(solution)/shard_map/pallas_call | solution.py:328
  78.8 4.2 %collective-permute-start.12 = (bf16[16,160,128]{2,1,0:T(8,128)(2,1)S(1)}, bf16[16,160,128]{2,1,0:T(8,128)(2,1)S(1)}, u32[]{:S(2)}, u32[]{:S(2)}) collective-permute-start(bf16[16,160,128]{2,1,0:T(8,128)(2,1)S(1)} %get-tuple-element.26), channel_id=1, source_target_pairs={{0,1},{1,0},{2,3},{3,2},{4,5},{5,4},{6,7},{7,6},{8,9},{9,8},{10,11... | collective-permute-start | bytes 1966088 | tf_op jit(solution)/shard_map/ppermute | solution.py:335
  83.0 0.7 shard_map.80
  83.7 1.0 collective-permute-done.12
  84.7 0.2 add_convert_fusion
  84.9 15.8 %all_to_all.10.r_ref = bf16[16,160,128]{2,1,0:T(8,128)(2,1)S(1)} all-to-all(bf16[16,160,128]{2,1,0:T(8,128)(2,1)S(1)} %add_convert_fusion), channel_id=1, replica_groups=mesh['z'=16,'x'=4,'y'=4,'c'=2] {'x','y'}, dimensions={0} | all-to-all | bytes 1310720 | tf_op jit(solution)/shard_map/all_to_all | solution.py:338
  100.7 0.8 shard_map.81
  (3 shorter events, 0.0 us)
Async XLA Ops:
  2.8 10.7 %copy-start = (bf16[640,80]{0,1:T(8,128)(2,1)S(1)}, bf16[640,80]{0,1:T(8,128)(2,1)}, u32[]{:S(2)}) copy-start(bf16[640,80]{0,1:T(8,128)(2,1)} %param.13) | copy-start | bytes 307204
  2.8 31.5 %copy-start.1 = (s32[64,8]{0,1:T(8,128)S(1)}, s32[64,8]{0,1:T(8,128)}, u32[]{:S(2)}) copy-start(s32[64,8]{0,1:T(8,128)} %param.12) | copy-start | bytes 6148
  2.8 33.4 %all-to-all-start = ((bf16[32,192,128]{2,1,0:T(8,128)(2,1)}), bf16[32,192,128]{2,1,0:T(8,128)(2,1)S(1)}, u32[]{:S(2)}, u32[]{:S(2)}) async-start(bf16[32,192,128]{2,1,0:T(8,128)(2,1)} %shard_map.73), calls=%async_computation | async-start | bytes 3145728 | tf_op jit(solution)/shard_map/all_to_all | solution.py:304
  13.6 28.5 %collective-permute-start.7 = (bf16[400,128]{1,0:T(8,128)(2,1)S(1)}, bf16[400,128]{1,0:T(8,128)(2,1)S(1)}, u32[]{:S(2)}, u32[]{:S(2)}) collective-permute-start(bf16[400,128]{1,0:T(8,128)(2,1)S(1)} %bitcast.9), channel_id=1, source_target_pairs={{416,0},{97,1},{448,32},{129,33},{480,64},{161,65},{0,96},{193,97}... | collective-permute-start | bytes 307208 | tf_op jit(solution)/shard_map/ppermute | solution.py:275
  23.7 18.4 %collective-permute-start.6 = (bf16[400,128]{1,0:T(8,128)(2,1)S(1)}, bf16[400,128]{1,0:T(8,128)(2,1)S(1)}, u32[]{:S(2)}, u32[]{:S(2)}) collective-permute-start(bf16[400,128]{1,0:T(8,128)(2,1)S(1)} %bitcast.10), channel_id=1, source_target_pairs={{320,0},{193,1},{352,32},{225,33},{384,64},{257,65},{416,96},{289,... | collective-permute-start | bytes 307208 | tf_op jit(solution)/shard_map/ppermute | solution.py:275
  28.9 14.9 %collective-permute-start.5 = (bf16[400,128]{1,0:T(8,128)(2,1)S(1)}, bf16[400,128]{1,0:T(8,128)(2,1)S(1)}, u32[]{:S(2)}, u32[]{:S(2)}) collective-permute-start(bf16[400,128]{1,0:T(8,128)(2,1)S(1)} %bitcast.11), channel_id=1, source_target_pairs={{160,0},{353,1},{192,32},{385,33},{224,64},{417,65},{256,96},{449,... | collective-permute-start | bytes 307208 | tf_op jit(solution)/shard_map/ppermute | solution.py:275
  37.0 18.7 %collective-permute-start = (bf16[1280,128]{1,0:T(8,128)(2,1)S(1)}, bf16[1280,128]{1,0:T(8,128)(2,1)S(1)}, u32[]{:S(2)}, u32[]{:S(2)}) collective-permute-start(bf16[1280,128]{1,0:T(8,128)(2,1)S(1)} %get-tuple-element.17), channel_id=1, source_target_pairs={{0,32},{32,64},{64,96},{96,128},{128,160},{160,192},{192,224},{224... | collective-permute-start | bytes 983048 | tf_op jit(solution)/shard_map/ppermute | solution.py:306
  38.5 17.2 %collective-permute-start.1 = (bf16[1280,128]{1,0:T(8,128)(2,1)S(1)}, bf16[1280,128]{1,0:T(8,128)(2,1)S(1)}, u32[]{:S(2)}, u32[]{:S(2)}) collective-permute-start(bf16[1280,128]{1,0:T(8,128)(2,1)S(1)} %get-tuple-element.18), channel_id=1, source_target_pairs={{32,0},{64,32},{96,64},{128,96},{160,128},{192,160},{224,192},{256... | collective-permute-start | bytes 983048 | tf_op jit(solution)/shard_map/ppermute | solution.py:307
  43.8 21.8 %collective-permute-start.9 = (bf16[1200,128]{1,0:T(8,128)(2,1)S(1)}, bf16[1200,128]{1,0:T(8,128)(2,1)S(1)}, u32[]{:S(2)}, u32[]{:S(2)}) collective-permute-start(bf16[1200,128]{1,0:T(8,128)(2,1)S(1)} %shard_map.77), channel_id=1, source_target_pairs={{32,0},{64,32},{96,64},{128,96},{160,128},{192,160},{224,192},{256... | collective-permute-start | bytes 921608 | tf_op jit(solution)/shard_map/ppermute | solution.py:270
  53.8 11.9 %collective-permute-start.8 = (bf16[1200,128]{1,0:T(8,128)(2,1)S(1)}, bf16[1200,128]{1,0:T(8,128)(2,1)S(1)}, u32[]{:S(2)}, u32[]{:S(2)}) collective-permute-start(bf16[1200,128]{1,0:T(8,128)(2,1)S(1)} %shard_map.77), channel_id=1, source_target_pairs={{480,0},{0,32},{32,64},{64,96},{96,128},{128,160},{160,192},{192,2... | collective-permute-start | bytes 921608 | tf_op jit(solution)/shard_map/ppermute | solution.py:270
  56.9 19.9 %collective-permute-start.4 = (bf16[304,512]{1,0:T(8,128)(2,1)S(1)}, bf16[304,512]{1,0:T(8,128)(2,1)S(1)}, u32[]{:S(2)}, u32[]{:S(2)}) collective-permute-start(bf16[304,512]{1,0:T(8,128)(2,1)S(1)} %shard_map.76.attended.g0), channel_id=1, source_target_pairs={{24,0},{0,8},{8,16},{16,24},{25,1},{1,9},{9,17},{17,25},{26,2},{2,... | collective-permute-start | bytes 933896 | tf_op jit(solution)/shard_map/ppermute | solution.py:325
  58.8 17.9 %collective-permute-start.3 = (bf16[304,512]{1,0:T(8,128)(2,1)S(1)}, bf16[304,512]{1,0:T(8,128)(2,1)S(1)}, u32[]{:S(2)}, u32[]{:S(2)}) collective-permute-start(bf16[304,512]{1,0:T(8,128)(2,1)S(1)} %shard_map.76.attended.g0), channel_id=1, source_target_pairs={{16,0},{24,8},{0,16},{8,24},{17,1},{25,9},{1,17},{9,25},{18,2},{26... | collective-permute-start | bytes 933896 | tf_op jit(solution)/shard_map/ppermute | solution.py:325
  62.4 15.0 %collective-permute-start.2 = (bf16[304,512]{1,0:T(8,128)(2,1)S(1)}, bf16[304,512]{1,0:T(8,128)(2,1)S(1)}, u32[]{:S(2)}, u32[]{:S(2)}) collective-permute-start(bf16[304,512]{1,0:T(8,128)(2,1)S(1)} %shard_map.76.attended.g0), channel_id=1, source_target_pairs={{8,0},{16,8},{24,16},{0,24},{9,1},{17,9},{25,17},{1,25},{10,2},{18... | collective-permute-start | bytes 933896 | tf_op jit(solution)/shard_map/ppermute | solution.py:325
  65.7 10.1 %collective-permute-start.10 = (bf16[1200,128]{1,0:T(8,128)(2,1)S(1)}, bf16[1200,128]{1,0:T(8,128)(2,1)S(1)}, u32[]{:S(2)}, u32[]{:S(2)}) collective-permute-start(bf16[1200,128]{1,0:T(8,128)(2,1)S(1)} %get-tuple-element.22.before), channel_id=1, source_target_pairs={{480,0},{0,32},{32,64},{64,96},{96,128},{128,160},{160,192},{192,2... | collective-permute-start | bytes 921608 | tf_op jit(solution)/shard_map/ppermute | solution.py:270
  67.6 9.1 %collective-permute-start.11 = (bf16[1200,128]{1,0:T(8,128)(2,1)S(1)}, bf16[1200,128]{1,0:T(8,128)(2,1)S(1)}, u32[]{:S(2)}, u32[]{:S(2)}) collective-permute-start(bf16[1200,128]{1,0:T(8,128)(2,1)S(1)} %get-tuple-element.23.after), channel_id=1, source_target_pairs={{32,0},{64,32},{96,64},{128,96},{160,128},{192,160},{224,192},{256... | collective-permute-start | bytes 921608 | tf_op jit(solution)/shard_map/ppermute | solution.py:270
  78.8 5.9 %collective-permute-start.12 = (bf16[16,160,128]{2,1,0:T(8,128)(2,1)S(1)}, bf16[16,160,128]{2,1,0:T(8,128)(2,1)S(1)}, u32[]{:S(2)}, u32[]{:S(2)}) collective-permute-start(bf16[16,160,128]{2,1,0:T(8,128)(2,1)S(1)} %get-tuple-element.26), channel_id=1, source_target_pairs={{0,1},{1,0},{2,3},{3,2},{4,5},{5,4},{6,7},{7,6},{8,9},{9,8},{10,11... | collective-permute-start | bytes 1966088 | tf_op jit(solution)/shard_map/ppermute | solution.py:335
